TPU v7x, 512 devices: a whole 4x8x8 slice. The times are simulated.
512 devices in a mesh: row: 32 (over y, z_hi, core), col: 16 (over x, z_lo).
Axes of the slice: x: 4, y: 8, z: 8 (z_hi: 2, z_lo: 4; z = z_hi * 4 + z_lo), core: 2. Of those that a mesh axis runs over, the one named last changes fastest.
Arguments:
- obj_field: float32 [2, 2, 2048, 4096], P(None, None, 'row', 'col'), may hold values from -5 to 5
- probe: float32 [2, 4, 128, 128], replicated, may hold values from -4 to 4
- scan_pos: int32 [32, 16, 1, 2], P('row', 'col'), may hold values from -64 to 4031, as said below
- live_count: int32 [32, 16], P('row', 'col'), may hold values from 0 to 1, as said below
- patterns: float32 [32, 16, 1, 128, 128], P('row', 'col'), may hold values from 0 to 4
Outputs:
- obj_grad: float32 [2, 2, 2048, 4096], P(None, None, 'row', 'col')
- probe_grad: float32 [2, 4, 128, 128], replicated
Inputs may be any that keep to these rules, and one draw needn't show every extreme that they name: For slot k of tile (r, c), the window's centre (scan_pos[r, c, k, 0] + 64, scan_pos[r, c, k, 1] + 64) lies in that tile, rows r * 64 to (r + 1) * 64 - 1 and columns c * 256 to (c + 1) * 256 - 1. `live_count`: some tile holds 1 positions and some tile none.
All inputs are finite; a program needn't handle non-finite values.
Results may differ from a plain program's by a relative error of at most 0.0003.
Values sent between devices are 32-bit elements; how exact they have to be, the bound alone decides.
No kernel may reach another device: no remote copies, remote signals or barrier semaphores. Data moves between devices by JAX's collectives and lax.ppermute only.
A program may use at most 64 MiB of HBM per device.

v0:
```python
import functools
import math

import jax
import jax.numpy as jnp
import ml_dtypes
import numpy as np
from jax import lax
from jax.experimental import pallas as pl
from jax.experimental.pallas import tpu as pltpu
from jax.sharding import Mesh
from jax.sharding import PartitionSpec as P

PHASE_COEF = 20.0
LOSS_WEIGHT = 0.125
ROW = ("y", "zh", "core")
COL = ("x", "zl")
VMEM_LIMIT = 48 * 1024 * 1024


def split_bf16(table):
    high = table.astype(np.float32).astype(ml_dtypes.bfloat16)
    low = (table - high.astype(np.float64)).astype(np.float32).astype(ml_dtypes.bfloat16)
    return high, low


def tables(side):
    counter = np.arange(side)
    phase = 2.0 * math.pi / side * (counter[:, None] * counter[None, :] % side)
    fourier = np.exp(-1j * phase) / math.sqrt(side)
    spatial = ((counter + side // 2) % side - side // 2) / side
    factor = np.exp(-1j * PHASE_COEF * spatial * spatial)
    propagate = np.conj(fourier) @ (factor[:, None] * fourier)
    propagate = 0.5 * (propagate + propagate.T)
    parts = []
    for matrix in (propagate, fourier):
        real, imaginary = matrix.real, matrix.imag
        right = np.block([[real, imaginary], [-imaginary, real]])
        left = np.block([[real, -imaginary], [imaginary, real]])
        parts += [*split_bf16(right), *split_bf16(left)]
    return np.stack(parts)


def split(value):
    high = value.astype(jnp.bfloat16)
    low = (value - high.astype(jnp.float32)).astype(jnp.bfloat16)
    return high, low


def product(left, right):
    (left_high, left_low), (right_high, right_low) = left, right
    dot = functools.partial(jnp.dot, preferred_element_type=jnp.float32)
    return dot(left_high, right_high) + (dot(left_low, right_high) + dot(left_high, right_low))


def two_sided(real, imaginary, right, left):
    side = real[0].shape[0]
    modes = len(real)
    stacked = jnp.concatenate(
        [jnp.concatenate([r, i], axis=1) for r, i in zip(real, imaginary)], axis=0
    )
    middle = product(split(stacked), right)
    blocks = [middle[m * side : (m + 1) * side] for m in range(modes)]
    spread = jnp.concatenate(
        [
            jnp.concatenate([b[:, :side] for b in blocks], axis=1),
            jnp.concatenate([b[:, side:] for b in blocks], axis=1),
        ],
        axis=0,
    )
    out = product(left, split(spread))
    return (
        [out[:side, m * side : (m + 1) * side] for m in range(modes)],
        [out[side:, m * side : (m + 1) * side] for m in range(modes)],
    )


def times(ar, ai, br, bi):
    return ar * br - ai * bi, ar * bi + ai * br


def times_conj(ar, ai, br, bi):
    return ar * br + ai * bi, ar * bi - ai * br


def model(window, probe, pattern, weight, tabs):
    (o0r, o1r), (o0i, o1i) = window
    qr, qi = probe
    modes = len(qr)
    prop_right, prop_left, four_right, four_left = [
        (tabs[2 * n], tabs[2 * n + 1]) for n in range(4)
    ]
    e0 = [times(qr[m], qi[m], o0r, o0i) for m in range(modes)]
    a1r, a1i = two_sided([e[0] for e in e0], [e[1] for e in e0], prop_right, prop_left)
    e1 = [times(a1r[m], a1i[m], o1r, o1i) for m in range(modes)]
    gr, gi = two_sided([e[0] for e in e1], [e[1] for e in e1], four_right, four_left)
    intensity = gr[0] * gr[0] + gi[0] * gi[0]
    for m in range(1, modes):
        intensity = intensity + (gr[m] * gr[m] + gi[m] * gi[m])
    residue = (intensity - pattern) * (4.0 * LOSS_WEIGHT * weight)
    br, bi = two_sided(
        [residue * g for g in gr], [residue * g for g in gi], four_left, four_right
    )
    grad1 = [times_conj(a1r[m], a1i[m], br[m], bi[m]) for m in range(modes)]
    back = [times_conj(o1r, o1i, br[m], bi[m]) for m in range(modes)]
    cr, ci = two_sided([b[0] for b in back], [b[1] for b in back], prop_left, prop_right)
    grad0 = [times_conj(qr[m], qi[m], cr[m], ci[m]) for m in range(modes)]
    probe_grad = [times_conj(o0r, o0i, cr[m], ci[m]) for m in range(modes)]

    def over_modes(terms, part):
        return functools.reduce(lambda a, b: a + b, [t[part] for t in terms])

    window_grad = [
        [over_modes(grad0, 0), over_modes(grad1, 0)],
        [over_modes(grad0, 1), over_modes(grad1, 1)],
    ]
    return window_grad, probe_grad


def main_kernel(
    place, own, other, beyond, from_left, from_right, probe, pattern, tabs,
    keep, message_core, message_beyond, own_strip, extended, shifted,
):
    row, col, core, live = place[0], place[1], place[2], place[3]
    side = probe.shape[-1]
    half = side // 2
    rows, cols = own.shape[2], own.shape[3]
    modes = probe.shape[1]
    other_at = pl.multiple_of((1 - core) * 2 * half, 8)
    beyond_at = pl.multiple_of(core * 2 * half, 8)
    for layer in range(2):
        for part in range(2):
            plane = 2 * part + layer
            inner = pl.ds(half, cols)
            extended[plane, half : half + rows, inner] = own[part, layer]
            extended[plane, pl.ds(other_at, rows), inner] = other[part, layer]
            extended[plane, pl.ds(beyond_at, rows), inner] = beyond[part, layer]
            mine = pl.ds(part * half, half)
            extended[plane, :, 0:half] = from_left[layer, :, mine]
            extended[plane, :, half + cols : 2 * half + cols] = from_right[layer, :, mine]

    tall = side + 8
    step = lax.rem(row, 8)
    base_row = pl.multiple_of(row - step, 8)

    def window_of(plane):
        wide = extended[plane, pl.ds(base_row, tall), :]
        narrow = pltpu.roll(wide, lax.rem(wide.shape[1] - col, wide.shape[1]), 1)[:, :side]
        return pltpu.roll(narrow, lax.rem(tall - step, tall), 0)[:side]

    window = [[window_of(2 * part + layer) for layer in range(2)] for part in range(2)]
    fields = [[probe[part, m] for m in range(modes)] for part in range(2)]
    weight = live.astype(jnp.float32)
    window_grad, probe_grad = model(
        window, fields, pattern[0, 0, 0], weight, [tabs[n] for n in range(8)]
    )
    first = core == 0
    for m in range(modes):
        at = pl.ds(m * side, side)
        real, imaginary = probe_grad[m]
        keep[at, :] = jnp.where(first, real, imaginary)
        message_core[at, :] = jnp.where(first, imaginary, real)
    base = modes * side
    shifted[...] = jnp.zeros_like(shifted)
    for part in range(2):
        for layer in range(2):
            plane = 2 * part + layer
            padded = jnp.concatenate(
                [window_grad[part][layer], jnp.zeros((8, side), jnp.float32)], axis=0
            )
            shifted[plane, pl.ds(base_row, tall), :] = pltpu.roll(padded, step, 0)
            message_core[pl.ds(base + plane * rows, rows), :] = shifted[plane, pl.ds(other_at, rows), :]
            message_beyond[pl.ds(plane * rows, rows), :] = shifted[plane, pl.ds(beyond_at, rows), :]
            own_strip[pl.ds(plane * rows, rows), :] = shifted[plane, half : half + rows, :]
    offset = jnp.full((8, side), col.astype(jnp.float32))
    message_core[pl.ds(base + 4 * rows, 8), :] = offset
    message_beyond[pl.ds(4 * rows, 8), :] = offset


def pack_kernel(place, own, other, beyond, to_left, to_right):
    core = place[2]
    half = own.shape[2]
    cols = own.shape[3]
    other_at = pl.multiple_of((1 - core) * 2 * half, 8)
    beyond_at = pl.multiple_of(core * 2 * half, 8)
    for source, at in ((own, half), (other, other_at), (beyond, beyond_at)):
        for layer in range(2):
            for part in range(2):
                mine = pl.ds(part * half, half)
                to_left[layer, pl.ds(at, half), mine] = source[part, layer, :, 0:half]
                to_right[layer, pl.ds(at, half), mine] = source[part, layer, :, cols - half : cols]


def merge_kernel(place, own_strip, from_core, from_beyond, centre, to_left, to_right):
    side = own_strip.shape[1]
    half = side // 2
    rows = centre.shape[2]
    cols = centre.shape[3]
    wide = cols + side
    base = from_core.shape[0] - from_beyond.shape[0]
    core_col = jnp.max(from_core[pl.ds(base + 4 * rows, 8), :]).astype(jnp.int32)
    beyond_col = jnp.max(from_beyond[pl.ds(4 * rows, 8), :]).astype(jnp.int32)
    gap = jnp.zeros((rows, cols), jnp.float32)

    def placed(strip, col):
        return pltpu.roll(jnp.concatenate([strip, gap], axis=1), col, 1)

    for layer in range(2):
        for part in range(2):
            plane = 2 * part + layer
            total = placed(own_strip[pl.ds(plane * rows, rows), :], place[1])
            total = total + placed(from_core[pl.ds(base + plane * rows, rows), :], core_col)
            total = total + placed(from_beyond[pl.ds(plane * rows, rows), :], beyond_col)
            centre[part, layer] = total[:, half : half + cols]
            mine = pl.ds(part * half, half)
            to_left[layer, :, mine] = total[:, :half]
            to_right[layer, :, mine] = total[:, wide - half :]


def finish_kernel(centre, from_left, from_right, out):
    half = centre.shape[2]
    cols = centre.shape[3]
    for layer in range(2):
        for part in range(2):
            mine = pl.ds(part * half, half)
            value = centre[part, layer]
            out[part, layer] = value
            out[part, layer, :, 0:half] = value[:, :half] + from_left[layer, :, mine]
            out[part, layer, :, cols - half : cols] = value[:, cols - half :] + from_right[layer, :, mine]


def call(kernel, out_shape, n_scalars, n_in, scratch=(), cost=None):
    many = isinstance(out_shape, (list, tuple))
    vmem = pl.BlockSpec(memory_space=pltpu.VMEM)
    return pl.pallas_call(
        kernel,
        out_shape=out_shape,
        in_specs=[pl.BlockSpec(memory_space=pltpu.SMEM)] * n_scalars + [vmem] * n_in,
        out_specs=[vmem] * len(out_shape) if many else vmem,
        scratch_shapes=list(scratch),
        compiler_params=pltpu.CompilerParams(vmem_limit_bytes=VMEM_LIMIT),
        cost_estimate=cost,
    )


def chain(n, step):
    return [(i, i + step) for i in range(n) if 0 <= i + step < n]


def body(obj_field, probe, scan_pos, live_count, patterns):
    side = probe.shape[2]
    modes = probe.shape[1]
    half = side // 2
    rows, cols = obj_field.shape[2], obj_field.shape[3]
    n_row, n_col = lax.axis_size(ROW), lax.axis_size(COL)
    f32 = jnp.float32
    core = lax.axis_index("core")
    row = scan_pos[0, 0, 0, 0] - (lax.axis_index(ROW) * rows - half)
    col = scan_pos[0, 0, 0, 1] - (lax.axis_index(COL) * cols - half)
    live = (live_count[0, 0] > 0).astype(jnp.int32)
    place = jnp.stack([row, col, core, live]).astype(jnp.int32)
    swap = [(0, 1), (1, 0)]
    pairs = [(i, i + 1) for i in range(1, n_row - 1, 2)]
    pairs = pairs + [(j, i) for i, j in pairs]

    def shape(*dims):
        return jax.ShapeDtypeStruct(dims, f32)

    beyond = lax.ppermute(obj_field, ROW, pairs)
    other = lax.ppermute(obj_field, "core", swap)
    column = shape(2, 2 * half + rows, side)
    to_left, to_right = call(pack_kernel, [column, column], 1, 3)(place, obj_field, other, beyond)
    from_left = lax.ppermute(to_right, COL, chain(n_col, 1))
    from_right = lax.ppermute(to_left, COL, chain(n_col, -1))

    tabs = jnp.asarray(tables(side))
    strip = 4 * rows
    keep, message_core, message_beyond, own_strip = call(
        main_kernel,
        [
            shape(modes * side, side),
            shape(modes * side + strip + 8, side),
            shape(strip + 8, side),
            shape(strip, side),
        ],
        1,
        8,
        [
            pltpu.VMEM((4, 2 * half + rows, 2 * half + cols), f32),
            pltpu.VMEM((4, 2 * half + rows, side), f32),
        ],
    )(place, obj_field, other, beyond, from_left, from_right, probe, patterns, tabs)

    from_core = lax.ppermute(message_core, "core", swap)
    from_beyond = lax.ppermute(message_beyond, ROW, pairs)

    n_yx = lax.axis_size(("y", "x"))
    n_z = lax.axis_size(("zh", "zl"))
    total = modes * side
    chunk = total // n_yx
    summed = keep + from_core[:total]
    spread = lax.all_to_all(summed.reshape(n_yx, chunk, side), ("y", "x"), 0, 0)

    edge = shape(2, rows, side)
    centre, grad_left, grad_right = call(
        merge_kernel, [shape(2, 2, rows, cols), edge, edge], 1, 3
    )(place, own_strip, from_core, from_beyond)
    got_left = lax.ppermute(grad_right, COL, chain(n_col, 1))
    got_right = lax.ppermute(grad_left, COL, chain(n_col, -1))

    part = jnp.sum(spread, axis=0)
    part = lax.all_to_all(jnp.broadcast_to(part, (n_z, chunk, side)), ("zh", "zl"), 0, 0)
    part = jnp.sum(part, axis=0)
    whole = lax.all_to_all(jnp.broadcast_to(part, (n_yx, chunk, side)), ("y", "x"), 0, 0)
    whole = whole.reshape(modes, side, side)
    facing = lax.ppermute(whole, "core", swap)
    first = core == 0
    probe_grad = jnp.stack([jnp.where(first, whole, facing), jnp.where(first, facing, whole)])

    obj_grad = call(finish_kernel, shape(2, 2, rows, cols), 0, 3)(centre, got_left, got_right)
    return (obj_grad, probe_grad)


def solution(mesh):
    fine = Mesh(
        mesh.devices.reshape(8, 2, 2, 4, 4), ("y", "zh", "core", "x", "zl")
    )
    return jax.shard_map(
        body,
        mesh=fine,
        in_specs=(
            P(None, None, ROW, COL),
            P(),
            P(ROW, COL, None, None),
            P(ROW, COL),
            P(ROW, COL, None, None, None),
        ),
        out_specs=(P(None, None, ROW, COL), P()),
        check_vma=False,
    )
```

profile of v0, /device:TPU:11, one launch (start us, length us, event | category | flops | bytes accessed | tf_op | source)
XLA Modules:
  0.0 131.0 jit_solution(11164905642660307019)
XLA Ops:
  0.6 11.2 %collective-permute-start.1 = (f32[2,2,64,256]{3,2,1,0:T(8,128)}, f32[2,2,64,256]{3,2,1,0:T(8,128)S(1)}, u32[]{:S(2)}, u32[]{:S(2)}) collective-permute-start(f32[2,2,64,256]{3,2,1,0:T(8,128)} %own.3), channel_id=1, source_target_pairs={{16,32},{48,64},{80,96},{112,128},{144,160},{176,192},{208,224},{2... | collective-permute-start | bytes 786440 | tf_op jit(solution)/shard_map/ppermute | solution.py:269
  11.8 1.9 %collective-permute-start = (f32[2,2,64,256]{3,2,1,0:T(8,128)}, f32[2,2,64,256]{3,2,1,0:T(8,128)S(1)}, u32[]{:S(2)}, u32[]{:S(2)}) collective-permute-start(f32[2,2,64,256]{3,2,1,0:T(8,128)} %own.3), channel_id=1, source_target_pairs={{0,16},{16,0},{1,17},{17,1},{2,18},{18,2},{3,19},{19,3},{4,20},{20... | collective-permute-start | bytes 786440 | tf_op jit(solution)/shard_map/ppermute | solution.py:270
  17.0 7.9 %collective-permute-done.1.beyond = f32[2,2,64,256]{3,2,1,0:T(8,128)S(1)} collective-permute-done((f32[2,2,64,256]{3,2,1,0:T(8,128)}, f32[2,2,64,256]{3,2,1,0:T(8,128)S(1)}, u32[]{:S(2)}, u32[]{:S(2)}) %collective-permute-start.1) | collective-permute-done | bytes 262176 | tf_op jit(solution)/shard_map/ppermute | solution.py:269
  24.9 0.9 copy-done.1
  26.6 1.9 %collective-permute-start.2 = (f32[2,192,128]{2,1,0:T(8,128)S(1)}, f32[2,192,128]{2,1,0:T(8,128)S(1)}, u32[]{:S(2)}, u32[]{:S(2)}) collective-permute-start(f32[2,192,128]{2,1,0:T(8,128)S(1)} %get-tuple-element.11), channel_id=1, source_target_pairs={{0,1},{1,2},{2,3},{3,4},{4,5},{5,6},{6,7},{7,8},{8,9},{9,10},{10,1... | collective-permute-start | bytes 589832 | tf_op jit(solution)/shard_map/ppermute | solution.py:273
  28.5 6.1 %collective-permute-start.3 = (f32[2,192,128]{2,1,0:T(8,128)S(1)}, f32[2,192,128]{2,1,0:T(8,128)S(1)}, u32[]{:S(2)}, u32[]{:S(2)}) collective-permute-start(f32[2,192,128]{2,1,0:T(8,128)S(1)} %get-tuple-element.12), channel_id=1, source_target_pairs={{1,0},{2,1},{3,2},{4,3},{5,4},{6,5},{7,6},{8,7},{9,8},{10,9},{11,1... | collective-permute-start | bytes 589832 | tf_op jit(solution)/shard_map/ppermute | solution.py:274
  34.6 1.3 collective-permute-done.2.from_left
  35.9 1.3 %collective-permute-done.3.from_right = f32[2,192,128]{2,1,0:T(8,128)S(1)} collective-permute-done((f32[2,192,128]{2,1,0:T(8,128)S(1)}, f32[2,192,128]{2,1,0:T(8,128)S(1)}, u32[]{:S(2)}, u32[]{:S(2)}) %collective-permute-start.3) | collective-permute-done | bytes 196640 | tf_op jit(solution)/shard_map/ppermute | solution.py:274
  37.2 1.2 copy-done
  38.4 5.2 %shard_map.78 = (f32[512,128]{1,0:T(8,128)S(1)}, f32[776,128]{1,0:T(8,128)S(1)}, f32[264,128]{1,0:T(8,128)S(1)}, f32[256,128]{1,0:T(8,128)S(1)}) custom-call(s32[4]{0:T(128)S(1)} %pad_add_fusion.place, f32[2,2,64,256]{3,2,1,0:T(8,128)S(1)} %copy-done.1, f32[2,2,64,256]{3,2,1,0:T(8,128)S(1)} %collective-permute-done.other, ...), custom_call_target="tpu_custom_call" | custom-call | tf_op jit(solution)/shard_map/pallas_call | solution.py:278
  43.6 1.9 %collective-permute-start.4 = (f32[776,128]{1,0:T(8,128)S(1)}, f32[776,128]{1,0:T(8,128)S(1)}, u32[]{:S(2)}, u32[]{:S(2)}) collective-permute-start(f32[776,128]{1,0:T(8,128)S(1)} %get-tuple-element.14), channel_id=1, source_target_pairs={{0,16},{16,0},{1,17},{17,1},{2,18},{18,2},{3,19},{19,3},{4,20},{20... | collective-permute-start | bytes 1191944 | tf_op jit(solution)/shard_map/ppermute | solution.py:294
  45.5 1.7 %collective-permute-done.4.from_core = f32[776,128]{1,0:T(8,128)S(1)} collective-permute-done((f32[776,128]{1,0:T(8,128)S(1)}, f32[776,128]{1,0:T(8,128)S(1)}, u32[]{:S(2)}, u32[]{:S(2)}) %collective-permute-start.4) | collective-permute-done | bytes 397344 | tf_op jit(solution)/shard_map/ppermute | solution.py:294
  47.3 19.8 %all_to_all.15 = f32[32,16,128]{2,1,0:T(8,128)S(1)} all-to-all(f32[32,16,128]{2,1,0:T(8,128)S(1)} %bitcast.15), channel_id=1, replica_groups=mesh['y'=8,'zh'=2,'core'=2,'x'=4,'zl'=4] {'y','x'}, dimensions={0} | all-to-all | bytes 524288 | tf_op jit(solution)/shard_map/all_to_all | solution.py:302
  67.2 16.8 %all_to_all.16 = f32[8,16,128]{2,1,0:T(8,128)S(1)} all-to-all(f32[8,16,128]{2,1,0:T(8,128)S(1)} %broadcast_in_dim.6), channel_id=1, replica_groups=mesh['y'=8,'zh'=2,'core'=2,'x'=4,'zl'=4] {'zh','zl'}, dimensions={0} | all-to-all | bytes 131072 | tf_op jit(solution)/shard_map/all_to_all | solution.py:312
  84.0 14.6 %all_to_all.17 = f32[32,16,128]{2,1,0:T(8,128)S(1)} all-to-all(f32[32,16,128]{2,1,0:T(8,128)S(1)} %broadcast_in_dim.7), channel_id=1, replica_groups=mesh['y'=8,'zh'=2,'core'=2,'x'=4,'zl'=4] {'y','x'}, dimensions={0} | all-to-all | bytes 524288 | tf_op jit(solution)/shard_map/all_to_all | solution.py:314
  98.6 6.0 %collective-permute-start.8 = (f32[4,128,128]{2,1,0:T(8,128)S(1)}, f32[4,128,128]{2,1,0:T(8,128)S(1)}, u32[]{:S(2)}, u32[]{:S(2)}) collective-permute-start(f32[4,128,128]{2,1,0:T(8,128)S(1)} %bitcast.16), channel_id=1, source_target_pairs={{0,16},{16,0},{1,17},{17,1},{2,18},{18,2},{3,19},{19,3},{4,20},{20... | collective-permute-start | bytes 786440 | tf_op jit(solution)/shard_map/ppermute | solution.py:316
  104.6 2.0 %collective-permute-start.5 = (f32[264,128]{1,0:T(8,128)S(1)}, f32[264,128]{1,0:T(8,128)S(1)}, u32[]{:S(2)}, u32[]{:S(2)}) collective-permute-start(f32[264,128]{1,0:T(8,128)S(1)} %get-tuple-element.15), channel_id=1, source_target_pairs={{16,32},{48,64},{80,96},{112,128},{144,160},{176,192},{208,224},{2... | collective-permute-start | bytes 405512 | tf_op jit(solution)/shard_map/ppermute | solution.py:295
  106.6 12.4 %collective-permute-done.5.from_beyond = f32[264,128]{1,0:T(8,128)S(1)} collective-permute-done((f32[264,128]{1,0:T(8,128)S(1)}, f32[264,128]{1,0:T(8,128)S(1)}, u32[]{:S(2)}, u32[]{:S(2)}) %collective-permute-start.5) | collective-permute-done | bytes 135200 | tf_op jit(solution)/shard_map/ppermute | solution.py:295
  119.0 0.9 shard_map.79
  120.0 1.9 %collective-permute-start.6 = (f32[2,64,128]{2,1,0:T(8,128)S(1)}, f32[2,64,128]{2,1,0:T(8,128)S(1)}, u32[]{:S(2)}, u32[]{:S(2)}) collective-permute-start(f32[2,64,128]{2,1,0:T(8,128)S(1)} %get-tuple-element.17), channel_id=1, source_target_pairs={{0,1},{1,2},{2,3},{3,4},{4,5},{5,6},{6,7},{7,8},{8,9},{9,10},{10,1... | collective-permute-start | bytes 196616 | tf_op jit(solution)/shard_map/ppermute | solution.py:308
  121.9 6.1 %collective-permute-start.7 = (f32[2,64,128]{2,1,0:T(8,128)S(1)}, f32[2,64,128]{2,1,0:T(8,128)S(1)}, u32[]{:S(2)}, u32[]{:S(2)}) collective-permute-start(f32[2,64,128]{2,1,0:T(8,128)S(1)} %get-tuple-element.18), channel_id=1, source_target_pairs={{1,0},{2,1},{3,2},{4,3},{5,4},{6,5},{7,6},{8,7},{9,8},{10,9},{11,1... | collective-permute-start | bytes 196616 | tf_op jit(solution)/shard_map/ppermute | solution.py:309
  128.3 1.0 collective-permute-done.7.from_right
  129.3 0.8 shard_map.80
  130.2 0.8 pad_maximum_fusion
  (20 shorter events, 2.5 us)
Async XLA Ops:
  0.6 24.3 %collective-permute-start.1 = (f32[2,2,64,256]{3,2,1,0:T(8,128)}, f32[2,2,64,256]{3,2,1,0:T(8,128)S(1)}, u32[]{:S(2)}, u32[]{:S(2)}) collective-permute-start(f32[2,2,64,256]{3,2,1,0:T(8,128)} %own.3), channel_id=1, source_target_pairs={{16,32},{48,64},{80,96},{112,128},{144,160},{176,192},{208,224},{2... | collective-permute-start | bytes 786440 | tf_op jit(solution)/shard_map/ppermute | solution.py:269
  11.8 13.1 %collective-permute-start = (f32[2,2,64,256]{3,2,1,0:T(8,128)}, f32[2,2,64,256]{3,2,1,0:T(8,128)S(1)}, u32[]{:S(2)}, u32[]{:S(2)}) collective-permute-start(f32[2,2,64,256]{3,2,1,0:T(8,128)} %own.3), channel_id=1, source_target_pairs={{0,16},{16,0},{1,17},{17,1},{2,18},{18,2},{3,19},{19,3},{4,20},{20... | collective-permute-start | bytes 786440 | tf_op jit(solution)/shard_map/ppermute | solution.py:270
  14.4 0.7 copy-start.4
  24.9 1.0 copy-start.1
  25.9 11.3 %copy-start.2 = (f32[2,4,128,128]{3,2,1,0:T(8,128)S(1)}, f32[2,4,128,128]{3,2,1,0:T(8,128)}, u32[]{:S(2)}) copy-start(f32[2,4,128,128]{3,2,1,0:T(8,128)} %probe.1) | copy-start | bytes 1572868
  25.9 11.3 %copy-start.3 = (f32[1,1,1,128,128]{4,3,2,1,0:T(8,128)S(1)}, f32[1,1,1,128,128]{4,3,2,1,0:T(8,128)}, u32[]{:S(2)}) copy-start(f32[1,1,1,128,128]{4,3,2,1,0:T(8,128)} %pattern.1) | copy-start | bytes 196612
  26.6 9.3 %collective-permute-start.2 = (f32[2,192,128]{2,1,0:T(8,128)S(1)}, f32[2,192,128]{2,1,0:T(8,128)S(1)}, u32[]{:S(2)}, u32[]{:S(2)}) collective-permute-start(f32[2,192,128]{2,1,0:T(8,128)S(1)} %get-tuple-element.11), channel_id=1, source_target_pairs={{0,1},{1,2},{2,3},{3,4},{4,5},{5,6},{6,7},{7,8},{8,9},{9,10},{10,1... | collective-permute-start | bytes 589832 | tf_op jit(solution)/shard_map/ppermute | solution.py:273
  28.5 8.7 %collective-permute-start.3 = (f32[2,192,128]{2,1,0:T(8,128)S(1)}, f32[2,192,128]{2,1,0:T(8,128)S(1)}, u32[]{:S(2)}, u32[]{:S(2)}) collective-permute-start(f32[2,192,128]{2,1,0:T(8,128)S(1)} %get-tuple-element.12), channel_id=1, source_target_pairs={{1,0},{2,1},{3,2},{4,3},{5,4},{6,5},{7,6},{8,7},{9,8},{10,9},{11,1... | collective-permute-start | bytes 589832 | tf_op jit(solution)/shard_map/ppermute | solution.py:274
  37.2 1.2 copy-start
  43.6 3.6 %collective-permute-start.4 = (f32[776,128]{1,0:T(8,128)S(1)}, f32[776,128]{1,0:T(8,128)S(1)}, u32[]{:S(2)}, u32[]{:S(2)}) collective-permute-start(f32[776,128]{1,0:T(8,128)S(1)} %get-tuple-element.14), channel_id=1, source_target_pairs={{0,16},{16,0},{1,17},{17,1},{2,18},{18,2},{3,19},{19,3},{4,20},{20... | collective-permute-start | bytes 1191944 | tf_op jit(solution)/shard_map/ppermute | solution.py:294
  98.6 31.5 %collective-permute-start.8 = (f32[4,128,128]{2,1,0:T(8,128)S(1)}, f32[4,128,128]{2,1,0:T(8,128)S(1)}, u32[]{:S(2)}, u32[]{:S(2)}) collective-permute-start(f32[4,128,128]{2,1,0:T(8,128)S(1)} %bitcast.16), channel_id=1, source_target_pairs={{0,16},{16,0},{1,17},{17,1},{2,18},{18,2},{3,19},{19,3},{4,20},{20... | collective-permute-start | bytes 786440 | tf_op jit(solution)/shard_map/ppermute | solution.py:316
  104.6 14.4 %collective-permute-start.5 = (f32[264,128]{1,0:T(8,128)S(1)}, f32[264,128]{1,0:T(8,128)S(1)}, u32[]{:S(2)}, u32[]{:S(2)}) collective-permute-start(f32[264,128]{1,0:T(8,128)S(1)} %get-tuple-element.15), channel_id=1, source_target_pairs={{16,32},{48,64},{80,96},{112,128},{144,160},{176,192},{208,224},{2... | collective-permute-start | bytes 405512 | tf_op jit(solution)/shard_map/ppermute | solution.py:295
  120.0 8.3 %collective-permute-start.6 = (f32[2,64,128]{2,1,0:T(8,128)S(1)}, f32[2,64,128]{2,1,0:T(8,128)S(1)}, u32[]{:S(2)}, u32[]{:S(2)}) collective-permute-start(f32[2,64,128]{2,1,0:T(8,128)S(1)} %get-tuple-element.17), channel_id=1, source_target_pairs={{0,1},{1,2},{2,3},{3,4},{4,5},{5,6},{6,7},{7,8},{8,9},{9,10},{10,1... | collective-permute-start | bytes 196616 | tf_op jit(solution)/shard_map/ppermute | solution.py:308
  121.9 7.4 %collective-permute-start.7 = (f32[2,64,128]{2,1,0:T(8,128)S(1)}, f32[2,64,128]{2,1,0:T(8,128)S(1)}, u32[]{:S(2)}, u32[]{:S(2)}) collective-permute-start(f32[2,64,128]{2,1,0:T(8,128)S(1)} %get-tuple-element.18), channel_id=1, source_target_pairs={{1,0},{2,1},{3,2},{4,3},{5,4},{6,5},{7,6},{8,7},{9,8},{10,9},{11,1... | collective-permute-start | bytes 196616 | tf_op jit(solution)/shard_map/ppermute | solution.py:309
where the time goes:
time: 132 us; the launch traced here: 131 us
  blocking collectives  51.2 us (39%)
  starting transfers between devices  39 us (30%)
  waiting for transfers between devices  25.9 us (20%)
  Pallas kernels  7.66 us (6%)
  local copies, waits for them, and re-layouts  3.5 us (3%)
  between operations  2.62 us (2%)
    all_to_all x1, blocking collectives, body(): spread = lax.all_to_all(summed.reshape(n_yx, chunk, side), ('y', 'x'), 0, 0)  19.8 us
    all_to_all x1, blocking collectives, body(): lax.all_to_all(jnp.broadcast_to(part, (n_z, chunk, side)), ('zh', 'zl'),...  16.8 us
    all_to_all x1, blocking collectives, body(): lax.all_to_all(jnp.broadcast_to(part, (n_yx, chunk, side)), ('y', 'x'), 0...  14.6 us
    ppermute x1, waiting for transfers between devices, body(): from_beyond = lax.ppermute(message_beyond, ROW, pairs)  12.4 us
    ppermute x1, starting transfers between devices, body(): beyond = lax.ppermute(obj_field, ROW, pairs)  11.2 us
    ppermute x1, waiting for transfers between devices, body(): beyond = lax.ppermute(obj_field, ROW, pairs)  7.93 us
    ppermute x1, starting transfers between devices, body(): from_right = lax.ppermute(to_left, COL, chain(n_col, -1))  6.06 us
    ppermute x1, starting transfers between devices, body(): got_right = lax.ppermute(grad_left, COL, chain(n_col, -1))  6.06 us
  transfers between devices with their start and end apart: 9, of which 7 were waited for; matrix products, arithmetic and copies ran while one was open for 1% of the time, Pallas kernels for 1%

commit v1 on v0

--- a/solution.py
+++ b/solution.py
@@ -34,11 +34,27 @@
     propagate = 0.5 * (propagate + propagate.T)
     parts = []
     for matrix in (propagate, fourier):
-        real, imaginary = matrix.real, matrix.imag
-        right = np.block([[real, imaginary], [-imaginary, real]])
-        left = np.block([[real, -imaginary], [imaginary, real]])
-        parts += [*split_bf16(right), *split_bf16(left)]
+        for block in (matrix.real, matrix.imag, -matrix.imag):
+            parts += split_bf16(block)
     return np.stack(parts)
+
+
+def on_sides(tabs, which):
+    def block(n, part):
+        return tabs[6 * which + 2 * n + part]
+
+    def square(a, b, c, d, part):
+        return jnp.concatenate(
+            [
+                jnp.concatenate([block(a, part), block(b, part)], axis=1),
+                jnp.concatenate([block(c, part), block(d, part)], axis=1),
+            ],
+            axis=0,
+        )
+
+    right = tuple(square(0, 1, 2, 0, part) for part in range(2))
+    left = tuple(square(0, 2, 1, 0, part) for part in range(2))
+    return right, left
 
 
 def split(value):
@@ -87,9 +103,8 @@
     (o0r, o1r), (o0i, o1i) = window
     qr, qi = probe
     modes = len(qr)
-    prop_right, prop_left, four_right, four_left = [
-        (tabs[2 * n], tabs[2 * n + 1]) for n in range(4)
-    ]
+    prop_right, prop_left = on_sides(tabs, 0)
+    four_right, four_left = on_sides(tabs, 1)
     e0 = [times(qr[m], qi[m], o0r, o0i) for m in range(modes)]
     a1r, a1i = two_sided([e[0] for e in e0], [e[1] for e in e0], prop_right, prop_left)
     e1 = [times(a1r[m], a1i[m], o1r, o1i) for m in range(modes)]
@@ -152,7 +167,7 @@
     fields = [[probe[part, m] for m in range(modes)] for part in range(2)]
     weight = live.astype(jnp.float32)
     window_grad, probe_grad = model(
-        window, fields, pattern[0, 0, 0], weight, [tabs[n] for n in range(8)]
+        window, fields, pattern[0, 0, 0], weight, tabs
     )
     first = core == 0
     for m in range(modes):
@@ -305,12 +320,13 @@
     centre, grad_left, grad_right = call(
         merge_kernel, [shape(2, 2, rows, cols), edge, edge], 1, 3
     )(place, own_strip, from_core, from_beyond)
+    part = jnp.sum(spread, axis=0)
+    part, grad_left, grad_right = lax.optimization_barrier((part, grad_left, grad_right))
     got_left = lax.ppermute(grad_right, COL, chain(n_col, 1))
     got_right = lax.ppermute(grad_left, COL, chain(n_col, -1))
-
-    part = jnp.sum(spread, axis=0)
     part = lax.all_to_all(jnp.broadcast_to(part, (n_z, chunk, side)), ("zh", "zl"), 0, 0)
     part = jnp.sum(part, axis=0)
+    part, got_left, got_right = lax.optimization_barrier((part, got_left, got_right))
     whole = lax.all_to_all(jnp.broadcast_to(part, (n_yx, chunk, side)), ("y", "x"), 0, 0)
     whole = whole.reshape(modes, side, side)
     facing = lax.ppermute(whole, "core", swap)

time: 132 us -> 119 us (0.902)
  the two profiles are of different devices: /device:TPU:11 before, /device:TPU:1 now
where the time goes in v1:
time: 119 us
  starting transfers between devices  60.3 us (51%)
  waiting for transfers between devices  21.5 us (18%)
  blocking collectives  20.9 us (18%)
  Pallas kernels  7.64 us (6%)
  local copies, waits for them, and re-layouts  3.91 us (3%)
  between operations  2.69 us (2%)
  other arithmetic  1.75 us (1%)
    all_to_all x1, blocking collectives, body(): lax.all_to_all(jnp.broadcast_to(part, (n_yx, chunk, side)), ('y', 'x'), 0...  20.9 us
    ppermute x1, starting transfers between devices, body(): beyond = lax.ppermute(obj_field, ROW, pairs)  12 us
    all_to_all x1, starting transfers between devices, body(): spread = lax.all_to_all(summed.reshape(n_yx, chunk, side), ('y', 'x'), 0, 0)  11 us
    ppermute x1, starting transfers between devices, body(): from_beyond = lax.ppermute(message_beyond, ROW, pairs)  9.6 us
    all_to_all x1, starting transfers between devices, body(): lax.all_to_all(jnp.broadcast_to(part, (n_z, chunk, side)), ('zh', 'zl'),...  7.31 us
    ppermute x1, starting transfers between devices, body(): facing = lax.ppermute(whole, 'core', swap)  5.66 us
    pallas_call x1, Pallas kernels, body(): call(main_kernel, [shape(modes * side, side), shape(modes * side + strip...  5.18 us
    ppermute x1, starting transfers between devices, body(): from_left = lax.ppermute(to_right, COL, chain(n_col, 1))  4.99 us
  transfers between devices with their start and end apart: 11, of which 8 were waited for; matrix products, arithmetic and copies ran while one was open for 1% of the time, Pallas kernels for 1%

profile of v1, /device:TPU:1, one launch (start us, length us, event | category | flops | bytes accessed | tf_op | source)
XLA Modules:
  0.0 118.8 jit_solution(16689554339554037764)
XLA Ops:
  0.6 12.0 %collective-permute-start.1 = (f32[2,2,64,256]{3,2,1,0:T(8,128)}, f32[2,2,64,256]{3,2,1,0:T(8,128)S(1)}, u32[]{:S(2)}, u32[]{:S(2)}) collective-permute-start(f32[2,2,64,256]{3,2,1,0:T(8,128)} %own.3), channel_id=1, source_target_pairs={{16,32},{48,64},{80,96},{112,128},{144,160},{176,192},{208,224},{2... | collective-permute-start | bytes 786440 | tf_op jit(solution)/shard_map/ppermute | solution.py:284
  12.7 1.9 %collective-permute-start = (f32[2,2,64,256]{3,2,1,0:T(8,128)}, f32[2,2,64,256]{3,2,1,0:T(8,128)S(1)}, u32[]{:S(2)}, u32[]{:S(2)}) collective-permute-start(f32[2,2,64,256]{3,2,1,0:T(8,128)} %own.3), channel_id=1, source_target_pairs={{0,16},{16,0},{1,17},{17,1},{2,18},{18,2},{3,19},{19,3},{4,20},{20... | collective-permute-start | bytes 786440 | tf_op jit(solution)/shard_map/ppermute | solution.py:285
  17.9 4.9 %collective-permute-done.1.beyond = f32[2,2,64,256]{3,2,1,0:T(8,128)S(1)} collective-permute-done((f32[2,2,64,256]{3,2,1,0:T(8,128)}, f32[2,2,64,256]{3,2,1,0:T(8,128)S(1)}, u32[]{:S(2)}, u32[]{:S(2)}) %collective-permute-start.1) | collective-permute-done | bytes 262176 | tf_op jit(solution)/shard_map/ppermute | solution.py:284
  22.8 0.9 copy-done
  24.5 5.0 %collective-permute-start.2 = (f32[2,192,128]{2,1,0:T(8,128)S(1)}, f32[2,192,128]{2,1,0:T(8,128)S(1)}, u32[]{:S(2)}, u32[]{:S(2)}) collective-permute-start(f32[2,192,128]{2,1,0:T(8,128)S(1)} %get-tuple-element.17), channel_id=1, source_target_pairs={{0,1},{1,2},{2,3},{3,4},{4,5},{5,6},{6,7},{7,8},{8,9},{9,10},{10,1... | collective-permute-start | bytes 589832 | tf_op jit(solution)/shard_map/ppermute | solution.py:288
  29.5 1.3 %collective-permute-start.3 = (f32[2,192,128]{2,1,0:T(8,128)S(1)}, f32[2,192,128]{2,1,0:T(8,128)S(1)}, u32[]{:S(2)}, u32[]{:S(2)}) collective-permute-start(f32[2,192,128]{2,1,0:T(8,128)S(1)} %get-tuple-element.18), channel_id=1, source_target_pairs={{1,0},{2,1},{3,2},{4,3},{5,4},{6,5},{7,6},{8,7},{9,8},{10,9},{11,1... | collective-permute-start | bytes 589832 | tf_op jit(solution)/shard_map/ppermute | solution.py:289
  30.8 1.3 %collective-permute-done.2.from_left = f32[2,192,128]{2,1,0:T(8,128)S(1)} collective-permute-done((f32[2,192,128]{2,1,0:T(8,128)S(1)}, f32[2,192,128]{2,1,0:T(8,128)S(1)}, u32[]{:S(2)}, u32[]{:S(2)}) %collective-permute-start.2) | collective-permute-done | bytes 196640 | tf_op jit(solution)/shard_map/ppermute | solution.py:288
  32.1 4.3 %collective-permute-done.3.from_right = f32[2,192,128]{2,1,0:T(8,128)S(1)} collective-permute-done((f32[2,192,128]{2,1,0:T(8,128)S(1)}, f32[2,192,128]{2,1,0:T(8,128)S(1)}, u32[]{:S(2)}, u32[]{:S(2)}) %collective-permute-start.3) | collective-permute-done | bytes 196640 | tf_op jit(solution)/shard_map/ppermute | solution.py:289
  36.4 1.0 copy-done.2
  37.4 5.2 %shard_map.78 = (f32[512,128]{1,0:T(8,128)S(1)}, f32[776,128]{1,0:T(8,128)S(1)}, f32[264,128]{1,0:T(8,128)S(1)}, f32[256,128]{1,0:T(8,128)S(1)}) custom-call(s32[4]{0:T(128)S(1)} %pad_add_fusion.place, f32[2,2,64,256]{3,2,1,0:T(8,128)S(1)} %copy-done, f32[2,2,64,256]{3,2,1,0:T(8,128)S(1)} %collective-permute-done.other, ...), custom_call_target="tpu_custom_call" | custom-call | tf_op jit(solution)/shard_map/pallas_call | solution.py:293
  42.6 1.9 %collective-permute-start.4 = (f32[776,128]{1,0:T(8,128)S(1)}, f32[776,128]{1,0:T(8,128)S(1)}, u32[]{:S(2)}, u32[]{:S(2)}) collective-permute-start(f32[776,128]{1,0:T(8,128)S(1)} %get-tuple-element.20), channel_id=1, source_target_pairs={{0,16},{16,0},{1,17},{17,1},{2,18},{18,2},{3,19},{19,3},{4,20},{20... | collective-permute-start | bytes 1191944 | tf_op jit(solution)/shard_map/ppermute | solution.py:309
  44.5 1.7 %collective-permute-done.4.from_core = f32[776,128]{1,0:T(8,128)S(1)} collective-permute-done((f32[776,128]{1,0:T(8,128)S(1)}, f32[776,128]{1,0:T(8,128)S(1)}, u32[]{:S(2)}, u32[]{:S(2)}) %collective-permute-start.4) | collective-permute-done | bytes 397344 | tf_op jit(solution)/shard_map/ppermute | solution.py:309
  46.9 11.0 %all-to-all-start = ((f32[32,16,128]{2,1,0:T(8,128)}), f32[32,16,128]{2,1,0:T(8,128)S(1)}, u32[]{:S(2)}, u32[]{:S(2)}) async-start(f32[32,16,128]{2,1,0:T(8,128)} %bitcast.6), calls=%async_computation | async-start | bytes 524288 | tf_op jit(solution)/shard_map/all_to_all | solution.py:317
  57.9 9.6 %collective-permute-start.5 = (f32[264,128]{1,0:T(8,128)S(1)}, f32[264,128]{1,0:T(8,128)S(1)}, u32[]{:S(2)}, u32[]{:S(2)}) collective-permute-start(f32[264,128]{1,0:T(8,128)S(1)} %get-tuple-element.21), channel_id=1, source_target_pairs={{16,32},{48,64},{80,96},{112,128},{144,160},{176,192},{208,224},{2... | collective-permute-start | bytes 405512 | tf_op jit(solution)/shard_map/ppermute | solution.py:310
  67.5 4.4 %collective-permute-done.5.from_beyond = f32[264,128]{1,0:T(8,128)S(1)} collective-permute-done((f32[264,128]{1,0:T(8,128)S(1)}, f32[264,128]{1,0:T(8,128)S(1)}, u32[]{:S(2)}, u32[]{:S(2)}) %collective-permute-start.5) | collective-permute-done | bytes 135200 | tf_op jit(solution)/shard_map/ppermute | solution.py:310
  71.9 0.9 shard_map.79
  73.5 7.3 %all-to-all-start.1 = ((f32[8,16,128]{2,1,0:T(8,128)}), f32[8,16,128]{2,1,0:T(8,128)S(1)}, u32[]{:S(2)}, u32[]{:S(2)}) async-start(f32[8,16,128]{2,1,0:T(8,128)} %broadcast_in_dim.6), calls=%async_computation.1 | async-start | bytes 131072 | tf_op jit(solution)/shard_map/all_to_all | solution.py:327
  80.9 3.4 %collective-permute-start.6 = (f32[2,64,128]{2,1,0:T(8,128)S(1)}, f32[2,64,128]{2,1,0:T(8,128)S(1)}, u32[]{:S(2)}, u32[]{:S(2)}) collective-permute-start(f32[2,64,128]{2,1,0:T(8,128)S(1)} %get-tuple-element.27), channel_id=1, source_target_pairs={{0,1},{1,2},{2,3},{3,4},{4,5},{5,6},{6,7},{7,8},{8,9},{9,10},{10,1... | collective-permute-start | bytes 196616 | tf_op jit(solution)/shard_map/ppermute | solution.py:325
  84.2 1.3 %collective-permute-start.7 = (f32[2,64,128]{2,1,0:T(8,128)S(1)}, f32[2,64,128]{2,1,0:T(8,128)S(1)}, u32[]{:S(2)}, u32[]{:S(2)}) collective-permute-start(f32[2,64,128]{2,1,0:T(8,128)S(1)} %get-tuple-element.28), channel_id=1, source_target_pairs={{1,0},{2,1},{3,2},{4,3},{5,4},{6,5},{7,6},{8,7},{9,8},{10,9},{11,1... | collective-permute-start | bytes 196616 | tf_op jit(solution)/shard_map/ppermute | solution.py:326
  85.5 2.7 %all-to-all-done.1 = f32[8,16,128]{2,1,0:T(8,128)S(1)} async-done(((f32[8,16,128]{2,1,0:T(8,128)}), f32[8,16,128]{2,1,0:T(8,128)S(1)}, u32[]{:S(2)}, u32[]{:S(2)}) %all-to-all-start.1) | async-done | bytes 65568 | tf_op jit(solution)/shard_map/all_to_all | solution.py:327
  88.2 1.9 %collective-permute-done.7.from_right = f32[2,64,128]{2,1,0:T(8,128)S(1)} collective-permute-done((f32[2,64,128]{2,1,0:T(8,128)S(1)}, f32[2,64,128]{2,1,0:T(8,128)S(1)}, u32[]{:S(2)}, u32[]{:S(2)}) %collective-permute-start.7) | collective-permute-done | bytes 65568 | tf_op jit(solution)/shard_map/ppermute | solution.py:326
  90.2 20.9 %all_to_all.15 = f32[32,16,128]{2,1,0:T(8,128)S(1)} all-to-all(f32[32,16,128]{2,1,0:T(8,128)S(1)} %broadcast_in_dim.7), channel_id=1, replica_groups=mesh['y'=8,'zh'=2,'core'=2,'x'=4,'zl'=4] {'y','x'}, dimensions={0} | all-to-all | bytes 524288 | tf_op jit(solution)/shard_map/all_to_all | solution.py:330
  111.1 5.7 %collective-permute-start.8 = (f32[4,128,128]{2,1,0:T(8,128)S(1)}, f32[4,128,128]{2,1,0:T(8,128)S(1)}, u32[]{:S(2)}, u32[]{:S(2)}) collective-permute-start(f32[4,128,128]{2,1,0:T(8,128)S(1)} %bitcast.15), channel_id=1, source_target_pairs={{0,16},{16,0},{1,17},{17,1},{2,18},{18,2},{3,19},{19,3},{4,20},{20... | collective-permute-start | bytes 786440 | tf_op jit(solution)/shard_map/ppermute | solution.py:332
  117.9 0.8 pad_maximum_fusion
  (22 shorter events, 4.7 us)
Async XLA Ops:
  0.6 22.2 %collective-permute-start.1 = (f32[2,2,64,256]{3,2,1,0:T(8,128)}, f32[2,2,64,256]{3,2,1,0:T(8,128)S(1)}, u32[]{:S(2)}, u32[]{:S(2)}) collective-permute-start(f32[2,2,64,256]{3,2,1,0:T(8,128)} %own.3), channel_id=1, source_target_pairs={{16,32},{48,64},{80,96},{112,128},{144,160},{176,192},{208,224},{2... | collective-permute-start | bytes 786440 | tf_op jit(solution)/shard_map/ppermute | solution.py:284
  12.7 10.2 %collective-permute-start = (f32[2,2,64,256]{3,2,1,0:T(8,128)}, f32[2,2,64,256]{3,2,1,0:T(8,128)S(1)}, u32[]{:S(2)}, u32[]{:S(2)}) collective-permute-start(f32[2,2,64,256]{3,2,1,0:T(8,128)} %own.3), channel_id=1, source_target_pairs={{0,16},{16,0},{1,17},{17,1},{2,18},{18,2},{3,19},{19,3},{4,20},{20... | collective-permute-start | bytes 786440 | tf_op jit(solution)/shard_map/ppermute | solution.py:285
  15.3 0.7 copy-start.4
  22.8 1.0 copy-start
  23.8 12.6 %copy-start.1 = (f32[2,4,128,128]{3,2,1,0:T(8,128)S(1)}, f32[2,4,128,128]{3,2,1,0:T(8,128)}, u32[]{:S(2)}) copy-start(f32[2,4,128,128]{3,2,1,0:T(8,128)} %probe.1) | copy-start | bytes 1572868
  23.8 12.6 %copy-start.3 = (f32[1,1,1,128,128]{4,3,2,1,0:T(8,128)S(1)}, f32[1,1,1,128,128]{4,3,2,1,0:T(8,128)}, u32[]{:S(2)}) copy-start(f32[1,1,1,128,128]{4,3,2,1,0:T(8,128)} %pattern.1) | copy-start | bytes 196612
  24.5 7.6 %collective-permute-start.2 = (f32[2,192,128]{2,1,0:T(8,128)S(1)}, f32[2,192,128]{2,1,0:T(8,128)S(1)}, u32[]{:S(2)}, u32[]{:S(2)}) collective-permute-start(f32[2,192,128]{2,1,0:T(8,128)S(1)} %get-tuple-element.17), channel_id=1, source_target_pairs={{0,1},{1,2},{2,3},{3,4},{4,5},{5,6},{6,7},{7,8},{8,9},{9,10},{10,1... | collective-permute-start | bytes 589832 | tf_op jit(solution)/shard_map/ppermute | solution.py:288
  29.5 6.9 %collective-permute-start.3 = (f32[2,192,128]{2,1,0:T(8,128)S(1)}, f32[2,192,128]{2,1,0:T(8,128)S(1)}, u32[]{:S(2)}, u32[]{:S(2)}) collective-permute-start(f32[2,192,128]{2,1,0:T(8,128)S(1)} %get-tuple-element.18), channel_id=1, source_target_pairs={{1,0},{2,1},{3,2},{4,3},{5,4},{6,5},{7,6},{8,7},{9,8},{10,9},{11,1... | collective-permute-start | bytes 589832 | tf_op jit(solution)/shard_map/ppermute | solution.py:289
  36.4 1.0 copy-start.2
  42.6 3.6 %collective-permute-start.4 = (f32[776,128]{1,0:T(8,128)S(1)}, f32[776,128]{1,0:T(8,128)S(1)}, u32[]{:S(2)}, u32[]{:S(2)}) collective-permute-start(f32[776,128]{1,0:T(8,128)S(1)} %get-tuple-element.20), channel_id=1, source_target_pairs={{0,16},{16,0},{1,17},{17,1},{2,18},{18,2},{3,19},{19,3},{4,20},{20... | collective-permute-start | bytes 1191944 | tf_op jit(solution)/shard_map/ppermute | solution.py:309
  46.9 25.9 %all-to-all-start = ((f32[32,16,128]{2,1,0:T(8,128)}), f32[32,16,128]{2,1,0:T(8,128)S(1)}, u32[]{:S(2)}, u32[]{:S(2)}) async-start(f32[32,16,128]{2,1,0:T(8,128)} %bitcast.6), calls=%async_computation | async-start | bytes 524288 | tf_op jit(solution)/shard_map/all_to_all | solution.py:317
  57.9 14.0 %collective-permute-start.5 = (f32[264,128]{1,0:T(8,128)S(1)}, f32[264,128]{1,0:T(8,128)S(1)}, u32[]{:S(2)}, u32[]{:S(2)}) collective-permute-start(f32[264,128]{1,0:T(8,128)S(1)} %get-tuple-element.21), channel_id=1, source_target_pairs={{16,32},{48,64},{80,96},{112,128},{144,160},{176,192},{208,224},{2... | collective-permute-start | bytes 405512 | tf_op jit(solution)/shard_map/ppermute | solution.py:310
  73.5 14.6 %all-to-all-start.1 = ((f32[8,16,128]{2,1,0:T(8,128)}), f32[8,16,128]{2,1,0:T(8,128)S(1)}, u32[]{:S(2)}, u32[]{:S(2)}) async-start(f32[8,16,128]{2,1,0:T(8,128)} %broadcast_in_dim.6), calls=%async_computation.1 | async-start | bytes 131072 | tf_op jit(solution)/shard_map/all_to_all | solution.py:327
  80.9 7.4 %collective-permute-start.6 = (f32[2,64,128]{2,1,0:T(8,128)S(1)}, f32[2,64,128]{2,1,0:T(8,128)S(1)}, u32[]{:S(2)}, u32[]{:S(2)}) collective-permute-start(f32[2,64,128]{2,1,0:T(8,128)S(1)} %get-tuple-element.27), channel_id=1, source_target_pairs={{0,1},{1,2},{2,3},{3,4},{4,5},{5,6},{6,7},{7,8},{8,9},{9,10},{10,1... | collective-permute-start | bytes 196616 | tf_op jit(solution)/shard_map/ppermute | solution.py:325
  84.2 5.9 %collective-permute-start.7 = (f32[2,64,128]{2,1,0:T(8,128)S(1)}, f32[2,64,128]{2,1,0:T(8,128)S(1)}, u32[]{:S(2)}, u32[]{:S(2)}) collective-permute-start(f32[2,64,128]{2,1,0:T(8,128)S(1)} %get-tuple-element.28), channel_id=1, source_target_pairs={{1,0},{2,1},{3,2},{4,3},{5,4},{6,5},{7,6},{8,7},{9,8},{10,9},{11,1... | collective-permute-start | bytes 196616 | tf_op jit(solution)/shard_map/ppermute | solution.py:326
  111.1 6.8 %collective-permute-start.8 = (f32[4,128,128]{2,1,0:T(8,128)S(1)}, f32[4,128,128]{2,1,0:T(8,128)S(1)}, u32[]{:S(2)}, u32[]{:S(2)}) collective-permute-start(f32[4,128,128]{2,1,0:T(8,128)S(1)} %bitcast.15), channel_id=1, source_target_pairs={{0,16},{16,0},{1,17},{17,1},{2,18},{18,2},{3,19},{19,3},{4,20},{20... | collective-permute-start | bytes 786440 | tf_op jit(solution)/shard_map/ppermute | solution.py:332

commit v2 on v1

--- a/solution.py
+++ b/solution.py
@@ -16,6 +16,7 @@
 ROW = ("y", "zh", "core")
 COL = ("x", "zl")
 VMEM_LIMIT = 48 * 1024 * 1024
+TILE_COLS = 256
 
 
 def split_bf16(table):
@@ -132,44 +133,101 @@
     return window_grad, probe_grad
 
 
+def place_of(scan, rows, cols, half):
+    row = scan[0] - (lax.axis_index(ROW) * rows - half)
+    col = scan[1] - (lax.axis_index(COL) * cols - half)
+    return row, col
+
+
+def strips_at(half):
+    core = lax.axis_index("core")
+    return pl.multiple_of((1 - core) * 2 * half, 8), pl.multiple_of(core * 2 * half, 8)
+
+
+def cut(wide, col, side):
+    length = wide.shape[1]
+    return pltpu.roll(wide, lax.rem(length - col, length), 1)[:, :side]
+
+
+def edges_kernel(own, to_left, to_right):
+    half = own.shape[2]
+    cols = own.shape[3]
+    for layer in range(2):
+        for part in range(2):
+            mine = pl.ds(part * half, half)
+            to_left[layer, :, mine] = own[part, layer, :, 0:half]
+            to_right[layer, :, mine] = own[part, layer, :, cols - half : cols]
+
+
+def widened(own, from_left, from_right, part, layer):
+    half = own.shape[2]
+    mine = pl.ds(part * half, half)
+    return jnp.concatenate(
+        [from_left[layer, :, mine], own[part, layer], from_right[layer, :, mine]], axis=1
+    )
+
+
+def beyond_kernel(scan_beyond, own, from_left, from_right, to_beyond):
+    rows, cols = own.shape[2], own.shape[3]
+    side = to_beyond.shape[1]
+    half = side // 2
+    unused, col = place_of(scan_beyond, rows, cols, half)
+    col = jnp.clip(col, 0, cols - 1)
+    for layer in range(2):
+        for part in range(2):
+            at = pl.ds((2 * part + layer) * rows, rows)
+            wide = widened(own, from_left, from_right, part, layer)
+            to_beyond[at, :] = cut(wide, col, side)
+
+
+def core_kernel(own, from_left, from_right, to_core):
+    rows = own.shape[2]
+    for layer in range(2):
+        for part in range(2):
+            at = pl.ds((2 * part + layer) * rows, rows)
+            to_core[at, :] = widened(own, from_left, from_right, part, layer)
+
+
+def near_kernel(scan, own, from_left, from_right, other, probe, pattern, tabs, near):
+    rows, cols = own.shape[2], own.shape[3]
+    side = near.shape[2]
+    half = side // 2
+    unused, col = place_of(scan, rows, cols, half)
+    for layer in range(2):
+        for part in range(2):
+            plane = 2 * part + layer
+            near[plane, 0:rows, :] = cut(widened(own, from_left, from_right, part, layer), col, side)
+            near[plane, rows : 2 * rows, :] = cut(other[pl.ds(plane * rows, rows), :], col, side)
+
+
 def main_kernel(
-    place, own, other, beyond, from_left, from_right, probe, pattern, tabs,
-    keep, message_core, message_beyond, own_strip, extended, shifted,
+    scan, live, near, beyond, probe, pattern, tabs,
+    keep, message_core, message_beyond, own_strip, column, shifted,
 ):
-    row, col, core, live = place[0], place[1], place[2], place[3]
     side = probe.shape[-1]
     half = side // 2
-    rows, cols = own.shape[2], own.shape[3]
+    rows = beyond.shape[0] // 4
+    cols = TILE_COLS
     modes = probe.shape[1]
-    other_at = pl.multiple_of((1 - core) * 2 * half, 8)
-    beyond_at = pl.multiple_of(core * 2 * half, 8)
-    for layer in range(2):
-        for part in range(2):
-            plane = 2 * part + layer
-            inner = pl.ds(half, cols)
-            extended[plane, half : half + rows, inner] = own[part, layer]
-            extended[plane, pl.ds(other_at, rows), inner] = other[part, layer]
-            extended[plane, pl.ds(beyond_at, rows), inner] = beyond[part, layer]
-            mine = pl.ds(part * half, half)
-            extended[plane, :, 0:half] = from_left[layer, :, mine]
-            extended[plane, :, half + cols : 2 * half + cols] = from_right[layer, :, mine]
-
+    row, col = place_of(scan, rows, cols, half)
+    other_at, beyond_at = strips_at(half)
+    for plane in range(4):
+        column[plane, half : half + rows, :] = near[plane, 0:rows, :]
+        column[plane, pl.ds(other_at, rows), :] = near[plane, rows : 2 * rows, :]
+        column[plane, pl.ds(beyond_at, rows), :] = beyond[pl.ds(plane * rows, rows), :]
     tall = side + 8
     step = lax.rem(row, 8)
     base_row = pl.multiple_of(row - step, 8)
 
     def window_of(plane):
-        wide = extended[plane, pl.ds(base_row, tall), :]
-        narrow = pltpu.roll(wide, lax.rem(wide.shape[1] - col, wide.shape[1]), 1)[:, :side]
-        return pltpu.roll(narrow, lax.rem(tall - step, tall), 0)[:side]
+        high = column[plane, pl.ds(base_row, tall), :]
+        return pltpu.roll(high, lax.rem(tall - step, tall), 0)[:side]
 
     window = [[window_of(2 * part + layer) for layer in range(2)] for part in range(2)]
     fields = [[probe[part, m] for m in range(modes)] for part in range(2)]
-    weight = live.astype(jnp.float32)
-    window_grad, probe_grad = model(
-        window, fields, pattern[0, 0, 0], weight, tabs
-    )
-    first = core == 0
+    weight = (live[0] > 0).astype(jnp.float32)
+    window_grad, probe_grad = model(window, fields, pattern[0, 0, 0], weight, tabs)
+    first = lax.axis_index("core") == 0
     for m in range(modes):
         at = pl.ds(m * side, side)
         real, imaginary = probe_grad[m]
@@ -184,29 +242,16 @@
                 [window_grad[part][layer], jnp.zeros((8, side), jnp.float32)], axis=0
             )
             shifted[plane, pl.ds(base_row, tall), :] = pltpu.roll(padded, step, 0)
+            at = pl.ds(plane * rows, rows)
             message_core[pl.ds(base + plane * rows, rows), :] = shifted[plane, pl.ds(other_at, rows), :]
-            message_beyond[pl.ds(plane * rows, rows), :] = shifted[plane, pl.ds(beyond_at, rows), :]
-            own_strip[pl.ds(plane * rows, rows), :] = shifted[plane, half : half + rows, :]
+            message_beyond[at, :] = shifted[plane, pl.ds(beyond_at, rows), :]
+            own_strip[at, :] = shifted[plane, half : half + rows, :]
     offset = jnp.full((8, side), col.astype(jnp.float32))
     message_core[pl.ds(base + 4 * rows, 8), :] = offset
     message_beyond[pl.ds(4 * rows, 8), :] = offset
 
 
-def pack_kernel(place, own, other, beyond, to_left, to_right):
-    core = place[2]
-    half = own.shape[2]
-    cols = own.shape[3]
-    other_at = pl.multiple_of((1 - core) * 2 * half, 8)
-    beyond_at = pl.multiple_of(core * 2 * half, 8)
-    for source, at in ((own, half), (other, other_at), (beyond, beyond_at)):
-        for layer in range(2):
-            for part in range(2):
-                mine = pl.ds(part * half, half)
-                to_left[layer, pl.ds(at, half), mine] = source[part, layer, :, 0:half]
-                to_right[layer, pl.ds(at, half), mine] = source[part, layer, :, cols - half : cols]
-
-
-def merge_kernel(place, own_strip, from_core, from_beyond, centre, to_left, to_right):
+def merge_kernel(scan, own_strip, from_core, from_beyond, centre, to_left, to_right):
     side = own_strip.shape[1]
     half = side // 2
     rows = centre.shape[2]
@@ -215,6 +260,7 @@
     base = from_core.shape[0] - from_beyond.shape[0]
     core_col = jnp.max(from_core[pl.ds(base + 4 * rows, 8), :]).astype(jnp.int32)
     beyond_col = jnp.max(from_beyond[pl.ds(4 * rows, 8), :]).astype(jnp.int32)
+    unused, own_col = place_of(scan, rows, cols, half)
     gap = jnp.zeros((rows, cols), jnp.float32)
 
     def placed(strip, col):
@@ -223,7 +269,7 @@
     for layer in range(2):
         for part in range(2):
             plane = 2 * part + layer
-            total = placed(own_strip[pl.ds(plane * rows, rows), :], place[1])
+            total = placed(own_strip[pl.ds(plane * rows, rows), :], own_col)
             total = total + placed(from_core[pl.ds(base + plane * rows, rows), :], core_col)
             total = total + placed(from_beyond[pl.ds(plane * rows, rows), :], beyond_col)
             centre[part, layer] = total[:, half : half + cols]
@@ -270,26 +316,37 @@
     n_row, n_col = lax.axis_size(ROW), lax.axis_size(COL)
     f32 = jnp.float32
     core = lax.axis_index("core")
-    row = scan_pos[0, 0, 0, 0] - (lax.axis_index(ROW) * rows - half)
-    col = scan_pos[0, 0, 0, 1] - (lax.axis_index(COL) * cols - half)
-    live = (live_count[0, 0] > 0).astype(jnp.int32)
-    place = jnp.stack([row, col, core, live]).astype(jnp.int32)
+    scan = scan_pos.reshape(2)
+    live = live_count.reshape(1)
     swap = [(0, 1), (1, 0)]
     pairs = [(i, i + 1) for i in range(1, n_row - 1, 2)]
     pairs = pairs + [(j, i) for i, j in pairs]
+    strip = 4 * rows
 
     def shape(*dims):
         return jax.ShapeDtypeStruct(dims, f32)
 
-    beyond = lax.ppermute(obj_field, ROW, pairs)
-    other = lax.ppermute(obj_field, "core", swap)
-    column = shape(2, 2 * half + rows, side)
-    to_left, to_right = call(pack_kernel, [column, column], 1, 3)(place, obj_field, other, beyond)
+    scan_beyond = lax.ppermute(scan, ROW, pairs)
+    edge = shape(2, rows, side)
+    to_left, to_right = call(edges_kernel, [edge, edge], 0, 1)(obj_field)
     from_left = lax.ppermute(to_right, COL, chain(n_col, 1))
     from_right = lax.ppermute(to_left, COL, chain(n_col, -1))
-
+    to_beyond = call(beyond_kernel, shape(strip, side), 1, 3)(
+        scan_beyond, obj_field, from_left, from_right
+    )
+    beyond = lax.ppermute(to_beyond, ROW, pairs)
+    to_beyond_first, own_edge = lax.optimization_barrier((to_beyond, from_left))
+    small = pl.CostEstimate(flops=1000, bytes_accessed=1000, transcendentals=0)
+    to_core = call(core_kernel, shape(strip, 2 * half + cols), 0, 3, cost=small)(
+        obj_field, own_edge, from_right
+    )
+    other = lax.ppermute(to_core, "core", swap)
     tabs = jnp.asarray(tables(side))
-    strip = 4 * rows
+    near = call(near_kernel, shape(4, 2 * rows, side), 1, 7, cost=small)(
+        scan, obj_field, from_left, from_right, other, probe, patterns, tabs
+    )
+    near, beyond = lax.optimization_barrier((near, beyond))
+    tall = pltpu.VMEM((4, 2 * half + rows, side), f32)
     keep, message_core, message_beyond, own_strip = call(
         main_kernel,
         [
@@ -298,13 +355,10 @@
             shape(strip + 8, side),
             shape(strip, side),
         ],
-        1,
-        8,
-        [
-            pltpu.VMEM((4, 2 * half + rows, 2 * half + cols), f32),
-            pltpu.VMEM((4, 2 * half + rows, side), f32),
-        ],
-    )(place, obj_field, other, beyond, from_left, from_right, probe, patterns, tabs)
+        2,
+        5,
+        [tall, tall],
+    )(scan, live, near, beyond, probe, patterns, tabs)
 
     from_core = lax.ppermute(message_core, "core", swap)
     from_beyond = lax.ppermute(message_beyond, ROW, pairs)
@@ -316,18 +370,17 @@
     summed = keep + from_core[:total]
     spread = lax.all_to_all(summed.reshape(n_yx, chunk, side), ("y", "x"), 0, 0)
 
-    edge = shape(2, rows, side)
     centre, grad_left, grad_right = call(
         merge_kernel, [shape(2, 2, rows, cols), edge, edge], 1, 3
-    )(place, own_strip, from_core, from_beyond)
+    )(scan, own_strip, from_core, from_beyond)
     part = jnp.sum(spread, axis=0)
-    part, grad_left, grad_right = lax.optimization_barrier((part, grad_left, grad_right))
-    got_left = lax.ppermute(grad_right, COL, chain(n_col, 1))
-    got_right = lax.ppermute(grad_left, COL, chain(n_col, -1))
     part = lax.all_to_all(jnp.broadcast_to(part, (n_z, chunk, side)), ("zh", "zl"), 0, 0)
     part = jnp.sum(part, axis=0)
-    part, got_left, got_right = lax.optimization_barrier((part, got_left, got_right))
+    got_left = lax.ppermute(grad_right, COL, chain(n_col, 1))
+    part, got_left, grad_left = lax.optimization_barrier((part, got_left, grad_left))
+    got_right = lax.ppermute(grad_left, COL, chain(n_col, -1))
     whole = lax.all_to_all(jnp.broadcast_to(part, (n_yx, chunk, side)), ("y", "x"), 0, 0)
+    whole, got_right = lax.optimization_barrier((whole, got_right))
     whole = whole.reshape(modes, side, side)
     facing = lax.ppermute(whole, "core", swap)
     first = core == 0

time: 119 us -> 111 us (0.933)
  blocking collectives: 20.9 us -> 0 us
  starting transfers between devices: 60.3 us -> 75.3 us
  local copies, waits for them, and re-layouts: 3.91 us -> 2.32 us
    all_to_all x1 -> x0, blocking collectives: 20.9 us -> none  [body(): lax.all_to_all(jnp.broadcast_to(part, (n_yx, chunk, side)), ('y', 'x'), 0...]
    ppermute x2 -> x3, starting transfers between devices: 14 us -> 20.5 us  [the longest x1 10.6 us: body(): scan_beyond = lax.ppermute(scan, ROW, pairs)]
    all_to_all x0 -> x1, starting transfers between devices: none -> 6.33 us  [body(): lax.all_to_all(jnp.broadcast_to(part, (n_yx, chunk, side)), ('y', 'x'), 0...]
    all_to_all x1, starting transfers between devices: 11 us -> 16.7 us  [body(): spread = lax.all_to_all(summed.reshape(n_yx, chunk, side), ('y', 'x'), 0, 0)]
    all_to_all x0 -> x1, waiting for transfers between devices: none -> 5.39 us  [body(): lax.all_to_all(jnp.broadcast_to(part, (n_yx, chunk, side)), ('y', 'x'), 0...]
    all_to_all x1, waiting for transfers between devices: 0.01 us -> 4.52 us  [body(): spread = lax.all_to_all(summed.reshape(n_yx, chunk, side), ('y', 'x'), 0, 0)]
    ppermute x1, waiting for transfers between devices: 4.41 us -> 0.01 us  [body(): from_beyond = lax.ppermute(message_beyond, ROW, pairs)]
    ppermute x1, waiting for transfers between devices: 4.29 us -> 0.01 us  [body(): from_right = lax.ppermute(to_left, COL, chain(n_col, -1))]
  transfers between devices with their start and end apart: 11 -> 13, of which waited for: 8 -> 8; matrix products, arithmetic and copies ran while one was open for 1% -> 1% of each run, Pallas kernels for 1% -> 3%
where the time goes in v2:
time: 111 us; the launch traced here: 110 us
  starting transfers between devices  75.3 us (68%)
  waiting for transfers between devices  20.6 us (19%)
  Pallas kernels  8.79 us (8%)
  local copies, waits for them, and re-layouts  2.32 us (2%)
  other arithmetic  1.67 us (2%)
  between operations  1.52 us (1%)
    all_to_all x1, starting transfers between devices, body(): spread = lax.all_to_all(summed.reshape(n_yx, chunk, side), ('y', 'x'), 0, 0)  16.7 us
    ppermute x1, starting transfers between devices, body(): scan_beyond = lax.ppermute(scan, ROW, pairs)  10.6 us
    ppermute x1, starting transfers between devices, body(): beyond = lax.ppermute(to_beyond, ROW, pairs)  7.99 us
    ppermute x1, starting transfers between devices, body(): from_beyond = lax.ppermute(message_beyond, ROW, pairs)  7.05 us
    all_to_all x1, starting transfers between devices, body(): lax.all_to_all(jnp.broadcast_to(part, (n_yx, chunk, side)), ('y', 'x'), 0...  6.33 us
    ppermute x1, starting transfers between devices, body(): facing = lax.ppermute(whole, 'core', swap)  6.15 us
    all_to_all x1, starting transfers between devices, body(): lax.all_to_all(jnp.broadcast_to(part, (n_z, chunk, side)), ('zh', 'zl'),...  5.88 us
    all_to_all x1, waiting for transfers between devices, body(): lax.all_to_all(jnp.broadcast_to(part, (n_yx, chunk, side)), ('y', 'x'), 0...  5.39 us
  transfers between devices with their start and end apart: 13, of which 8 were waited for; matrix products, arithmetic and copies ran while one was open for 1% of the time, Pallas kernels for 3%

profile of v2, /device:TPU:1, one launch (start us, length us, event | category | flops | bytes accessed | tf_op | source)
XLA Modules:
  0.0 110.2 jit_solution(16938875980718171627)
XLA Ops:
  0.6 0.9 copy-done
  1.7 4.8 %collective-permute-start = (f32[2,64,128]{2,1,0:T(8,128)S(1)}, f32[2,64,128]{2,1,0:T(8,128)S(1)}, u32[]{:S(2)}, u32[]{:S(2)}) collective-permute-start(f32[2,64,128]{2,1,0:T(8,128)S(1)} %get-tuple-element.19), channel_id=1, source_target_pairs={{0,1},{1,2},{2,3},{3,4},{4,5},{5,6},{6,7},{7,8},{8,9},{9,10},{10,1... | collective-permute-start | bytes 196616 | tf_op jit(solution)/shard_map/ppermute | solution.py:332
  6.5 1.3 %collective-permute-start.1 = (f32[2,64,128]{2,1,0:T(8,128)S(1)}, f32[2,64,128]{2,1,0:T(8,128)S(1)}, u32[]{:S(2)}, u32[]{:S(2)}) collective-permute-start(f32[2,64,128]{2,1,0:T(8,128)S(1)} %get-tuple-element.20), channel_id=1, source_target_pairs={{1,0},{2,1},{3,2},{4,3},{5,4},{6,5},{7,6},{8,7},{9,8},{10,9},{11,1... | collective-permute-start | bytes 196616 | tf_op jit(solution)/shard_map/ppermute | solution.py:333
  7.8 10.6 %collective-permute-start.2 = (s32[2]{0:T(128)S(1)}, s32[2]{0:T(128)S(1)}, u32[]{:S(2)}, u32[]{:S(2)}) collective-permute-start(s32[2]{0:T(128)S(1)} %bitcast.12), channel_id=1, source_target_pairs={{16,32},{48,64},{80,96},{112,128},{144,160},{176,192},{208,224},{2... | collective-permute-start | bytes 32 | tf_op jit(solution)/shard_map/ppermute | solution.py:329
  18.4 1.2 %collective-permute-done.2.scan_beyond = s32[2]{0:T(128)S(1)} collective-permute-done((s32[2]{0:T(128)S(1)}, s32[2]{0:T(128)S(1)}, u32[]{:S(2)}, u32[]{:S(2)}) %collective-permute-start.2) | collective-permute-done | bytes 40 | tf_op jit(solution)/shard_map/ppermute | solution.py:329
  19.6 1.0 shard_map.78
  20.8 1.9 %collective-permute-start.3 = (f32[256,384]{1,0:T(8,128)S(1)}, f32[256,384]{1,0:T(8,128)S(1)}, u32[]{:S(2)}, u32[]{:S(2)}) collective-permute-start(f32[256,384]{1,0:T(8,128)S(1)} %shard_map.79), channel_id=1, source_target_pairs={{0,16},{16,0},{1,17},{17,1},{2,18},{18,2},{3,19},{19,3},{4,20},{20... | collective-permute-start | bytes 1179656 | tf_op jit(solution)/shard_map/ppermute | solution.py:343
  22.8 8.0 %collective-permute-start.4 = (f32[256,128]{1,0:T(8,128)S(1)}, f32[256,128]{1,0:T(8,128)S(1)}, u32[]{:S(2)}, u32[]{:S(2)}) collective-permute-start(f32[256,128]{1,0:T(8,128)S(1)} %shard_map.78), channel_id=1, source_target_pairs={{16,32},{48,64},{80,96},{112,128},{144,160},{176,192},{208,224},{2... | collective-permute-start | bytes 393224 | tf_op jit(solution)/shard_map/ppermute | solution.py:337
  31.5 1.1 %shard_map.80.near = f32[4,128,128]{2,1,0:T(8,128)S(1)} custom-call(s32[2]{0:T(128)S(1)} %bitcast.13, f32[2,2,64,256]{3,2,1,0:T(8,128)S(1)} %copy-done, f32[2,64,128]{2,1,0:T(8,128)S(1)} %collective-permute-done.from_left, f32[2,64,128]{2,1,0:T(8,128)S(1)} %collective-permute-done.1.from_right, f32[256,384]{1,0:T(8,128)S(1)} %collective-permute-done.3.other, ...), custom_call_target="tpu_custom_call" | custom-call | flops 1000 | bytes 1000 | tf_op jit(solution)/shard_map/pallas_call | solution.py:345
  33.5 4.7 %shard_map.81 = (f32[512,128]{1,0:T(8,128)S(1)}, f32[776,128]{1,0:T(8,128)S(1)}, f32[264,128]{1,0:T(8,128)S(1)}, f32[256,128]{1,0:T(8,128)S(1)}) custom-call(s32[2]{0:T(128)S(1)} %bitcast.14, s32[1]{0:T(128)} %bitcast.11.live, f32[4,128,128]{2,1,0:T(8,128)S(1)} %shard_map.80.near, f32[256,128]{1,0:T(8,128)S(1)} %collective-permute-done.4.beyond, ...), custom_call_target="tpu_custom_call" | custom-call | tf_op jit(solution)/shard_map/pallas_call | solution.py:350
  38.1 1.9 %collective-permute-start.5 = (f32[776,128]{1,0:T(8,128)S(1)}, f32[776,128]{1,0:T(8,128)S(1)}, u32[]{:S(2)}, u32[]{:S(2)}) collective-permute-start(f32[776,128]{1,0:T(8,128)S(1)} %get-tuple-element.25), channel_id=1, source_target_pairs={{0,16},{16,0},{1,17},{17,1},{2,18},{18,2},{3,19},{19,3},{4,20},{20... | collective-permute-start | bytes 1191944 | tf_op jit(solution)/shard_map/ppermute | solution.py:363
  40.1 1.7 %collective-permute-done.5.from_core = f32[776,128]{1,0:T(8,128)S(1)} collective-permute-done((f32[776,128]{1,0:T(8,128)S(1)}, f32[776,128]{1,0:T(8,128)S(1)}, u32[]{:S(2)}, u32[]{:S(2)}) %collective-permute-start.5) | collective-permute-done | bytes 397344 | tf_op jit(solution)/shard_map/ppermute | solution.py:363
  42.5 16.7 %all-to-all-start = ((f32[32,16,128]{2,1,0:T(8,128)}), f32[32,16,128]{2,1,0:T(8,128)S(1)}, u32[]{:S(2)}, u32[]{:S(2)}) async-start(f32[32,16,128]{2,1,0:T(8,128)} %bitcast.2), calls=%async_computation | async-start | bytes 524288 | tf_op jit(solution)/shard_map/all_to_all | solution.py:371
  59.2 7.0 %collective-permute-start.6 = (f32[264,128]{1,0:T(8,128)S(1)}, f32[264,128]{1,0:T(8,128)S(1)}, u32[]{:S(2)}, u32[]{:S(2)}) collective-permute-start(f32[264,128]{1,0:T(8,128)S(1)} %get-tuple-element.26), channel_id=1, source_target_pairs={{16,32},{48,64},{80,96},{112,128},{144,160},{176,192},{208,224},{2... | collective-permute-start | bytes 405512 | tf_op jit(solution)/shard_map/ppermute | solution.py:364
  66.3 4.5 %all-to-all-done = f32[32,16,128]{2,1,0:T(8,128)S(1)} async-done(((f32[32,16,128]{2,1,0:T(8,128)}), f32[32,16,128]{2,1,0:T(8,128)S(1)}, u32[]{:S(2)}, u32[]{:S(2)}) %all-to-all-start) | async-done | bytes 262176 | tf_op jit(solution)/shard_map/all_to_all | solution.py:371
  71.5 5.9 %all-to-all-start.1 = ((f32[8,16,128]{2,1,0:T(8,128)}), f32[8,16,128]{2,1,0:T(8,128)S(1)}, u32[]{:S(2)}, u32[]{:S(2)}) async-start(f32[8,16,128]{2,1,0:T(8,128)} %broadcast_in_dim.6), calls=%async_computation.1 | async-start | bytes 131072 | tf_op jit(solution)/shard_map/all_to_all | solution.py:377
  77.3 1.0 shard_map.82
  78.3 3.4 %collective-permute-start.7 = (f32[2,64,128]{2,1,0:T(8,128)S(1)}, f32[2,64,128]{2,1,0:T(8,128)S(1)}, u32[]{:S(2)}, u32[]{:S(2)}) collective-permute-start(f32[2,64,128]{2,1,0:T(8,128)S(1)} %get-tuple-element.29), channel_id=1, source_target_pairs={{0,1},{1,2},{2,3},{3,4},{4,5},{5,6},{6,7},{7,8},{8,9},{9,10},{10,1... | collective-permute-start | bytes 196616 | tf_op jit(solution)/shard_map/ppermute | solution.py:379
  81.7 2.9 %all-to-all-done.1 = f32[8,16,128]{2,1,0:T(8,128)S(1)} async-done(((f32[8,16,128]{2,1,0:T(8,128)}), f32[8,16,128]{2,1,0:T(8,128)S(1)}, u32[]{:S(2)}, u32[]{:S(2)}) %all-to-all-start.1) | async-done | bytes 65568 | tf_op jit(solution)/shard_map/all_to_all | solution.py:377
  85.3 6.3 %all-to-all-start.2 = ((f32[32,16,128]{2,1,0:T(8,128)}), f32[32,16,128]{2,1,0:T(8,128)S(1)}, u32[]{:S(2)}, u32[]{:S(2)}) async-start(f32[32,16,128]{2,1,0:T(8,128)} %broadcast_in_dim.7), calls=%async_computation.2 | async-start | bytes 524288 | tf_op jit(solution)/shard_map/all_to_all | solution.py:382
  91.7 1.3 %collective-permute-start.8 = (f32[2,64,128]{2,1,0:T(8,128)S(1)}, f32[2,64,128]{2,1,0:T(8,128)S(1)}, u32[]{:S(2)}, u32[]{:S(2)}) collective-permute-start(f32[2,64,128]{2,1,0:T(8,128)S(1)} %get-tuple-element.33), channel_id=1, source_target_pairs={{1,0},{2,1},{3,2},{4,3},{5,4},{6,5},{7,6},{8,7},{9,8},{10,9},{11,1... | collective-permute-start | bytes 196616 | tf_op jit(solution)/shard_map/ppermute | solution.py:381
  93.0 3.7 %collective-permute-done.8.from_right = f32[2,64,128]{2,1,0:T(8,128)S(1)} collective-permute-done((f32[2,64,128]{2,1,0:T(8,128)S(1)}, f32[2,64,128]{2,1,0:T(8,128)S(1)}, u32[]{:S(2)}, u32[]{:S(2)}) %collective-permute-start.8) | collective-permute-done | bytes 65568 | tf_op jit(solution)/shard_map/ppermute | solution.py:381
  96.7 5.4 %all-to-all-done.2 = f32[32,16,128]{2,1,0:T(8,128)S(1)} async-done(((f32[32,16,128]{2,1,0:T(8,128)}), f32[32,16,128]{2,1,0:T(8,128)S(1)}, u32[]{:S(2)}, u32[]{:S(2)}) %all-to-all-start.2) | async-done | bytes 262176 | tf_op jit(solution)/shard_map/all_to_all | solution.py:382
  102.1 6.2 %collective-permute-start.9 = (f32[4,128,128]{2,1,0:T(8,128)S(1)}, f32[4,128,128]{2,1,0:T(8,128)S(1)}, u32[]{:S(2)}, u32[]{:S(2)}) collective-permute-start(f32[4,128,128]{2,1,0:T(8,128)S(1)} %bitcast.16), channel_id=1, source_target_pairs={{0,16},{16,0},{1,17},{17,1},{2,18},{18,2},{3,19},{19,3},{4,20},{20... | collective-permute-start | bytes 786440 | tf_op jit(solution)/shard_map/ppermute | solution.py:385
  (26 shorter events, 5.3 us)
Async XLA Ops:
  0.6 1.0 copy-start
  1.7 18.0 %collective-permute-start = (f32[2,64,128]{2,1,0:T(8,128)S(1)}, f32[2,64,128]{2,1,0:T(8,128)S(1)}, u32[]{:S(2)}, u32[]{:S(2)}) collective-permute-start(f32[2,64,128]{2,1,0:T(8,128)S(1)} %get-tuple-element.19), channel_id=1, source_target_pairs={{0,1},{1,2},{2,3},{3,4},{4,5},{5,6},{6,7},{7,8},{8,9},{9,10},{10,1... | collective-permute-start | bytes 196616 | tf_op jit(solution)/shard_map/ppermute | solution.py:332
  6.5 1.3 %copy-start.4 = (s32[1,1,1,2]{3,2,1,0:T(1,128)S(1)}, s32[1,1,1,2]{3,2,1,0:T(1,128)}, u32[]{:S(2)}) copy-start(s32[1,1,1,2]{3,2,1,0:T(1,128)} %param.8) | copy-start | bytes 28
  6.5 13.1 %collective-permute-start.1 = (f32[2,64,128]{2,1,0:T(8,128)S(1)}, f32[2,64,128]{2,1,0:T(8,128)S(1)}, u32[]{:S(2)}, u32[]{:S(2)}) collective-permute-start(f32[2,64,128]{2,1,0:T(8,128)S(1)} %get-tuple-element.20), channel_id=1, source_target_pairs={{1,0},{2,1},{3,2},{4,3},{5,4},{6,5},{7,6},{8,7},{9,8},{10,9},{11,1... | collective-permute-start | bytes 196616 | tf_op jit(solution)/shard_map/ppermute | solution.py:333
  7.8 11.8 %collective-permute-start.2 = (s32[2]{0:T(128)S(1)}, s32[2]{0:T(128)S(1)}, u32[]{:S(2)}, u32[]{:S(2)}) collective-permute-start(s32[2]{0:T(128)S(1)} %bitcast.12), channel_id=1, source_target_pairs={{16,32},{48,64},{80,96},{112,128},{144,160},{176,192},{208,224},{2... | collective-permute-start | bytes 32 | tf_op jit(solution)/shard_map/ppermute | solution.py:329
  19.6 11.8 %copy-start.2 = (bf16[12,128,128]{2,1,0:T(8,128)(2,1)S(1)}, bf16[12,128,128]{2,1,0:T(8,128)(2,1)}, u32[]{:S(2)}) copy-start(bf16[12,128,128]{2,1,0:T(8,128)(2,1)} %constant.12.clone.tabs) | copy-start | bytes 1179652
  20.6 10.8 %copy-start.1 = (f32[2,4,128,128]{3,2,1,0:T(8,128)S(1)}, f32[2,4,128,128]{3,2,1,0:T(8,128)}, u32[]{:S(2)}) copy-start(f32[2,4,128,128]{3,2,1,0:T(8,128)} %probe.3) | copy-start | bytes 1572868
  20.6 10.8 %copy-start.3 = (f32[1,1,1,128,128]{4,3,2,1,0:T(8,128)S(1)}, f32[1,1,1,128,128]{4,3,2,1,0:T(8,128)}, u32[]{:S(2)}) copy-start(f32[1,1,1,128,128]{4,3,2,1,0:T(8,128)} %pattern.3) | copy-start | bytes 196612
  20.8 10.6 %collective-permute-start.3 = (f32[256,384]{1,0:T(8,128)S(1)}, f32[256,384]{1,0:T(8,128)S(1)}, u32[]{:S(2)}, u32[]{:S(2)}) collective-permute-start(f32[256,384]{1,0:T(8,128)S(1)} %shard_map.79), channel_id=1, source_target_pairs={{0,16},{16,0},{1,17},{17,1},{2,18},{18,2},{3,19},{19,3},{4,20},{20... | collective-permute-start | bytes 1179656 | tf_op jit(solution)/shard_map/ppermute | solution.py:343
  22.8 10.7 %collective-permute-start.4 = (f32[256,128]{1,0:T(8,128)S(1)}, f32[256,128]{1,0:T(8,128)S(1)}, u32[]{:S(2)}, u32[]{:S(2)}) collective-permute-start(f32[256,128]{1,0:T(8,128)S(1)} %shard_map.78), channel_id=1, source_target_pairs={{16,32},{48,64},{80,96},{112,128},{144,160},{176,192},{208,224},{2... | collective-permute-start | bytes 393224 | tf_op jit(solution)/shard_map/ppermute | solution.py:337
  38.1 3.6 %collective-permute-start.5 = (f32[776,128]{1,0:T(8,128)S(1)}, f32[776,128]{1,0:T(8,128)S(1)}, u32[]{:S(2)}, u32[]{:S(2)}) collective-permute-start(f32[776,128]{1,0:T(8,128)S(1)} %get-tuple-element.25), channel_id=1, source_target_pairs={{0,16},{16,0},{1,17},{17,1},{2,18},{18,2},{3,19},{19,3},{4,20},{20... | collective-permute-start | bytes 1191944 | tf_op jit(solution)/shard_map/ppermute | solution.py:363
  42.5 28.3 %all-to-all-start = ((f32[32,16,128]{2,1,0:T(8,128)}), f32[32,16,128]{2,1,0:T(8,128)S(1)}, u32[]{:S(2)}, u32[]{:S(2)}) async-start(f32[32,16,128]{2,1,0:T(8,128)} %bitcast.2), calls=%async_computation | async-start | bytes 524288 | tf_op jit(solution)/shard_map/all_to_all | solution.py:371
  59.2 18.1 %collective-permute-start.6 = (f32[264,128]{1,0:T(8,128)S(1)}, f32[264,128]{1,0:T(8,128)S(1)}, u32[]{:S(2)}, u32[]{:S(2)}) collective-permute-start(f32[264,128]{1,0:T(8,128)S(1)} %get-tuple-element.26), channel_id=1, source_target_pairs={{16,32},{48,64},{80,96},{112,128},{144,160},{176,192},{208,224},{2... | collective-permute-start | bytes 405512 | tf_op jit(solution)/shard_map/ppermute | solution.py:364
  71.5 13.1 %all-to-all-start.1 = ((f32[8,16,128]{2,1,0:T(8,128)}), f32[8,16,128]{2,1,0:T(8,128)S(1)}, u32[]{:S(2)}, u32[]{:S(2)}) async-start(f32[8,16,128]{2,1,0:T(8,128)} %broadcast_in_dim.6), calls=%async_computation.1 | async-start | bytes 131072 | tf_op jit(solution)/shard_map/all_to_all | solution.py:377
  78.3 6.3 %collective-permute-start.7 = (f32[2,64,128]{2,1,0:T(8,128)S(1)}, f32[2,64,128]{2,1,0:T(8,128)S(1)}, u32[]{:S(2)}, u32[]{:S(2)}) collective-permute-start(f32[2,64,128]{2,1,0:T(8,128)S(1)} %get-tuple-element.29), channel_id=1, source_target_pairs={{0,1},{1,2},{2,3},{3,4},{4,5},{5,6},{6,7},{7,8},{8,9},{9,10},{10,1... | collective-permute-start | bytes 196616 | tf_op jit(solution)/shard_map/ppermute | solution.py:379
  85.3 16.7 %all-to-all-start.2 = ((f32[32,16,128]{2,1,0:T(8,128)}), f32[32,16,128]{2,1,0:T(8,128)S(1)}, u32[]{:S(2)}, u32[]{:S(2)}) async-start(f32[32,16,128]{2,1,0:T(8,128)} %broadcast_in_dim.7), calls=%async_computation.2 | async-start | bytes 524288 | tf_op jit(solution)/shard_map/all_to_all | solution.py:382
  91.7 5.0 %collective-permute-start.8 = (f32[2,64,128]{2,1,0:T(8,128)S(1)}, f32[2,64,128]{2,1,0:T(8,128)S(1)}, u32[]{:S(2)}, u32[]{:S(2)}) collective-permute-start(f32[2,64,128]{2,1,0:T(8,128)S(1)} %get-tuple-element.33), channel_id=1, source_target_pairs={{1,0},{2,1},{3,2},{4,3},{5,4},{6,5},{7,6},{8,7},{9,8},{10,9},{11,1... | collective-permute-start | bytes 196616 | tf_op jit(solution)/shard_map/ppermute | solution.py:381
  102.1 7.3 %collective-permute-start.9 = (f32[4,128,128]{2,1,0:T(8,128)S(1)}, f32[4,128,128]{2,1,0:T(8,128)S(1)}, u32[]{:S(2)}, u32[]{:S(2)}) collective-permute-start(f32[4,128,128]{2,1,0:T(8,128)S(1)} %bitcast.16), channel_id=1, source_target_pairs={{0,16},{16,0},{1,17},{17,1},{2,18},{18,2},{3,19},{19,3},{4,20},{20... | collective-permute-start | bytes 786440 | tf_op jit(solution)/shard_map/ppermute | solution.py:385

commit v3 on v2

--- a/solution.py
+++ b/solution.py
@@ -144,30 +144,44 @@
     return pl.multiple_of((1 - core) * 2 * half, 8), pl.multiple_of(core * 2 * half, 8)
 
 
-def cut(wide, col, side):
-    length = wide.shape[1]
-    return pltpu.roll(wide, lax.rem(length - col, length), 1)[:, :side]
-
-
-def edges_kernel(own, to_left, to_right):
-    half = own.shape[2]
+def even_col():
+    return lax.rem(lax.axis_index(COL), 2) == 0
+
+
+def fill(frame, own, with_even, with_odd, part, layer):
+    side = with_even.shape[2]
+    half = side // 2
     cols = own.shape[3]
+    plane = 2 * part + layer
+    left = jnp.where(even_col(), with_odd[layer], with_even[layer])
+    right = jnp.where(even_col(), with_even[layer], with_odd[layer])
+    if part:
+        left, right = pltpu.roll(left, half, 1), pltpu.roll(right, half, 1)
+    frame[plane, :, 0:side] = left
+    frame[plane, :, side : side + cols] = own[part, layer]
+    frame[plane, :, side + cols :] = right
+
+
+def cut(frame, plane, at, side):
+    step = lax.rem(at, side)
+    wide = frame[plane, :, pl.ds(pl.multiple_of(at - step, side), 2 * side)]
+    return pltpu.roll(wide, lax.rem(2 * side - step, 2 * side), 1)[:, :side]
+
+
+def edges_kernel(own, with_even, with_odd):
+    rows, cols = own.shape[2], own.shape[3]
+    side = with_even.shape[2]
+    half = side // 2
+    inner = lax.broadcasted_iota(jnp.int32, (rows, side), 1) < half
     for layer in range(2):
-        for part in range(2):
-            mine = pl.ds(part * half, half)
-            to_left[layer, :, mine] = own[part, layer, :, 0:half]
-            to_right[layer, :, mine] = own[part, layer, :, cols - half : cols]
-
-
-def widened(own, from_left, from_right, part, layer):
-    half = own.shape[2]
-    mine = pl.ds(part * half, half)
-    return jnp.concatenate(
-        [from_left[layer, :, mine], own[part, layer], from_right[layer, :, mine]], axis=1
-    )
-
-
-def beyond_kernel(scan_beyond, own, from_left, from_right, to_beyond):
+        real, imaginary = own[0, layer], own[1, layer]
+        left = jnp.where(inner, real[:, :side], pltpu.roll(imaginary[:, :side], half, 1))
+        right = jnp.where(inner, pltpu.roll(imaginary[:, cols - side :], half, 1), real[:, cols - side :])
+        with_even[layer] = jnp.where(even_col(), right, left)
+        with_odd[layer] = jnp.where(even_col(), left, right)
+
+
+def beyond_kernel(scan_beyond, own, with_even, with_odd, to_beyond, frame):
     rows, cols = own.shape[2], own.shape[3]
     side = to_beyond.shape[1]
     half = side // 2
@@ -175,29 +189,19 @@
     col = jnp.clip(col, 0, cols - 1)
     for layer in range(2):
         for part in range(2):
-            at = pl.ds((2 * part + layer) * rows, rows)
-            wide = widened(own, from_left, from_right, part, layer)
-            to_beyond[at, :] = cut(wide, col, side)
-
-
-def core_kernel(own, from_left, from_right, to_core):
-    rows = own.shape[2]
-    for layer in range(2):
-        for part in range(2):
-            at = pl.ds((2 * part + layer) * rows, rows)
-            to_core[at, :] = widened(own, from_left, from_right, part, layer)
-
-
-def near_kernel(scan, own, from_left, from_right, other, probe, pattern, tabs, near):
-    rows, cols = own.shape[2], own.shape[3]
+            plane = 2 * part + layer
+            fill(frame, own, with_even, with_odd, part, layer)
+            to_beyond[pl.ds(plane * rows, rows), :] = cut(frame, plane, col + half, side)
+
+
+def near_kernel(scan, frame, other, probe, pattern, tabs, near):
+    rows, cols = frame.shape[1], frame.shape[2] - 2 * near.shape[2]
     side = near.shape[2]
     half = side // 2
     unused, col = place_of(scan, rows, cols, half)
-    for layer in range(2):
-        for part in range(2):
-            plane = 2 * part + layer
-            near[plane, 0:rows, :] = cut(widened(own, from_left, from_right, part, layer), col, side)
-            near[plane, rows : 2 * rows, :] = cut(other[pl.ds(plane * rows, rows), :], col, side)
+    for plane in range(4):
+        near[plane, 0:rows, :] = cut(frame, plane, col + half, side)
+        near[plane, rows : 2 * rows, :] = cut(other, plane, col + half, side)
 
 
 def main_kernel(
@@ -251,43 +255,57 @@
     message_beyond[pl.ds(4 * rows, 8), :] = offset
 
 
-def merge_kernel(scan, own_strip, from_core, from_beyond, centre, to_left, to_right):
+def merge_kernel(scan, own_strip, from_core, from_beyond, centre, with_even, with_odd, frame):
     side = own_strip.shape[1]
     half = side // 2
     rows = centre.shape[2]
     cols = centre.shape[3]
-    wide = cols + side
     base = from_core.shape[0] - from_beyond.shape[0]
     core_col = jnp.max(from_core[pl.ds(base + 4 * rows, 8), :]).astype(jnp.int32)
     beyond_col = jnp.max(from_beyond[pl.ds(4 * rows, 8), :]).astype(jnp.int32)
     unused, own_col = place_of(scan, rows, cols, half)
-    gap = jnp.zeros((rows, cols), jnp.float32)
-
-    def placed(strip, col):
-        return pltpu.roll(jnp.concatenate([strip, gap], axis=1), col, 1)
-
+    lane = lax.broadcasted_iota(jnp.int32, (rows, side), 1)
+    zero = jnp.zeros((rows, side), jnp.float32)
+    frame[...] = jnp.zeros_like(frame)
+    for source, first, col in (
+        (own_strip, 0, own_col),
+        (from_core, base, jnp.clip(core_col, 0, cols - 1)),
+        (from_beyond, 0, jnp.clip(beyond_col, 0, cols - 1)),
+    ):
+        at = col + half
+        step = lax.rem(at, side)
+        near = pl.multiple_of(at - step, side)
+        here, there = pl.ds(near, side), pl.ds(pl.multiple_of(near + side, side), side)
+        for plane in range(4):
+            strip = pltpu.roll(source[pl.ds(first + plane * rows, rows), :], step, 1)
+            frame[plane, :, here] += jnp.where(lane >= step, strip, zero)
+            frame[plane, :, there] += jnp.where(lane < step, strip, zero)
+    inner = lane < half
     for layer in range(2):
+        real, imaginary = layer, 2 + layer
+        left = jnp.where(inner, pltpu.roll(frame[imaginary, :, 0:side], half, 1), frame[real, :, 0:side])
+        right = jnp.where(inner, frame[real, :, side + cols :], pltpu.roll(frame[imaginary, :, side + cols :], half, 1))
+        with_even[layer] = jnp.where(even_col(), right, left)
+        with_odd[layer] = jnp.where(even_col(), left, right)
+        centre[0, layer] = frame[real, :, side : side + cols]
+        centre[1, layer] = frame[imaginary, :, side : side + cols]
+
+
+def finish_kernel(centre, with_even, with_odd, out):
+    rows, cols = centre.shape[2], centre.shape[3]
+    side = with_even.shape[2]
+    half = side // 2
+    inner = lax.broadcasted_iota(jnp.int32, (rows, side), 1) < half
+    zero = jnp.zeros((rows, side), jnp.float32)
+    for layer in range(2):
+        left = jnp.where(even_col(), with_odd[layer], with_even[layer])
+        right = jnp.where(even_col(), with_even[layer], with_odd[layer])
         for part in range(2):
-            plane = 2 * part + layer
-            total = placed(own_strip[pl.ds(plane * rows, rows), :], own_col)
-            total = total + placed(from_core[pl.ds(base + plane * rows, rows), :], core_col)
-            total = total + placed(from_beyond[pl.ds(plane * rows, rows), :], beyond_col)
-            centre[part, layer] = total[:, half : half + cols]
-            mine = pl.ds(part * half, half)
-            to_left[layer, :, mine] = total[:, :half]
-            to_right[layer, :, mine] = total[:, wide - half :]
-
-
-def finish_kernel(centre, from_left, from_right, out):
-    half = centre.shape[2]
-    cols = centre.shape[3]
-    for layer in range(2):
-        for part in range(2):
-            mine = pl.ds(part * half, half)
+            if part:
+                left, right = pltpu.roll(left, half, 1), pltpu.roll(right, half, 1)
             value = centre[part, layer]
-            out[part, layer] = value
-            out[part, layer, :, 0:half] = value[:, :half] + from_left[layer, :, mine]
-            out[part, layer, :, cols - half : cols] = value[:, cols - half :] + from_right[layer, :, mine]
+            out[part, layer, :, 0:side] = value[:, :side] + jnp.where(inner, left, zero)
+            out[part, layer, :, cols - side :] = value[:, cols - side :] + jnp.where(inner, zero, right)
 
 
 def call(kernel, out_shape, n_scalars, n_in, scratch=(), cost=None):
@@ -304,8 +322,8 @@
     )
 
 
-def chain(n, step):
-    return [(i, i + step) for i in range(n) if 0 <= i + step < n]
+def both_ways(pairs):
+    return pairs + [(j, i) for i, j in pairs]
 
 
 def body(obj_field, probe, scan_pos, live_count, patterns):
@@ -319,8 +337,9 @@
     scan = scan_pos.reshape(2)
     live = live_count.reshape(1)
     swap = [(0, 1), (1, 0)]
-    pairs = [(i, i + 1) for i in range(1, n_row - 1, 2)]
-    pairs = pairs + [(j, i) for i, j in pairs]
+    pairs = both_ways([(i, i + 1) for i in range(1, n_row - 1, 2)])
+    even_pairs = both_ways([(i, i + 1) for i in range(0, n_col - 1, 2)])
+    odd_pairs = both_ways([(i, i + 1) for i in range(1, n_col - 1, 2)])
     strip = 4 * rows
 
     def shape(*dims):
@@ -328,22 +347,18 @@
 
     scan_beyond = lax.ppermute(scan, ROW, pairs)
     edge = shape(2, rows, side)
-    to_left, to_right = call(edges_kernel, [edge, edge], 0, 1)(obj_field)
-    from_left = lax.ppermute(to_right, COL, chain(n_col, 1))
-    from_right = lax.ppermute(to_left, COL, chain(n_col, -1))
-    to_beyond = call(beyond_kernel, shape(strip, side), 1, 3)(
-        scan_beyond, obj_field, from_left, from_right
-    )
+    to_even, to_odd = call(edges_kernel, [edge, edge], 0, 1)(obj_field)
+    with_even = lax.ppermute(to_even, COL, even_pairs)
+    with_odd = lax.ppermute(to_odd, COL, odd_pairs)
+    to_beyond, frame = call(
+        beyond_kernel, [shape(strip, side), shape(4, rows, cols + 2 * side)], 1, 3
+    )(scan_beyond, obj_field, with_even, with_odd)
+    other = lax.ppermute(frame, "core", swap)
     beyond = lax.ppermute(to_beyond, ROW, pairs)
-    to_beyond_first, own_edge = lax.optimization_barrier((to_beyond, from_left))
+    tabs = jnp.asarray(tables(side))
     small = pl.CostEstimate(flops=1000, bytes_accessed=1000, transcendentals=0)
-    to_core = call(core_kernel, shape(strip, 2 * half + cols), 0, 3, cost=small)(
-        obj_field, own_edge, from_right
-    )
-    other = lax.ppermute(to_core, "core", swap)
-    tabs = jnp.asarray(tables(side))
-    near = call(near_kernel, shape(4, 2 * rows, side), 1, 7, cost=small)(
-        scan, obj_field, from_left, from_right, other, probe, patterns, tabs
+    near = call(near_kernel, shape(4, 2 * rows, side), 1, 5, cost=small)(
+        scan, frame, other, probe, patterns, tabs
     )
     near, beyond = lax.optimization_barrier((near, beyond))
     tall = pltpu.VMEM((4, 2 * half + rows, side), f32)
@@ -370,23 +385,28 @@
     summed = keep + from_core[:total]
     spread = lax.all_to_all(summed.reshape(n_yx, chunk, side), ("y", "x"), 0, 0)
 
-    centre, grad_left, grad_right = call(
-        merge_kernel, [shape(2, 2, rows, cols), edge, edge], 1, 3
+    centre, grad_even, grad_odd = call(
+        merge_kernel,
+        [shape(2, 2, rows, cols), edge, edge],
+        1,
+        3,
+        [pltpu.VMEM((4, rows, cols + 2 * side), f32)],
     )(scan, own_strip, from_core, from_beyond)
     part = jnp.sum(spread, axis=0)
     part = lax.all_to_all(jnp.broadcast_to(part, (n_z, chunk, side)), ("zh", "zl"), 0, 0)
     part = jnp.sum(part, axis=0)
-    got_left = lax.ppermute(grad_right, COL, chain(n_col, 1))
-    part, got_left, grad_left = lax.optimization_barrier((part, got_left, grad_left))
-    got_right = lax.ppermute(grad_left, COL, chain(n_col, -1))
-    whole = lax.all_to_all(jnp.broadcast_to(part, (n_yx, chunk, side)), ("y", "x"), 0, 0)
-    whole, got_right = lax.optimization_barrier((whole, got_right))
+    got_even = lax.ppermute(grad_even, COL, even_pairs)
+    part = jnp.broadcast_to(part, (n_yx, chunk, side))
+    part, got_even, grad_odd = lax.optimization_barrier((part, got_even, grad_odd))
+    got_odd = lax.ppermute(grad_odd, COL, odd_pairs)
+    whole = lax.all_to_all(part, ("y", "x"), 0, 0)
+    whole, got_odd = lax.optimization_barrier((whole, got_odd))
     whole = whole.reshape(modes, side, side)
     facing = lax.ppermute(whole, "core", swap)
     first = core == 0
     probe_grad = jnp.stack([jnp.where(first, whole, facing), jnp.where(first, facing, whole)])
 
-    obj_grad = call(finish_kernel, shape(2, 2, rows, cols), 0, 3)(centre, got_left, got_right)
+    obj_grad = call(finish_kernel, shape(2, 2, rows, cols), 0, 3)(centre, got_even, got_odd)
     return (obj_grad, probe_grad)
 
 

time: 111 us -> 110 us (level)
  starting transfers between devices: 75.3 us -> 73.3 us
    all_to_all x1, waiting for transfers between devices: 5.39 us -> 9.8 us  [body(): whole = lax.all_to_all(part, ('y', 'x'), 0, 0)]
    ppermute x5, waiting for transfers between devices: 3.72 us -> 0.01 us  [the longest x1 0.01 us: body(): with_odd = lax.ppermute(to_odd, COL, odd_pairs)]
    all_to_all x1, starting transfers between devices: 6.33 us -> 4.6 us  [body(): whole = lax.all_to_all(part, ('y', 'x'), 0, 0)]
    ppermute x5, starting transfers between devices: 12.7 us -> 11.4 us  [the longest x1 4.83 us: body(): with_even = lax.ppermute(to_even, COL, even_pairs)]
    pallas_call x5 -> x4, Pallas kernels: 3.31 us -> 2.58 us  [the longest x1 0.95 us: body(): call(merge_kernel, [shape(2, 2, rows, cols), edge, edge], 1, 3, [pltpu.VM...]
  transfers between devices with their start and end apart: 13 -> 13, of which waited for: 8 -> 7; matrix products, arithmetic and copies ran while one was open for 1% -> 1% of each run, Pallas kernels for 3% -> 2%
where the time goes in v3:
time: 110 us; the launch traced here: 109 us
  starting transfers between devices  73.3 us (67%)
  waiting for transfers between devices  21 us (19%)
  Pallas kernels  8.08 us (7%)
  local copies, waits for them, and re-layouts  3.4 us (3%)
  other arithmetic  1.67 us (2%)
  between operations  1.52 us (1%)
    all_to_all x1, starting transfers between devices, body(): spread = lax.all_to_all(summed.reshape(n_yx, chunk, side), ('y', 'x'), 0, 0)  17.6 us
    ppermute x1, starting transfers between devices, body(): scan_beyond = lax.ppermute(scan, ROW, pairs)  10.7 us
    all_to_all x1, waiting for transfers between devices, body(): whole = lax.all_to_all(part, ('y', 'x'), 0, 0)  9.8 us
    ppermute x1, starting transfers between devices, body(): beyond = lax.ppermute(to_beyond, ROW, pairs)  7.99 us
    ppermute x1, starting transfers between devices, body(): from_beyond = lax.ppermute(message_beyond, ROW, pairs)  6.79 us
    ppermute x1, starting transfers between devices, body(): facing = lax.ppermute(whole, 'core', swap)  6.64 us
    all_to_all x1, starting transfers between devices, body(): lax.all_to_all(jnp.broadcast_to(part, (n_z, chunk, side)), ('zh', 'zl'),...  5.61 us
    ppermute x1, starting transfers between devices, body(): with_even = lax.ppermute(to_even, COL, even_pairs)  4.83 us
  transfers between devices with their start and end apart: 13, of which 7 were waited for; matrix products, arithmetic and copies ran while one was open for 1% of the time, Pallas kernels for 2%

profile of v3, /device:TPU:1, one launch (start us, length us, event | category | flops | bytes accessed | tf_op | source)
XLA Modules:
  0.0 109.0 jit_solution(12566648016398758868)
XLA Ops:
  0.6 1.0 copy-done.3
  1.8 4.8 %collective-permute-start.1 = (f32[2,64,128]{2,1,0:T(8,128)S(1)}, f32[2,64,128]{2,1,0:T(8,128)S(1)}, u32[]{:S(2)}, u32[]{:S(2)}) collective-permute-start(f32[2,64,128]{2,1,0:T(8,128)S(1)} %get-tuple-element.20), channel_id=1, source_target_pairs={{0,1},{2,3},{4,5},{6,7},{8,9},{10,11},{12,13},{14,15},{1,0},{3,2},... | collective-permute-start | bytes 196616 | tf_op jit(solution)/shard_map/ppermute | solution.py:351
  7.3 10.7 %collective-permute-start = (s32[2]{0:T(128)}, s32[2]{0:T(128)S(1)}, u32[]{:S(2)}, u32[]{:S(2)}) collective-permute-start(s32[2]{0:T(128)} %bitcast.12), channel_id=1, source_target_pairs={{16,32},{48,64},{80,96},{112,128},{144,160},{176,192},{208,224},{2... | collective-permute-start | bytes 32 | tf_op jit(solution)/shard_map/ppermute | solution.py:348
  18.0 1.3 %collective-permute-done.scan_beyond = s32[2]{0:T(128)S(1)} collective-permute-done((s32[2]{0:T(128)}, s32[2]{0:T(128)S(1)}, u32[]{:S(2)}, u32[]{:S(2)}) %collective-permute-start) | collective-permute-done | bytes 40 | tf_op jit(solution)/shard_map/ppermute | solution.py:348
  19.3 0.8 shard_map.78
  20.1 1.9 %collective-permute-start.3 = (f32[4,64,512]{2,1,0:T(8,128)S(1)}, f32[4,64,512]{2,1,0:T(8,128)S(1)}, u32[]{:S(2)}, u32[]{:S(2)}) collective-permute-start(f32[4,64,512]{2,1,0:T(8,128)S(1)} %get-tuple-element.22.frame), channel_id=1, source_target_pairs={{0,16},{16,0},{1,17},{17,1},{2,18},{18,2},{3,19},{19,3},{4,20},{20... | collective-permute-start | bytes 1572872 | tf_op jit(solution)/shard_map/ppermute | solution.py:356
  22.1 8.0 %collective-permute-start.4 = (f32[256,128]{1,0:T(8,128)S(1)}, f32[256,128]{1,0:T(8,128)S(1)}, u32[]{:S(2)}, u32[]{:S(2)}) collective-permute-start(f32[256,128]{1,0:T(8,128)S(1)} %get-tuple-element.23), channel_id=1, source_target_pairs={{16,32},{48,64},{80,96},{112,128},{144,160},{176,192},{208,224},{2... | collective-permute-start | bytes 393224 | tf_op jit(solution)/shard_map/ppermute | solution.py:357
  30.8 1.0 copy-done.1
  31.8 0.8 shard_map.79.near
  32.8 4.7 %shard_map.80 = (f32[512,128]{1,0:T(8,128)S(1)}, f32[776,128]{1,0:T(8,128)S(1)}, f32[264,128]{1,0:T(8,128)S(1)}, f32[256,128]{1,0:T(8,128)S(1)}) custom-call(s32[2]{0:T(128)S(1)} %bitcast.14, s32[1]{0:T(128)} %bitcast.11.live, f32[4,128,128]{2,1,0:T(8,128)S(1)} %shard_map.79.near, f32[256,128]{1,0:T(8,128)S(1)} %collective-permute-done.4.beyond, ...), custom_call_target="tpu_custom_call" | custom-call | tf_op jit(solution)/shard_map/pallas_call | solution.py:365
  37.4 1.9 %collective-permute-start.5 = (f32[776,128]{1,0:T(8,128)S(1)}, f32[776,128]{1,0:T(8,128)S(1)}, u32[]{:S(2)}, u32[]{:S(2)}) collective-permute-start(f32[776,128]{1,0:T(8,128)S(1)} %get-tuple-element.27), channel_id=1, source_target_pairs={{0,16},{16,0},{1,17},{17,1},{2,18},{18,2},{3,19},{19,3},{4,20},{20... | collective-permute-start | bytes 1191944 | tf_op jit(solution)/shard_map/ppermute | solution.py:378
  39.4 1.7 %collective-permute-done.5.from_core = f32[776,128]{1,0:T(8,128)S(1)} collective-permute-done((f32[776,128]{1,0:T(8,128)S(1)}, f32[776,128]{1,0:T(8,128)S(1)}, u32[]{:S(2)}, u32[]{:S(2)}) %collective-permute-start.5) | collective-permute-done | bytes 397344 | tf_op jit(solution)/shard_map/ppermute | solution.py:378
  41.8 17.6 %all-to-all-start = ((f32[32,16,128]{2,1,0:T(8,128)}), f32[32,16,128]{2,1,0:T(8,128)S(1)}, u32[]{:S(2)}, u32[]{:S(2)}) async-start(f32[32,16,128]{2,1,0:T(8,128)} %bitcast.2), calls=%async_computation | async-start | bytes 524288 | tf_op jit(solution)/shard_map/all_to_all | solution.py:386
  59.4 6.8 %collective-permute-start.6 = (f32[264,128]{1,0:T(8,128)S(1)}, f32[264,128]{1,0:T(8,128)S(1)}, u32[]{:S(2)}, u32[]{:S(2)}) collective-permute-start(f32[264,128]{1,0:T(8,128)S(1)} %get-tuple-element.28), channel_id=1, source_target_pairs={{16,32},{48,64},{80,96},{112,128},{144,160},{176,192},{208,224},{2... | collective-permute-start | bytes 405512 | tf_op jit(solution)/shard_map/ppermute | solution.py:379
  66.2 4.8 %all-to-all-done = f32[32,16,128]{2,1,0:T(8,128)S(1)} async-done(((f32[32,16,128]{2,1,0:T(8,128)}), f32[32,16,128]{2,1,0:T(8,128)S(1)}, u32[]{:S(2)}, u32[]{:S(2)}) %all-to-all-start) | async-done | bytes 262176 | tf_op jit(solution)/shard_map/all_to_all | solution.py:386
  71.6 5.6 %all-to-all-start.1 = ((f32[8,16,128]{2,1,0:T(8,128)}), f32[8,16,128]{2,1,0:T(8,128)S(1)}, u32[]{:S(2)}, u32[]{:S(2)}) async-start(f32[8,16,128]{2,1,0:T(8,128)} %broadcast_in_dim.6), calls=%async_computation.1 | async-start | bytes 131072 | tf_op jit(solution)/shard_map/all_to_all | solution.py:396
  77.3 0.9 shard_map.81
  78.2 3.4 %collective-permute-start.7 = (f32[2,64,128]{2,1,0:T(8,128)S(1)}, f32[2,64,128]{2,1,0:T(8,128)S(1)}, u32[]{:S(2)}, u32[]{:S(2)}) collective-permute-start(f32[2,64,128]{2,1,0:T(8,128)S(1)} %get-tuple-element.31), channel_id=1, source_target_pairs={{0,1},{2,3},{4,5},{6,7},{8,9},{10,11},{12,13},{14,15},{1,0},{3,2},... | collective-permute-start | bytes 196616 | tf_op jit(solution)/shard_map/ppermute | solution.py:398
  81.6 2.9 %all-to-all-done.1 = f32[8,16,128]{2,1,0:T(8,128)S(1)} async-done(((f32[8,16,128]{2,1,0:T(8,128)}), f32[8,16,128]{2,1,0:T(8,128)S(1)}, u32[]{:S(2)}, u32[]{:S(2)}) %all-to-all-start.1) | async-done | bytes 65568 | tf_op jit(solution)/shard_map/all_to_all | solution.py:396
  85.2 4.6 %all-to-all-start.2 = ((f32[32,16,128]{2,1,0:T(8,128)}), f32[32,16,128]{2,1,0:T(8,128)S(1)}, u32[]{:S(2)}, u32[]{:S(2)}) async-start(f32[32,16,128]{2,1,0:T(8,128)} %broadcast_in_dim.7), calls=%async_computation.2 | async-start | bytes 524288 | tf_op jit(solution)/shard_map/all_to_all | solution.py:402
  90.5 9.8 %all-to-all-done.2 = f32[32,16,128]{2,1,0:T(8,128)S(1)} async-done(((f32[32,16,128]{2,1,0:T(8,128)}), f32[32,16,128]{2,1,0:T(8,128)S(1)}, u32[]{:S(2)}, u32[]{:S(2)}) %all-to-all-start.2) | async-done | bytes 262176 | tf_op jit(solution)/shard_map/all_to_all | solution.py:402
  100.3 6.6 %collective-permute-start.9 = (f32[4,128,128]{2,1,0:T(8,128)S(1)}, f32[4,128,128]{2,1,0:T(8,128)S(1)}, u32[]{:S(2)}, u32[]{:S(2)}) collective-permute-start(f32[4,128,128]{2,1,0:T(8,128)S(1)} %bitcast.16), channel_id=1, source_target_pairs={{0,16},{16,0},{1,17},{17,1},{2,18},{18,2},{3,19},{19,3},{4,20},{20... | collective-permute-start | bytes 786440 | tf_op jit(solution)/shard_map/ppermute | solution.py:405
  107.0 0.8 shard_map.82
  108.2 0.8 pad_maximum_fusion
  (27 shorter events, 4.2 us)
Async XLA Ops:
  0.6 30.1 %copy-start = (f32[2,4,128,128]{3,2,1,0:T(8,128)S(1)}, f32[2,4,128,128]{3,2,1,0:T(8,128)}, u32[]{:S(2)}) copy-start(f32[2,4,128,128]{3,2,1,0:T(8,128)} %probe.3) | copy-start | bytes 1572868
  0.6 1.0 copy-start.3
  1.8 17.6 %collective-permute-start.1 = (f32[2,64,128]{2,1,0:T(8,128)S(1)}, f32[2,64,128]{2,1,0:T(8,128)S(1)}, u32[]{:S(2)}, u32[]{:S(2)}) collective-permute-start(f32[2,64,128]{2,1,0:T(8,128)S(1)} %get-tuple-element.20), channel_id=1, source_target_pairs={{0,1},{2,3},{4,5},{6,7},{8,9},{10,11},{12,13},{14,15},{1,0},{3,2},... | collective-permute-start | bytes 196616 | tf_op jit(solution)/shard_map/ppermute | solution.py:351
  6.6 12.8 %collective-permute-start.2 = (f32[2,64,128]{2,1,0:T(8,128)S(1)}, f32[2,64,128]{2,1,0:T(8,128)S(1)}, u32[]{:S(2)}, u32[]{:S(2)}) collective-permute-start(f32[2,64,128]{2,1,0:T(8,128)S(1)} %get-tuple-element.21), channel_id=1, source_target_pairs={{1,2},{3,4},{5,6},{7,8},{9,10},{11,12},{13,14},{2,1},{4,3},{6,5},{... | collective-permute-start | bytes 196616 | tf_op jit(solution)/shard_map/ppermute | solution.py:352
  7.3 23.5 %copy-start.4 = (f32[1,1,1,128,128]{4,3,2,1,0:T(8,128)S(1)}, f32[1,1,1,128,128]{4,3,2,1,0:T(8,128)}, u32[]{:S(2)}) copy-start(f32[1,1,1,128,128]{4,3,2,1,0:T(8,128)} %pattern.3) | copy-start | bytes 196612
  7.3 12.1 %collective-permute-start = (s32[2]{0:T(128)}, s32[2]{0:T(128)S(1)}, u32[]{:S(2)}, u32[]{:S(2)}) collective-permute-start(s32[2]{0:T(128)} %bitcast.12), channel_id=1, source_target_pairs={{16,32},{48,64},{80,96},{112,128},{144,160},{176,192},{208,224},{2... | collective-permute-start | bytes 32 | tf_op jit(solution)/shard_map/ppermute | solution.py:348
  20.1 10.6 %collective-permute-start.3 = (f32[4,64,512]{2,1,0:T(8,128)S(1)}, f32[4,64,512]{2,1,0:T(8,128)S(1)}, u32[]{:S(2)}, u32[]{:S(2)}) collective-permute-start(f32[4,64,512]{2,1,0:T(8,128)S(1)} %get-tuple-element.22.frame), channel_id=1, source_target_pairs={{0,16},{16,0},{1,17},{17,1},{2,18},{18,2},{3,19},{19,3},{4,20},{20... | collective-permute-start | bytes 1572872 | tf_op jit(solution)/shard_map/ppermute | solution.py:356
  22.1 8.7 %copy-start.5 = (s32[1,1,1,2]{3,2,1,0:T(1,128)S(1)}, s32[1,1,1,2]{3,2,1,0:T(1,128)}, u32[]{:S(2)}) copy-start(s32[1,1,1,2]{3,2,1,0:T(1,128)} %param.8) | copy-start | bytes 28
  22.1 10.6 %collective-permute-start.4 = (f32[256,128]{1,0:T(8,128)S(1)}, f32[256,128]{1,0:T(8,128)S(1)}, u32[]{:S(2)}, u32[]{:S(2)}) collective-permute-start(f32[256,128]{1,0:T(8,128)S(1)} %get-tuple-element.23), channel_id=1, source_target_pairs={{16,32},{48,64},{80,96},{112,128},{144,160},{176,192},{208,224},{2... | collective-permute-start | bytes 393224 | tf_op jit(solution)/shard_map/ppermute | solution.py:357
  30.8 1.0 copy-start.1
  31.8 1.0 copy-start.2
  37.4 3.6 %collective-permute-start.5 = (f32[776,128]{1,0:T(8,128)S(1)}, f32[776,128]{1,0:T(8,128)S(1)}, u32[]{:S(2)}, u32[]{:S(2)}) collective-permute-start(f32[776,128]{1,0:T(8,128)S(1)} %get-tuple-element.27), channel_id=1, source_target_pairs={{0,16},{16,0},{1,17},{17,1},{2,18},{18,2},{3,19},{19,3},{4,20},{20... | collective-permute-start | bytes 1191944 | tf_op jit(solution)/shard_map/ppermute | solution.py:378
  41.8 29.2 %all-to-all-start = ((f32[32,16,128]{2,1,0:T(8,128)}), f32[32,16,128]{2,1,0:T(8,128)S(1)}, u32[]{:S(2)}, u32[]{:S(2)}) async-start(f32[32,16,128]{2,1,0:T(8,128)} %bitcast.2), calls=%async_computation | async-start | bytes 524288 | tf_op jit(solution)/shard_map/all_to_all | solution.py:386
  59.4 17.9 %collective-permute-start.6 = (f32[264,128]{1,0:T(8,128)S(1)}, f32[264,128]{1,0:T(8,128)S(1)}, u32[]{:S(2)}, u32[]{:S(2)}) collective-permute-start(f32[264,128]{1,0:T(8,128)S(1)} %get-tuple-element.28), channel_id=1, source_target_pairs={{16,32},{48,64},{80,96},{112,128},{144,160},{176,192},{208,224},{2... | collective-permute-start | bytes 405512 | tf_op jit(solution)/shard_map/ppermute | solution.py:379
  71.6 12.8 %all-to-all-start.1 = ((f32[8,16,128]{2,1,0:T(8,128)}), f32[8,16,128]{2,1,0:T(8,128)S(1)}, u32[]{:S(2)}, u32[]{:S(2)}) async-start(f32[8,16,128]{2,1,0:T(8,128)} %broadcast_in_dim.6), calls=%async_computation.1 | async-start | bytes 131072 | tf_op jit(solution)/shard_map/all_to_all | solution.py:396
  78.2 6.3 %collective-permute-start.7 = (f32[2,64,128]{2,1,0:T(8,128)S(1)}, f32[2,64,128]{2,1,0:T(8,128)S(1)}, u32[]{:S(2)}, u32[]{:S(2)}) collective-permute-start(f32[2,64,128]{2,1,0:T(8,128)S(1)} %get-tuple-element.31), channel_id=1, source_target_pairs={{0,1},{2,3},{4,5},{6,7},{8,9},{10,11},{12,13},{14,15},{1,0},{3,2},... | collective-permute-start | bytes 196616 | tf_op jit(solution)/shard_map/ppermute | solution.py:398
  85.2 15.1 %all-to-all-start.2 = ((f32[32,16,128]{2,1,0:T(8,128)}), f32[32,16,128]{2,1,0:T(8,128)S(1)}, u32[]{:S(2)}, u32[]{:S(2)}) async-start(f32[32,16,128]{2,1,0:T(8,128)} %broadcast_in_dim.7), calls=%async_computation.2 | async-start | bytes 524288 | tf_op jit(solution)/shard_map/all_to_all | solution.py:402
  89.8 0.7 collective-permute-start.8
  100.3 7.8 %collective-permute-start.9 = (f32[4,128,128]{2,1,0:T(8,128)S(1)}, f32[4,128,128]{2,1,0:T(8,128)S(1)}, u32[]{:S(2)}, u32[]{:S(2)}) collective-permute-start(f32[4,128,128]{2,1,0:T(8,128)S(1)} %bitcast.16), channel_id=1, source_target_pairs={{0,16},{16,0},{1,17},{17,1},{2,18},{18,2},{3,19},{19,3},{4,20},{20... | collective-permute-start | bytes 786440 | tf_op jit(solution)/shard_map/ppermute | solution.py:405

commit v4 on v3

--- a/solution.py
+++ b/solution.py
@@ -148,77 +148,85 @@
     return lax.rem(lax.axis_index(COL), 2) == 0
 
 
-def fill(frame, own, with_even, with_odd, part, layer):
-    side = with_even.shape[2]
-    half = side // 2
-    cols = own.shape[3]
-    plane = 2 * part + layer
-    left = jnp.where(even_col(), with_odd[layer], with_even[layer])
-    right = jnp.where(even_col(), with_even[layer], with_odd[layer])
-    if part:
-        left, right = pltpu.roll(left, half, 1), pltpu.roll(right, half, 1)
-    frame[plane, :, 0:side] = left
-    frame[plane, :, side : side + cols] = own[part, layer]
-    frame[plane, :, side + cols :] = right
-
-
-def cut(frame, plane, at, side):
-    step = lax.rem(at, side)
-    wide = frame[plane, :, pl.ds(pl.multiple_of(at - step, side), 2 * side)]
-    return pltpu.roll(wide, lax.rem(2 * side - step, 2 * side), 1)[:, :side]
-
-
-def edges_kernel(own, with_even, with_odd):
-    rows, cols = own.shape[2], own.shape[3]
+def pack(source, with_even, with_odd, at):
+    rows, cols = source.shape[2], source.shape[3]
     side = with_even.shape[2]
     half = side // 2
     inner = lax.broadcasted_iota(jnp.int32, (rows, side), 1) < half
     for layer in range(2):
-        real, imaginary = own[0, layer], own[1, layer]
+        real, imaginary = source[0, layer], source[1, layer]
         left = jnp.where(inner, real[:, :side], pltpu.roll(imaginary[:, :side], half, 1))
         right = jnp.where(inner, pltpu.roll(imaginary[:, cols - side :], half, 1), real[:, cols - side :])
-        with_even[layer] = jnp.where(even_col(), right, left)
-        with_odd[layer] = jnp.where(even_col(), left, right)
-
-
-def beyond_kernel(scan_beyond, own, with_even, with_odd, to_beyond, frame):
+        with_even[layer, at, :] = jnp.where(even_col(), right, left)
+        with_odd[layer, at, :] = jnp.where(even_col(), left, right)
+
+
+def pack_near_kernel(own, other, with_even, with_odd):
+    rows = own.shape[2]
+    pack(own, with_even, with_odd, pl.ds(0, rows))
+    pack(other, with_even, with_odd, pl.ds(rows, rows))
+
+
+def pack_kernel(beyond, near_even, near_odd, with_even, with_odd):
+    rows = beyond.shape[2]
+    other_at, beyond_at = strips_at(rows)
+    pack(beyond, with_even, with_odd, pl.ds(beyond_at, rows))
+    for packed, out in ((near_even, with_even), (near_odd, with_odd)):
+        for layer in range(2):
+            out[layer, rows : 2 * rows, :] = packed[layer, 0:rows, :]
+            out[layer, pl.ds(other_at, rows), :] = packed[layer, rows : 2 * rows, :]
+
+
+def tile_and_step(col, side):
+    at = col + side // 2
+    step = lax.rem(at, side)
+    return (at - step) // side, step
+
+
+def near_kernel(scan, own, other, beyond, after, probe, pattern, tabs, near):
     rows, cols = own.shape[2], own.shape[3]
-    side = to_beyond.shape[1]
-    half = side // 2
-    unused, col = place_of(scan_beyond, rows, cols, half)
-    col = jnp.clip(col, 0, cols - 1)
-    for layer in range(2):
-        for part in range(2):
-            plane = 2 * part + layer
-            fill(frame, own, with_even, with_odd, part, layer)
-            to_beyond[pl.ds(plane * rows, rows), :] = cut(frame, plane, col + half, side)
-
-
-def near_kernel(scan, frame, other, probe, pattern, tabs, near):
-    rows, cols = frame.shape[1], frame.shape[2] - 2 * near.shape[2]
     side = near.shape[2]
     half = side // 2
     unused, col = place_of(scan, rows, cols, half)
-    for plane in range(4):
-        near[plane, 0:rows, :] = cut(frame, plane, col + half, side)
-        near[plane, rows : 2 * rows, :] = cut(other, plane, col + half, side)
+    tile, step = tile_and_step(col, side)
+    other_at, beyond_at = strips_at(half)
+    lane = lax.broadcasted_iota(jnp.int32, (rows, side), 1)
+    back = lax.rem(side - step, side)
+    zero = jnp.zeros((rows, side), jnp.float32)
+    for source, first in ((own, half), (other, other_at), (beyond, beyond_at)):
+        for layer in range(2):
+            for part in range(2):
+                a, b = source[part, layer, :, 0:side], source[part, layer, :, side:]
+                early = jnp.where(tile == 0, zero, jnp.where(tile == 1, a, b))
+                late = jnp.where(tile == 0, a, jnp.where(tile == 1, b, zero))
+                near[2 * part + layer, pl.ds(first, rows), :] = jnp.where(
+                    lane < side - step, pltpu.roll(early, back, 1), pltpu.roll(late, back, 1)
+                )
 
 
 def main_kernel(
-    scan, live, near, beyond, probe, pattern, tabs,
+    scan, live, near, with_even, with_odd, probe, pattern, tabs,
     keep, message_core, message_beyond, own_strip, column, shifted,
 ):
     side = probe.shape[-1]
     half = side // 2
-    rows = beyond.shape[0] // 4
+    rows = own_strip.shape[0] // 4
     cols = TILE_COLS
     modes = probe.shape[1]
     row, col = place_of(scan, rows, cols, half)
     other_at, beyond_at = strips_at(half)
-    for plane in range(4):
-        column[plane, half : half + rows, :] = near[plane, 0:rows, :]
-        column[plane, pl.ds(other_at, rows), :] = near[plane, rows : 2 * rows, :]
-        column[plane, pl.ds(beyond_at, rows), :] = beyond[pl.ds(plane * rows, rows), :]
+    tile, tile_step = tile_and_step(col, side)
+    use_even = (tile == 0) != even_col()
+    lane = lax.broadcasted_iota(jnp.int32, column.shape[1:], 1)
+    from_left = jnp.logical_and(tile == 0, lane < side - tile_step)
+    from_right = jnp.logical_and(tile == 2, lane >= side - tile_step)
+    margin_lanes = jnp.logical_or(from_left, from_right)
+    for layer in range(2):
+        margin = jnp.where(use_even, with_even[layer], with_odd[layer])
+        for part in range(2):
+            plane = 2 * part + layer
+            moved = pltpu.roll(margin, lax.rem(side - tile_step + part * half, side), 1)
+            column[plane] = jnp.where(margin_lanes, moved, near[plane])
     tall = side + 8
     step = lax.rem(row, 8)
     base_row = pl.multiple_of(row - step, 8)
@@ -345,22 +353,19 @@
     def shape(*dims):
         return jax.ShapeDtypeStruct(dims, f32)
 
-    scan_beyond = lax.ppermute(scan, ROW, pairs)
+    beyond = lax.ppermute(obj_field, ROW, pairs)
+    other = lax.ppermute(obj_field, "core", swap)
     edge = shape(2, rows, side)
-    to_even, to_odd = call(edges_kernel, [edge, edge], 0, 1)(obj_field)
+    tall_edge = shape(2, 2 * half + rows, side)
+    near_edge = shape(2, 2 * rows, side)
+    near_even, near_odd = call(pack_near_kernel, [near_edge, near_edge], 0, 2)(obj_field, other)
+    to_even, to_odd = call(pack_kernel, [tall_edge, tall_edge], 0, 3)(beyond, near_even, near_odd)
     with_even = lax.ppermute(to_even, COL, even_pairs)
     with_odd = lax.ppermute(to_odd, COL, odd_pairs)
-    to_beyond, frame = call(
-        beyond_kernel, [shape(strip, side), shape(4, rows, cols + 2 * side)], 1, 3
-    )(scan_beyond, obj_field, with_even, with_odd)
-    other = lax.ppermute(frame, "core", swap)
-    beyond = lax.ppermute(to_beyond, ROW, pairs)
     tabs = jnp.asarray(tables(side))
-    small = pl.CostEstimate(flops=1000, bytes_accessed=1000, transcendentals=0)
-    near = call(near_kernel, shape(4, 2 * rows, side), 1, 5, cost=small)(
-        scan, frame, other, probe, patterns, tabs
-    )
-    near, beyond = lax.optimization_barrier((near, beyond))
+    near = call(near_kernel, shape(4, 2 * half + rows, side), 1, 7)(
+        scan, obj_field, other, beyond, to_even, probe, patterns, tabs
+    )
     tall = pltpu.VMEM((4, 2 * half + rows, side), f32)
     keep, message_core, message_beyond, own_strip = call(
         main_kernel,
@@ -371,9 +376,9 @@
             shape(strip, side),
         ],
         2,
-        5,
+        6,
         [tall, tall],
-    )(scan, live, near, beyond, probe, patterns, tabs)
+    )(scan, live, near, with_even, with_odd, probe, patterns, tabs)
 
     from_core = lax.ppermute(message_core, "core", swap)
     from_beyond = lax.ppermute(message_beyond, ROW, pairs)

time: 110 us -> 113 us (1.027)
  waiting for transfers between devices: 21 us -> 26.5 us
  starting transfers between devices: 73.3 us -> 70.7 us
    ppermute x3 -> x2, waiting for transfers between devices: 1.54 us -> 10.4 us  [the longest x1 10.4 us: body(): beyond = lax.ppermute(obj_field, ROW, pairs)]
    ppermute x3 -> x2, starting transfers between devices: 20.6 us -> 14.1 us  [the longest x1 8.92 us: body(): other = lax.ppermute(obj_field, 'core', swap)]
    all_to_all x1, starting transfers between devices: 17.6 us -> 11.5 us  [body(): spread = lax.all_to_all(summed.reshape(n_yx, chunk, side), ('y', 'x'), 0, 0)]
    ppermute x1, starting transfers between devices: 6.79 us -> 10.4 us  [body(): from_beyond = lax.ppermute(message_beyond, ROW, pairs)]
    all_to_all x1, waiting for transfers between devices: 4.79 us -> 1.43 us  [body(): spread = lax.all_to_all(summed.reshape(n_yx, chunk, side), ('y', 'x'), 0, 0)]
    all_to_all x1, starting transfers between devices: 5.61 us -> 8.93 us  [body(): lax.all_to_all(jnp.broadcast_to(part, (n_z, chunk, side)), ('zh', 'zl'),...]
    ppermute x1, starting transfers between devices: 4.83 us -> 7.8 us  [body(): with_even = lax.ppermute(to_even, COL, even_pairs)]
  transfers between devices with their start and end apart: 13 -> 12, of which waited for: 7 -> 6; matrix products, arithmetic and copies ran while one was open for 1% -> 1% of each run, Pallas kernels for 2% -> 2%
where the time goes in v4:
time: 113 us; the launch traced here: 112 us
  starting transfers between devices  70.7 us (63%)
  waiting for transfers between devices  26.5 us (23%)
  Pallas kernels  7.65 us (7%)
  local copies, waits for them, and re-layouts  3.92 us (3%)
  other arithmetic  1.67 us (1%)
  between operations  1.52 us (1%)
    all_to_all x1, starting transfers between devices, body(): spread = lax.all_to_all(summed.reshape(n_yx, chunk, side), ('y', 'x'), 0, 0)  11.5 us
    ppermute x1, waiting for transfers between devices, body(): beyond = lax.ppermute(obj_field, ROW, pairs)  10.4 us
    ppermute x1, starting transfers between devices, body(): from_beyond = lax.ppermute(message_beyond, ROW, pairs)  10.4 us
    all_to_all x1, waiting for transfers between devices, body(): whole = lax.all_to_all(part, ('y', 'x'), 0, 0)  9.75 us
    all_to_all x1, starting transfers between devices, body(): lax.all_to_all(jnp.broadcast_to(part, (n_z, chunk, side)), ('zh', 'zl'),...  8.93 us
    ppermute x1, starting transfers between devices, body(): other = lax.ppermute(obj_field, 'core', swap)  8.92 us
    ppermute x1, starting transfers between devices, body(): with_even = lax.ppermute(to_even, COL, even_pairs)  7.8 us
    ppermute x1, starting transfers between devices, body(): facing = lax.ppermute(whole, 'core', swap)  6.84 us
  transfers between devices with their start and end apart: 12, of which 6 were waited for; matrix products, arithmetic and copies ran while one was open for 1% of the time, Pallas kernels for 2%

profile of v4, /device:TPU:1, one launch (start us, length us, event | category | flops | bytes accessed | tf_op | source)
XLA Modules:
  0.0 112.0 jit_solution(13653239726230366152)
XLA Ops:
  0.6 8.9 %collective-permute-start = (f32[2,2,64,256]{3,2,1,0:T(8,128)}, f32[2,2,64,256]{3,2,1,0:T(8,128)S(1)}, u32[]{:S(2)}, u32[]{:S(2)}) collective-permute-start(f32[2,2,64,256]{3,2,1,0:T(8,128)} %own.3), channel_id=1, source_target_pairs={{0,16},{16,0},{1,17},{17,1},{2,18},{18,2},{3,19},{19,3},{4,20},{20... | collective-permute-start | bytes 786440 | tf_op jit(solution)/shard_map/ppermute | solution.py:357
  9.6 5.2 %collective-permute-start.1 = (f32[2,2,64,256]{3,2,1,0:T(8,128)}, f32[2,2,64,256]{3,2,1,0:T(8,128)S(1)}, u32[]{:S(2)}, u32[]{:S(2)}) collective-permute-start(f32[2,2,64,256]{3,2,1,0:T(8,128)} %own.3), channel_id=1, source_target_pairs={{16,32},{48,64},{80,96},{112,128},{144,160},{176,192},{208,224},{2... | collective-permute-start | bytes 786440 | tf_op jit(solution)/shard_map/ppermute | solution.py:356
  14.8 1.0 copy-done.2
  15.9 10.4 %collective-permute-done.1.beyond = f32[2,2,64,256]{3,2,1,0:T(8,128)S(1)} collective-permute-done((f32[2,2,64,256]{3,2,1,0:T(8,128)}, f32[2,2,64,256]{3,2,1,0:T(8,128)S(1)}, u32[]{:S(2)}, u32[]{:S(2)}) %collective-permute-start.1) | collective-permute-done | bytes 262176 | tf_op jit(solution)/shard_map/ppermute | solution.py:356
  26.4 7.8 %collective-permute-start.2 = (f32[2,192,128]{2,1,0:T(8,128)S(1)}, f32[2,192,128]{2,1,0:T(8,128)S(1)}, u32[]{:S(2)}, u32[]{:S(2)}) collective-permute-start(f32[2,192,128]{2,1,0:T(8,128)S(1)} %get-tuple-element.20.after), channel_id=1, source_target_pairs={{0,1},{2,3},{4,5},{6,7},{8,9},{10,11},{12,13},{14,15},{1,0},{3,2},... | collective-permute-start | bytes 589832 | tf_op jit(solution)/shard_map/ppermute | solution.py:363
  36.2 0.9 copy-done.3
  37.2 0.8 shard_map.79.near
  38.0 4.8 %shard_map.80 = (f32[512,128]{1,0:T(8,128)S(1)}, f32[776,128]{1,0:T(8,128)S(1)}, f32[264,128]{1,0:T(8,128)S(1)}, f32[256,128]{1,0:T(8,128)S(1)}) custom-call(s32[2]{0:T(128)S(1)} %bitcast.13, s32[1]{0:T(128)} %bitcast.11.live, f32[4,192,128]{2,1,0:T(8,128)S(1)} %shard_map.79.near, f32[2,192,128]{2,1,0:T(8,128)S(1)} %collective-permute-done.2.with_even, ...), custom_call_target="tpu_custom_call" | custom-call | tf_op jit(solution)/shard_map/pallas_call | solution.py:370
  42.8 1.9 %collective-permute-start.4 = (f32[776,128]{1,0:T(8,128)S(1)}, f32[776,128]{1,0:T(8,128)S(1)}, u32[]{:S(2)}, u32[]{:S(2)}) collective-permute-start(f32[776,128]{1,0:T(8,128)S(1)} %get-tuple-element.23), channel_id=1, source_target_pairs={{0,16},{16,0},{1,17},{17,1},{2,18},{18,2},{3,19},{19,3},{4,20},{20... | collective-permute-start | bytes 1191944 | tf_op jit(solution)/shard_map/ppermute | solution.py:383
  44.8 1.7 %collective-permute-done.4.from_core = f32[776,128]{1,0:T(8,128)S(1)} collective-permute-done((f32[776,128]{1,0:T(8,128)S(1)}, f32[776,128]{1,0:T(8,128)S(1)}, u32[]{:S(2)}, u32[]{:S(2)}) %collective-permute-start.4) | collective-permute-done | bytes 397344 | tf_op jit(solution)/shard_map/ppermute | solution.py:383
  46.5 0.7 slice_add_fusion
  47.2 11.5 %all-to-all-start = ((f32[32,16,128]{2,1,0:T(8,128)}), f32[32,16,128]{2,1,0:T(8,128)S(1)}, u32[]{:S(2)}, u32[]{:S(2)}) async-start(f32[32,16,128]{2,1,0:T(8,128)} %bitcast.2), calls=%async_computation | async-start | bytes 524288 | tf_op jit(solution)/shard_map/all_to_all | solution.py:391
  58.7 10.4 %collective-permute-start.5 = (f32[264,128]{1,0:T(8,128)S(1)}, f32[264,128]{1,0:T(8,128)S(1)}, u32[]{:S(2)}, u32[]{:S(2)}) collective-permute-start(f32[264,128]{1,0:T(8,128)S(1)} %get-tuple-element.24), channel_id=1, source_target_pairs={{16,32},{48,64},{80,96},{112,128},{144,160},{176,192},{208,224},{2... | collective-permute-start | bytes 405512 | tf_op jit(solution)/shard_map/ppermute | solution.py:384
  69.1 1.4 %all-to-all-done = f32[32,16,128]{2,1,0:T(8,128)S(1)} async-done(((f32[32,16,128]{2,1,0:T(8,128)}), f32[32,16,128]{2,1,0:T(8,128)S(1)}, u32[]{:S(2)}, u32[]{:S(2)}) %all-to-all-start) | async-done | bytes 262176 | tf_op jit(solution)/shard_map/all_to_all | solution.py:391
  71.2 8.9 %all-to-all-start.1 = ((f32[8,16,128]{2,1,0:T(8,128)}), f32[8,16,128]{2,1,0:T(8,128)S(1)}, u32[]{:S(2)}, u32[]{:S(2)}) async-start(f32[8,16,128]{2,1,0:T(8,128)} %broadcast_in_dim.6), calls=%async_computation.1 | async-start | bytes 131072 | tf_op jit(solution)/shard_map/all_to_all | solution.py:401
  80.1 0.9 shard_map.81
  81.1 3.4 %collective-permute-start.6 = (f32[2,64,128]{2,1,0:T(8,128)S(1)}, f32[2,64,128]{2,1,0:T(8,128)S(1)}, u32[]{:S(2)}, u32[]{:S(2)}) collective-permute-start(f32[2,64,128]{2,1,0:T(8,128)S(1)} %get-tuple-element.27), channel_id=1, source_target_pairs={{0,1},{2,3},{4,5},{6,7},{8,9},{10,11},{12,13},{14,15},{1,0},{3,2},... | collective-permute-start | bytes 196616 | tf_op jit(solution)/shard_map/ppermute | solution.py:403
  84.5 2.9 %all-to-all-done.1 = f32[8,16,128]{2,1,0:T(8,128)S(1)} async-done(((f32[8,16,128]{2,1,0:T(8,128)}), f32[8,16,128]{2,1,0:T(8,128)S(1)}, u32[]{:S(2)}, u32[]{:S(2)}) %all-to-all-start.1) | async-done | bytes 65568 | tf_op jit(solution)/shard_map/all_to_all | solution.py:401
  87.4 0.7 broadcast_in_dim.7
  88.1 4.6 %all-to-all-start.2 = ((f32[32,16,128]{2,1,0:T(8,128)}), f32[32,16,128]{2,1,0:T(8,128)S(1)}, u32[]{:S(2)}, u32[]{:S(2)}) async-start(f32[32,16,128]{2,1,0:T(8,128)} %broadcast_in_dim.7), calls=%async_computation.2 | async-start | bytes 524288 | tf_op jit(solution)/shard_map/all_to_all | solution.py:407
  93.4 9.7 %all-to-all-done.2 = f32[32,16,128]{2,1,0:T(8,128)S(1)} async-done(((f32[32,16,128]{2,1,0:T(8,128)}), f32[32,16,128]{2,1,0:T(8,128)S(1)}, u32[]{:S(2)}, u32[]{:S(2)}) %all-to-all-start.2) | async-done | bytes 262176 | tf_op jit(solution)/shard_map/all_to_all | solution.py:407
  103.1 6.8 %collective-permute-start.8 = (f32[4,128,128]{2,1,0:T(8,128)S(1)}, f32[4,128,128]{2,1,0:T(8,128)S(1)}, u32[]{:S(2)}, u32[]{:S(2)}) collective-permute-start(f32[4,128,128]{2,1,0:T(8,128)S(1)} %bitcast.15), channel_id=1, source_target_pairs={{0,16},{16,0},{1,17},{17,1},{2,18},{18,2},{3,19},{19,3},{4,20},{20... | collective-permute-start | bytes 786440 | tf_op jit(solution)/shard_map/ppermute | solution.py:410
  110.0 0.8 shard_map.82
  111.1 0.8 pad_maximum_fusion
  (25 shorter events, 3.3 us)
Async XLA Ops:
  0.6 34.9 %copy-start = (f32[2,4,128,128]{3,2,1,0:T(8,128)S(1)}, f32[2,4,128,128]{3,2,1,0:T(8,128)}, u32[]{:S(2)}) copy-start(f32[2,4,128,128]{3,2,1,0:T(8,128)} %probe.3) | copy-start | bytes 1572868
  0.6 14.1 %collective-permute-start = (f32[2,2,64,256]{3,2,1,0:T(8,128)}, f32[2,2,64,256]{3,2,1,0:T(8,128)S(1)}, u32[]{:S(2)}, u32[]{:S(2)}) collective-permute-start(f32[2,2,64,256]{3,2,1,0:T(8,128)} %own.3), channel_id=1, source_target_pairs={{0,16},{16,0},{1,17},{17,1},{2,18},{18,2},{3,19},{19,3},{4,20},{20... | collective-permute-start | bytes 786440 | tf_op jit(solution)/shard_map/ppermute | solution.py:357
  9.6 16.7 %collective-permute-start.1 = (f32[2,2,64,256]{3,2,1,0:T(8,128)}, f32[2,2,64,256]{3,2,1,0:T(8,128)S(1)}, u32[]{:S(2)}, u32[]{:S(2)}) collective-permute-start(f32[2,2,64,256]{3,2,1,0:T(8,128)} %own.3), channel_id=1, source_target_pairs={{16,32},{48,64},{80,96},{112,128},{144,160},{176,192},{208,224},{2... | collective-permute-start | bytes 786440 | tf_op jit(solution)/shard_map/ppermute | solution.py:356
  14.7 1.0 copy-start.2
  15.9 19.7 %copy-start.1 = (bf16[12,128,128]{2,1,0:T(8,128)(2,1)S(1)}, bf16[12,128,128]{2,1,0:T(8,128)(2,1)}, u32[]{:S(2)}) copy-start(bf16[12,128,128]{2,1,0:T(8,128)(2,1)} %constant.12.clone.tabs) | copy-start | bytes 1179652
  26.3 9.3 %copy-start.4 = (f32[1,1,1,128,128]{4,3,2,1,0:T(8,128)S(1)}, f32[1,1,1,128,128]{4,3,2,1,0:T(8,128)}, u32[]{:S(2)}) copy-start(f32[1,1,1,128,128]{4,3,2,1,0:T(8,128)} %pattern.3) | copy-start | bytes 196612
  26.4 11.6 %collective-permute-start.2 = (f32[2,192,128]{2,1,0:T(8,128)S(1)}, f32[2,192,128]{2,1,0:T(8,128)S(1)}, u32[]{:S(2)}, u32[]{:S(2)}) collective-permute-start(f32[2,192,128]{2,1,0:T(8,128)S(1)} %get-tuple-element.20.after), channel_id=1, source_target_pairs={{0,1},{2,3},{4,5},{6,7},{8,9},{10,11},{12,13},{14,15},{1,0},{3,2},... | collective-permute-start | bytes 589832 | tf_op jit(solution)/shard_map/ppermute | solution.py:363
  34.2 3.8 %collective-permute-start.3 = (f32[2,192,128]{2,1,0:T(8,128)S(1)}, f32[2,192,128]{2,1,0:T(8,128)S(1)}, u32[]{:S(2)}, u32[]{:S(2)}) collective-permute-start(f32[2,192,128]{2,1,0:T(8,128)S(1)} %get-tuple-element.21), channel_id=1, source_target_pairs={{1,2},{3,4},{5,6},{7,8},{9,10},{11,12},{13,14},{2,1},{4,3},{6,5},{... | collective-permute-start | bytes 589832 | tf_op jit(solution)/shard_map/ppermute | solution.py:364
  35.5 0.7 copy-start.5
  36.2 0.9 copy-start.3
  42.8 3.6 %collective-permute-start.4 = (f32[776,128]{1,0:T(8,128)S(1)}, f32[776,128]{1,0:T(8,128)S(1)}, u32[]{:S(2)}, u32[]{:S(2)}) collective-permute-start(f32[776,128]{1,0:T(8,128)S(1)} %get-tuple-element.23), channel_id=1, source_target_pairs={{0,16},{16,0},{1,17},{17,1},{2,18},{18,2},{3,19},{19,3},{4,20},{20... | collective-permute-start | bytes 1191944 | tf_op jit(solution)/shard_map/ppermute | solution.py:383
  47.2 23.3 %all-to-all-start = ((f32[32,16,128]{2,1,0:T(8,128)}), f32[32,16,128]{2,1,0:T(8,128)S(1)}, u32[]{:S(2)}, u32[]{:S(2)}) async-start(f32[32,16,128]{2,1,0:T(8,128)} %bitcast.2), calls=%async_computation | async-start | bytes 524288 | tf_op jit(solution)/shard_map/all_to_all | solution.py:391
  58.7 21.4 %collective-permute-start.5 = (f32[264,128]{1,0:T(8,128)S(1)}, f32[264,128]{1,0:T(8,128)S(1)}, u32[]{:S(2)}, u32[]{:S(2)}) collective-permute-start(f32[264,128]{1,0:T(8,128)S(1)} %get-tuple-element.24), channel_id=1, source_target_pairs={{16,32},{48,64},{80,96},{112,128},{144,160},{176,192},{208,224},{2... | collective-permute-start | bytes 405512 | tf_op jit(solution)/shard_map/ppermute | solution.py:384
  71.2 16.2 %all-to-all-start.1 = ((f32[8,16,128]{2,1,0:T(8,128)}), f32[8,16,128]{2,1,0:T(8,128)S(1)}, u32[]{:S(2)}, u32[]{:S(2)}) async-start(f32[8,16,128]{2,1,0:T(8,128)} %broadcast_in_dim.6), calls=%async_computation.1 | async-start | bytes 131072 | tf_op jit(solution)/shard_map/all_to_all | solution.py:401
  81.1 6.3 %collective-permute-start.6 = (f32[2,64,128]{2,1,0:T(8,128)S(1)}, f32[2,64,128]{2,1,0:T(8,128)S(1)}, u32[]{:S(2)}, u32[]{:S(2)}) collective-permute-start(f32[2,64,128]{2,1,0:T(8,128)S(1)} %get-tuple-element.27), channel_id=1, source_target_pairs={{0,1},{2,3},{4,5},{6,7},{8,9},{10,11},{12,13},{14,15},{1,0},{3,2},... | collective-permute-start | bytes 196616 | tf_op jit(solution)/shard_map/ppermute | solution.py:403
  88.1 15.0 %all-to-all-start.2 = ((f32[32,16,128]{2,1,0:T(8,128)}), f32[32,16,128]{2,1,0:T(8,128)S(1)}, u32[]{:S(2)}, u32[]{:S(2)}) async-start(f32[32,16,128]{2,1,0:T(8,128)} %broadcast_in_dim.7), calls=%async_computation.2 | async-start | bytes 524288 | tf_op jit(solution)/shard_map/all_to_all | solution.py:407
  92.7 0.7 collective-permute-start.7
  103.1 8.0 %collective-permute-start.8 = (f32[4,128,128]{2,1,0:T(8,128)S(1)}, f32[4,128,128]{2,1,0:T(8,128)S(1)}, u32[]{:S(2)}, u32[]{:S(2)}) collective-permute-start(f32[4,128,128]{2,1,0:T(8,128)S(1)} %bitcast.15), channel_id=1, source_target_pairs={{0,16},{16,0},{1,17},{17,1},{2,18},{18,2},{3,19},{19,3},{4,20},{20... | collective-permute-start | bytes 786440 | tf_op jit(solution)/shard_map/ppermute | solution.py:410

commit v5 on v3

--- a/solution.py
+++ b/solution.py
@@ -168,7 +168,7 @@
     return pltpu.roll(wide, lax.rem(2 * side - step, 2 * side), 1)[:, :side]
 
 
-def edges_kernel(own, with_even, with_odd):
+def edges_kernel(scan, own, with_even, with_odd, column, column_near):
     rows, cols = own.shape[2], own.shape[3]
     side = with_even.shape[2]
     half = side // 2
@@ -179,46 +179,60 @@
         right = jnp.where(inner, pltpu.roll(imaginary[:, cols - side :], half, 1), real[:, cols - side :])
         with_even[layer] = jnp.where(even_col(), right, left)
         with_odd[layer] = jnp.where(even_col(), left, right)
-
-
-def beyond_kernel(scan_beyond, own, with_even, with_odd, to_beyond, frame):
+    unused, col = place_of(scan, rows, cols, half)
+    column[...] = jnp.full(column.shape, col.astype(jnp.float32))
+    column_near[...] = jnp.full(column_near.shape, col.astype(jnp.float32))
+
+
+def partner_column(column, cols):
+    return jnp.clip(jnp.max(column[0:8, :]).astype(jnp.int32), 0, cols - 1)
+
+
+def beyond_kernel(column, own, with_even, with_odd, to_beyond, frame):
     rows, cols = own.shape[2], own.shape[3]
     side = to_beyond.shape[1]
-    half = side // 2
-    unused, col = place_of(scan_beyond, rows, cols, half)
-    col = jnp.clip(col, 0, cols - 1)
+    col = partner_column(column, cols)
     for layer in range(2):
         for part in range(2):
             plane = 2 * part + layer
             fill(frame, own, with_even, with_odd, part, layer)
-            to_beyond[pl.ds(plane * rows, rows), :] = cut(frame, plane, col + half, side)
-
-
-def near_kernel(scan, frame, other, probe, pattern, tabs, near):
-    rows, cols = frame.shape[1], frame.shape[2] - 2 * near.shape[2]
-    side = near.shape[2]
+            to_beyond[pl.ds(plane * rows, rows), :] = cut(frame, plane, col + side // 2, side)
+    to_beyond[pl.ds(4 * rows, 8), :] = jnp.zeros((8, side), jnp.float32)
+
+
+def core_kernel(column, frame, to_core):
+    side = to_core.shape[1]
+    rows, cols = frame.shape[1], frame.shape[2] - 2 * side
+    col = partner_column(column, cols)
+    for plane in range(4):
+        to_core[pl.ds(plane * rows, rows), :] = cut(frame, plane, col + side // 2, side)
+
+
+def near_kernel(scan, frame, probe, pattern, tabs, near):
+    rows, cols = frame.shape[1], frame.shape[2] - 2 * near.shape[1]
+    side = near.shape[1]
     half = side // 2
     unused, col = place_of(scan, rows, cols, half)
     for plane in range(4):
-        near[plane, 0:rows, :] = cut(frame, plane, col + half, side)
-        near[plane, rows : 2 * rows, :] = cut(other, plane, col + half, side)
+        near[pl.ds(plane * rows, rows), :] = cut(frame, plane, col + half, side)
 
 
 def main_kernel(
-    scan, live, near, beyond, probe, pattern, tabs,
+    scan, live, near, other, beyond, probe, pattern, tabs,
     keep, message_core, message_beyond, own_strip, column, shifted,
 ):
     side = probe.shape[-1]
     half = side // 2
-    rows = beyond.shape[0] // 4
+    rows = own_strip.shape[0] // 4
     cols = TILE_COLS
     modes = probe.shape[1]
     row, col = place_of(scan, rows, cols, half)
     other_at, beyond_at = strips_at(half)
     for plane in range(4):
-        column[plane, half : half + rows, :] = near[plane, 0:rows, :]
-        column[plane, pl.ds(other_at, rows), :] = near[plane, rows : 2 * rows, :]
-        column[plane, pl.ds(beyond_at, rows), :] = beyond[pl.ds(plane * rows, rows), :]
+        at = pl.ds(plane * rows, rows)
+        column[plane, half : half + rows, :] = near[at, :]
+        column[plane, pl.ds(other_at, rows), :] = other[at, :]
+        column[plane, pl.ds(beyond_at, rows), :] = beyond[at, :]
     tall = side + 8
     step = lax.rem(row, 8)
     base_row = pl.multiple_of(row - step, 8)
@@ -345,22 +359,26 @@
     def shape(*dims):
         return jax.ShapeDtypeStruct(dims, f32)
 
-    scan_beyond = lax.ppermute(scan, ROW, pairs)
     edge = shape(2, rows, side)
-    to_even, to_odd = call(edges_kernel, [edge, edge], 0, 1)(obj_field)
+    to_even, to_odd, column, column_near = call(
+        edges_kernel, [edge, edge, shape(136, side), shape(8, side)], 1, 1
+    )(scan, obj_field)
+    column = lax.ppermute(column, ROW, pairs)
     with_even = lax.ppermute(to_even, COL, even_pairs)
     with_odd = lax.ppermute(to_odd, COL, odd_pairs)
+    column_near = lax.ppermute(column_near, "core", swap)
     to_beyond, frame = call(
-        beyond_kernel, [shape(strip, side), shape(4, rows, cols + 2 * side)], 1, 3
-    )(scan_beyond, obj_field, with_even, with_odd)
-    other = lax.ppermute(frame, "core", swap)
+        beyond_kernel, [shape(strip + 8, side), shape(4, rows, cols + 2 * side)], 0, 4
+    )(column, obj_field, with_even, with_odd)
     beyond = lax.ppermute(to_beyond, ROW, pairs)
+    to_core = call(core_kernel, shape(strip, side), 0, 2)(column_near, frame)
+    other = lax.ppermute(to_core, "core", swap)
     tabs = jnp.asarray(tables(side))
     small = pl.CostEstimate(flops=1000, bytes_accessed=1000, transcendentals=0)
-    near = call(near_kernel, shape(4, 2 * rows, side), 1, 5, cost=small)(
-        scan, frame, other, probe, patterns, tabs
-    )
-    near, beyond = lax.optimization_barrier((near, beyond))
+    near = call(near_kernel, shape(strip, side), 1, 4, cost=small)(
+        scan, frame, probe, patterns, tabs
+    )
+    near, other, beyond = lax.optimization_barrier((near, other, beyond))
     tall = pltpu.VMEM((4, 2 * half + rows, side), f32)
     keep, message_core, message_beyond, own_strip = call(
         main_kernel,
@@ -371,9 +389,9 @@
             shape(strip, side),
         ],
         2,
-        5,
+        6,
         [tall, tall],
-    )(scan, live, near, beyond, probe, patterns, tabs)
+    )(scan, live, near, other, beyond, probe, patterns, tabs)
 
     from_core = lax.ppermute(message_core, "core", swap)
     from_beyond = lax.ppermute(message_beyond, ROW, pairs)

time: 110 us -> 108 us (0.982)
  starting transfers between devices: 73.3 us -> 65.9 us
  waiting for transfers between devices: 21 us -> 27 us
    ppermute x1, starting transfers between devices: 7.99 us -> 3.48 us  [body(): beyond = lax.ppermute(to_beyond, ROW, pairs)]
    all_to_all x1, waiting for transfers between devices: 4.79 us -> 8.39 us  [body(): spread = lax.all_to_all(summed.reshape(n_yx, chunk, side), ('y', 'x'), 0, 0)]
    ppermute x2 -> x3, starting transfers between devices: 12.6 us -> 16 us  [the longest x1 12 us: body(): column = lax.ppermute(column, ROW, pairs)]
    ppermute x1, starting transfers between devices: 6.79 us -> 3.43 us  [body(): from_beyond = lax.ppermute(message_beyond, ROW, pairs)]
    ppermute x1, waiting for transfers between devices: 0.2 us -> 3.27 us  [body(): beyond = lax.ppermute(to_beyond, ROW, pairs)]
    all_to_all x1, starting transfers between devices: 5.61 us -> 3.35 us  [body(): lax.all_to_all(jnp.broadcast_to(part, (n_z, chunk, side)), ('zh', 'zl'),...]
    ppermute x1, starting transfers between devices: 4.83 us -> 3.1 us  [body(): with_even = lax.ppermute(to_even, COL, even_pairs)]
    all_to_all x1, starting transfers between devices: 4.6 us -> 6.09 us  [body(): whole = lax.all_to_all(part, ('y', 'x'), 0, 0)]
  transfers between devices with their start and end apart: 13 -> 14, of which waited for: 7 -> 7; matrix products, arithmetic and copies ran while one was open for 1% -> 1% of each run, Pallas kernels for 2% -> 3%
where the time goes in v5:
time: 108 us; the launch traced here: 107 us
  starting transfers between devices  65.9 us (61%)
  waiting for transfers between devices  27 us (25%)
  Pallas kernels  8.32 us (8%)
  local copies, waits for them, and re-layouts  2.98 us (3%)
  other arithmetic  1.67 us (2%)
  between operations  1.55 us (1%)
    all_to_all x1, starting transfers between devices, body(): spread = lax.all_to_all(summed.reshape(n_yx, chunk, side), ('y', 'x'), 0, 0)  18.8 us
    ppermute x1, starting transfers between devices, body(): column = lax.ppermute(column, ROW, pairs)  12 us
    all_to_all x1, waiting for transfers between devices, body(): whole = lax.all_to_all(part, ('y', 'x'), 0, 0)  9.92 us
    all_to_all x1, waiting for transfers between devices, body(): spread = lax.all_to_all(summed.reshape(n_yx, chunk, side), ('y', 'x'), 0, 0)  8.39 us
    all_to_all x1, starting transfers between devices, body(): whole = lax.all_to_all(part, ('y', 'x'), 0, 0)  6.09 us
    ppermute x1, starting transfers between devices, body(): facing = lax.ppermute(whole, 'core', swap)  5.19 us
    pallas_call x1, Pallas kernels, body(): call(main_kernel, [shape(modes * side, side), shape(modes * side + strip...  4.67 us
    ppermute x1, starting transfers between devices, body(): beyond = lax.ppermute(to_beyond, ROW, pairs)  3.48 us
  transfers between devices with their start and end apart: 14, of which 7 were waited for; matrix products, arithmetic and copies ran while one was open for 1% of the time, Pallas kernels for 3%

profile of v5, /device:TPU:1, one launch (start us, length us, event | category | flops | bytes accessed | tf_op | source)
XLA Modules:
  0.0 107.4 jit_solution(18023705602123729138)
XLA Ops:
  1.3 0.9 copy-done.2
  2.9 12.0 %collective-permute-start = (f32[136,128]{1,0:T(8,128)S(1)}, f32[136,128]{1,0:T(8,128)S(1)}, u32[]{:S(2)}, u32[]{:S(2)}) collective-permute-start(f32[136,128]{1,0:T(8,128)S(1)} %get-tuple-element.23), channel_id=1, source_target_pairs={{16,32},{48,64},{80,96},{112,128},{144,160},{176,192},{208,224},{2... | collective-permute-start | bytes 208904 | tf_op jit(solution)/shard_map/ppermute | solution.py:366
  14.9 3.1 %collective-permute-start.1 = (f32[2,64,128]{2,1,0:T(8,128)S(1)}, f32[2,64,128]{2,1,0:T(8,128)S(1)}, u32[]{:S(2)}, u32[]{:S(2)}) collective-permute-start(f32[2,64,128]{2,1,0:T(8,128)S(1)} %get-tuple-element.24), channel_id=1, source_target_pairs={{0,1},{2,3},{4,5},{6,7},{8,9},{10,11},{12,13},{14,15},{1,0},{3,2},... | collective-permute-start | bytes 196616 | tf_op jit(solution)/shard_map/ppermute | solution.py:367
  18.7 2.1 %collective-permute-start.3 = (f32[8,128]{1,0:T(8,128)S(1)}, f32[8,128]{1,0:T(8,128)S(1)}, u32[]{:S(2)}, u32[]{:S(2)}) collective-permute-start(f32[8,128]{1,0:T(8,128)S(1)} %get-tuple-element.27), channel_id=1, source_target_pairs={{0,16},{16,0},{1,17},{17,1},{2,18},{18,2},{3,19},{19,3},{4,20},{20... | collective-permute-start | bytes 12296 | tf_op jit(solution)/shard_map/ppermute | solution.py:369
  21.5 3.5 %collective-permute-start.5 = (f32[264,128]{1,0:T(8,128)S(1)}, f32[264,128]{1,0:T(8,128)S(1)}, u32[]{:S(2)}, u32[]{:S(2)}) collective-permute-start(f32[264,128]{1,0:T(8,128)S(1)} %get-tuple-element.28), channel_id=1, source_target_pairs={{16,32},{48,64},{80,96},{112,128},{144,160},{176,192},{208,224},{2... | collective-permute-start | bytes 405512 | tf_op jit(solution)/shard_map/ppermute | solution.py:373
  25.3 1.9 %collective-permute-start.4 = (f32[256,128]{1,0:T(8,128)S(1)}, f32[256,128]{1,0:T(8,128)S(1)}, u32[]{:S(2)}, u32[]{:S(2)}) collective-permute-start(f32[256,128]{1,0:T(8,128)S(1)} %shard_map.80), channel_id=1, source_target_pairs={{0,16},{16,0},{1,17},{17,1},{2,18},{18,2},{3,19},{19,3},{4,20},{20... | collective-permute-start | bytes 393224 | tf_op jit(solution)/shard_map/ppermute | solution.py:375
  28.6 3.3 %collective-permute-done.5.beyond = f32[264,128]{1,0:T(8,128)S(1)} collective-permute-done((f32[264,128]{1,0:T(8,128)S(1)}, f32[264,128]{1,0:T(8,128)S(1)}, u32[]{:S(2)}, u32[]{:S(2)}) %collective-permute-start.5) | collective-permute-done | bytes 135200 | tf_op jit(solution)/shard_map/ppermute | solution.py:373
  31.9 4.7 %shard_map.81 = (f32[512,128]{1,0:T(8,128)S(1)}, f32[776,128]{1,0:T(8,128)S(1)}, f32[264,128]{1,0:T(8,128)S(1)}, f32[256,128]{1,0:T(8,128)S(1)}) custom-call(s32[2]{0:T(128)S(1)} %bitcast.14, s32[1]{0:T(128)} %bitcast.11.live, f32[256,128]{1,0:T(8,128)S(1)} %shard_map.79.near, f32[256,128]{1,0:T(8,128)S(1)} %collective-permute-done.4.other, ...), custom_call_target="tpu_custom_call" | custom-call | tf_op jit(solution)/shard_map/pallas_call | solution.py:383
  36.6 1.9 %collective-permute-start.6 = (f32[776,128]{1,0:T(8,128)S(1)}, f32[776,128]{1,0:T(8,128)S(1)}, u32[]{:S(2)}, u32[]{:S(2)}) collective-permute-start(f32[776,128]{1,0:T(8,128)S(1)} %get-tuple-element.33), channel_id=1, source_target_pairs={{0,16},{16,0},{1,17},{17,1},{2,18},{18,2},{3,19},{19,3},{4,20},{20... | collective-permute-start | bytes 1191944 | tf_op jit(solution)/shard_map/ppermute | solution.py:396
  38.5 1.7 %collective-permute-done.6.from_core = f32[776,128]{1,0:T(8,128)S(1)} collective-permute-done((f32[776,128]{1,0:T(8,128)S(1)}, f32[776,128]{1,0:T(8,128)S(1)}, u32[]{:S(2)}, u32[]{:S(2)}) %collective-permute-start.6) | collective-permute-done | bytes 397344 | tf_op jit(solution)/shard_map/ppermute | solution.py:396
  40.2 0.7 slice_add_fusion
  41.0 18.8 %all-to-all-start = ((f32[32,16,128]{2,1,0:T(8,128)}), f32[32,16,128]{2,1,0:T(8,128)S(1)}, u32[]{:S(2)}, u32[]{:S(2)}) async-start(f32[32,16,128]{2,1,0:T(8,128)} %bitcast.2), calls=%async_computation | async-start | bytes 524288 | tf_op jit(solution)/shard_map/all_to_all | solution.py:404
  59.7 3.4 %collective-permute-start.7 = (f32[264,128]{1,0:T(8,128)S(1)}, f32[264,128]{1,0:T(8,128)S(1)}, u32[]{:S(2)}, u32[]{:S(2)}) collective-permute-start(f32[264,128]{1,0:T(8,128)S(1)} %get-tuple-element.34), channel_id=1, source_target_pairs={{16,32},{48,64},{80,96},{112,128},{144,160},{176,192},{208,224},{2... | collective-permute-start | bytes 405512 | tf_op jit(solution)/shard_map/ppermute | solution.py:397
  63.2 8.4 %all-to-all-done = f32[32,16,128]{2,1,0:T(8,128)S(1)} async-done(((f32[32,16,128]{2,1,0:T(8,128)}), f32[32,16,128]{2,1,0:T(8,128)S(1)}, u32[]{:S(2)}, u32[]{:S(2)}) %all-to-all-start) | async-done | bytes 262176 | tf_op jit(solution)/shard_map/all_to_all | solution.py:404
  72.3 3.4 %all-to-all-start.1 = ((f32[8,16,128]{2,1,0:T(8,128)}), f32[8,16,128]{2,1,0:T(8,128)S(1)}, u32[]{:S(2)}, u32[]{:S(2)}) async-start(f32[8,16,128]{2,1,0:T(8,128)} %broadcast_in_dim.6), calls=%async_computation.1 | async-start | bytes 131072 | tf_op jit(solution)/shard_map/all_to_all | solution.py:414
  75.6 1.0 shard_map.82
  76.6 3.3 %collective-permute-start.8 = (f32[2,64,128]{2,1,0:T(8,128)S(1)}, f32[2,64,128]{2,1,0:T(8,128)S(1)}, u32[]{:S(2)}, u32[]{:S(2)}) collective-permute-start(f32[2,64,128]{2,1,0:T(8,128)S(1)} %get-tuple-element.37), channel_id=1, source_target_pairs={{0,1},{2,3},{4,5},{6,7},{8,9},{10,11},{12,13},{14,15},{1,0},{3,2},... | collective-permute-start | bytes 196616 | tf_op jit(solution)/shard_map/ppermute | solution.py:416
  79.8 2.9 %all-to-all-done.1 = f32[8,16,128]{2,1,0:T(8,128)S(1)} async-done(((f32[8,16,128]{2,1,0:T(8,128)}), f32[8,16,128]{2,1,0:T(8,128)S(1)}, u32[]{:S(2)}, u32[]{:S(2)}) %all-to-all-start.1) | async-done | bytes 65568 | tf_op jit(solution)/shard_map/all_to_all | solution.py:414
  82.8 0.7 broadcast_in_dim.7
  83.5 6.1 %all-to-all-start.2 = ((f32[32,16,128]{2,1,0:T(8,128)}), f32[32,16,128]{2,1,0:T(8,128)S(1)}, u32[]{:S(2)}, u32[]{:S(2)}) async-start(f32[32,16,128]{2,1,0:T(8,128)} %broadcast_in_dim.7), calls=%async_computation.2 | async-start | bytes 524288 | tf_op jit(solution)/shard_map/all_to_all | solution.py:420
  90.3 9.9 %all-to-all-done.2 = f32[32,16,128]{2,1,0:T(8,128)S(1)} async-done(((f32[32,16,128]{2,1,0:T(8,128)}), f32[32,16,128]{2,1,0:T(8,128)S(1)}, u32[]{:S(2)}, u32[]{:S(2)}) %all-to-all-start.2) | async-done | bytes 262176 | tf_op jit(solution)/shard_map/all_to_all | solution.py:420
  100.2 5.2 %collective-permute-start.10 = (f32[4,128,128]{2,1,0:T(8,128)S(1)}, f32[4,128,128]{2,1,0:T(8,128)S(1)}, u32[]{:S(2)}, u32[]{:S(2)}) collective-permute-start(f32[4,128,128]{2,1,0:T(8,128)S(1)} %bitcast.16), channel_id=1, source_target_pairs={{0,16},{16,0},{1,17},{17,1},{2,18},{18,2},{3,19},{19,3},{4,20},{20... | collective-permute-start | bytes 786440 | tf_op jit(solution)/shard_map/ppermute | solution.py:423
  105.4 0.8 shard_map.83
  106.6 0.8 pad_maximum_fusion
  (30 shorter events, 5.4 us)
Async XLA Ops:
  0.6 0.7 copy-start.5
  1.3 0.9 copy-start.2
  2.2 19.0 %copy-start.3 = (f32[2,2,64,256]{3,2,1,0:T(8,128)S(1)}, f32[2,2,64,256]{3,2,1,0:T(8,128)}, u32[]{:S(2)}) copy-start(f32[2,2,64,256]{3,2,1,0:T(8,128)} %own.3) | copy-start | bytes 786436
  2.9 18.4 %collective-permute-start = (f32[136,128]{1,0:T(8,128)S(1)}, f32[136,128]{1,0:T(8,128)S(1)}, u32[]{:S(2)}, u32[]{:S(2)}) collective-permute-start(f32[136,128]{1,0:T(8,128)S(1)} %get-tuple-element.23), channel_id=1, source_target_pairs={{16,32},{48,64},{80,96},{112,128},{144,160},{176,192},{208,224},{2... | collective-permute-start | bytes 208904 | tf_op jit(solution)/shard_map/ppermute | solution.py:366
  14.9 6.3 %collective-permute-start.1 = (f32[2,64,128]{2,1,0:T(8,128)S(1)}, f32[2,64,128]{2,1,0:T(8,128)S(1)}, u32[]{:S(2)}, u32[]{:S(2)}) collective-permute-start(f32[2,64,128]{2,1,0:T(8,128)S(1)} %get-tuple-element.24), channel_id=1, source_target_pairs={{0,1},{2,3},{4,5},{6,7},{8,9},{10,11},{12,13},{14,15},{1,0},{3,2},... | collective-permute-start | bytes 196616 | tf_op jit(solution)/shard_map/ppermute | solution.py:367
  18.0 3.2 %collective-permute-start.2 = (f32[2,64,128]{2,1,0:T(8,128)S(1)}, f32[2,64,128]{2,1,0:T(8,128)S(1)}, u32[]{:S(2)}, u32[]{:S(2)}) collective-permute-start(f32[2,64,128]{2,1,0:T(8,128)S(1)} %get-tuple-element.25), channel_id=1, source_target_pairs={{1,2},{3,4},{5,6},{7,8},{9,10},{11,12},{13,14},{2,1},{4,3},{6,5},{... | collective-permute-start | bytes 196616 | tf_op jit(solution)/shard_map/ppermute | solution.py:368
  18.7 9.2 %copy-start = (f32[2,4,128,128]{3,2,1,0:T(8,128)S(1)}, f32[2,4,128,128]{3,2,1,0:T(8,128)}, u32[]{:S(2)}) copy-start(f32[2,4,128,128]{3,2,1,0:T(8,128)} %probe.3) | copy-start | bytes 1572868
  18.7 6.3 %collective-permute-start.3 = (f32[8,128]{1,0:T(8,128)S(1)}, f32[8,128]{1,0:T(8,128)S(1)}, u32[]{:S(2)}, u32[]{:S(2)}) collective-permute-start(f32[8,128]{1,0:T(8,128)S(1)} %get-tuple-element.27), channel_id=1, source_target_pairs={{0,16},{16,0},{1,17},{17,1},{2,18},{18,2},{3,19},{19,3},{4,20},{20... | collective-permute-start | bytes 12296 | tf_op jit(solution)/shard_map/ppermute | solution.py:369
  21.5 6.4 %copy-start.1 = (bf16[12,128,128]{2,1,0:T(8,128)(2,1)S(1)}, bf16[12,128,128]{2,1,0:T(8,128)(2,1)}, u32[]{:S(2)}) copy-start(bf16[12,128,128]{2,1,0:T(8,128)(2,1)} %constant.12.clone.tabs) | copy-start | bytes 1179652
  21.5 10.4 %collective-permute-start.5 = (f32[264,128]{1,0:T(8,128)S(1)}, f32[264,128]{1,0:T(8,128)S(1)}, u32[]{:S(2)}, u32[]{:S(2)}) collective-permute-start(f32[264,128]{1,0:T(8,128)S(1)} %get-tuple-element.28), channel_id=1, source_target_pairs={{16,32},{48,64},{80,96},{112,128},{144,160},{176,192},{208,224},{2... | collective-permute-start | bytes 405512 | tf_op jit(solution)/shard_map/ppermute | solution.py:373
  25.0 2.9 %copy-start.4 = (f32[1,1,1,128,128]{4,3,2,1,0:T(8,128)S(1)}, f32[1,1,1,128,128]{4,3,2,1,0:T(8,128)}, u32[]{:S(2)}) copy-start(f32[1,1,1,128,128]{4,3,2,1,0:T(8,128)} %pattern.3) | copy-start | bytes 196612
  25.3 3.3 %collective-permute-start.4 = (f32[256,128]{1,0:T(8,128)S(1)}, f32[256,128]{1,0:T(8,128)S(1)}, u32[]{:S(2)}, u32[]{:S(2)}) collective-permute-start(f32[256,128]{1,0:T(8,128)S(1)} %shard_map.80), channel_id=1, source_target_pairs={{0,16},{16,0},{1,17},{17,1},{2,18},{18,2},{3,19},{19,3},{4,20},{20... | collective-permute-start | bytes 393224 | tf_op jit(solution)/shard_map/ppermute | solution.py:375
  36.6 3.6 %collective-permute-start.6 = (f32[776,128]{1,0:T(8,128)S(1)}, f32[776,128]{1,0:T(8,128)S(1)}, u32[]{:S(2)}, u32[]{:S(2)}) collective-permute-start(f32[776,128]{1,0:T(8,128)S(1)} %get-tuple-element.33), channel_id=1, source_target_pairs={{0,16},{16,0},{1,17},{17,1},{2,18},{18,2},{3,19},{19,3},{4,20},{20... | collective-permute-start | bytes 1191944 | tf_op jit(solution)/shard_map/ppermute | solution.py:396
  41.0 30.6 %all-to-all-start = ((f32[32,16,128]{2,1,0:T(8,128)}), f32[32,16,128]{2,1,0:T(8,128)S(1)}, u32[]{:S(2)}, u32[]{:S(2)}) async-start(f32[32,16,128]{2,1,0:T(8,128)} %bitcast.2), calls=%async_computation | async-start | bytes 524288 | tf_op jit(solution)/shard_map/all_to_all | solution.py:404
  59.7 15.9 %collective-permute-start.7 = (f32[264,128]{1,0:T(8,128)S(1)}, f32[264,128]{1,0:T(8,128)S(1)}, u32[]{:S(2)}, u32[]{:S(2)}) collective-permute-start(f32[264,128]{1,0:T(8,128)S(1)} %get-tuple-element.34), channel_id=1, source_target_pairs={{16,32},{48,64},{80,96},{112,128},{144,160},{176,192},{208,224},{2... | collective-permute-start | bytes 405512 | tf_op jit(solution)/shard_map/ppermute | solution.py:397
  72.3 10.5 %all-to-all-start.1 = ((f32[8,16,128]{2,1,0:T(8,128)}), f32[8,16,128]{2,1,0:T(8,128)S(1)}, u32[]{:S(2)}, u32[]{:S(2)}) async-start(f32[8,16,128]{2,1,0:T(8,128)} %broadcast_in_dim.6), calls=%async_computation.1 | async-start | bytes 131072 | tf_op jit(solution)/shard_map/all_to_all | solution.py:414
  76.6 6.2 %collective-permute-start.8 = (f32[2,64,128]{2,1,0:T(8,128)S(1)}, f32[2,64,128]{2,1,0:T(8,128)S(1)}, u32[]{:S(2)}, u32[]{:S(2)}) collective-permute-start(f32[2,64,128]{2,1,0:T(8,128)S(1)} %get-tuple-element.37), channel_id=1, source_target_pairs={{0,1},{2,3},{4,5},{6,7},{8,9},{10,11},{12,13},{14,15},{1,0},{3,2},... | collective-permute-start | bytes 196616 | tf_op jit(solution)/shard_map/ppermute | solution.py:416
  83.5 16.7 %all-to-all-start.2 = ((f32[32,16,128]{2,1,0:T(8,128)}), f32[32,16,128]{2,1,0:T(8,128)S(1)}, u32[]{:S(2)}, u32[]{:S(2)}) async-start(f32[32,16,128]{2,1,0:T(8,128)} %broadcast_in_dim.7), calls=%async_computation.2 | async-start | bytes 524288 | tf_op jit(solution)/shard_map/all_to_all | solution.py:420
  89.6 0.7 collective-permute-start.9
  100.2 6.3 %collective-permute-start.10 = (f32[4,128,128]{2,1,0:T(8,128)S(1)}, f32[4,128,128]{2,1,0:T(8,128)S(1)}, u32[]{:S(2)}, u32[]{:S(2)}) collective-permute-start(f32[4,128,128]{2,1,0:T(8,128)S(1)} %bitcast.16), channel_id=1, source_target_pairs={{0,16},{16,0},{1,17},{17,1},{2,18},{18,2},{3,19},{19,3},{4,20},{20... | collective-permute-start | bytes 786440 | tf_op jit(solution)/shard_map/ppermute | solution.py:423

commit v6 on v5

--- a/solution.py
+++ b/solution.py
@@ -70,26 +70,27 @@
     return dot(left_high, right_high) + (dot(left_low, right_high) + dot(left_high, right_low))
 
 
-def two_sided(real, imaginary, right, left):
+def two_sided(real, imaginary, right, left, group=2):
     side = real[0].shape[0]
-    modes = len(real)
-    stacked = jnp.concatenate(
-        [jnp.concatenate([r, i], axis=1) for r, i in zip(real, imaginary)], axis=0
-    )
-    middle = product(split(stacked), right)
-    blocks = [middle[m * side : (m + 1) * side] for m in range(modes)]
-    spread = jnp.concatenate(
-        [
-            jnp.concatenate([b[:, :side] for b in blocks], axis=1),
-            jnp.concatenate([b[:, side:] for b in blocks], axis=1),
-        ],
-        axis=0,
-    )
-    out = product(left, split(spread))
-    return (
-        [out[:side, m * side : (m + 1) * side] for m in range(modes)],
-        [out[side:, m * side : (m + 1) * side] for m in range(modes)],
-    )
+    middles = []
+    for n in range(0, len(real), group):
+        pairs = zip(real[n : n + group], imaginary[n : n + group])
+        stacked = jnp.concatenate([jnp.concatenate(pair, axis=1) for pair in pairs], axis=0)
+        middles.append(product(split(stacked), right))
+    out_real, out_imaginary = [], []
+    for middle in middles:
+        blocks = [middle[m * side : (m + 1) * side] for m in range(group)]
+        spread = jnp.concatenate(
+            [
+                jnp.concatenate([block[:, :side] for block in blocks], axis=1),
+                jnp.concatenate([block[:, side:] for block in blocks], axis=1),
+            ],
+            axis=0,
+        )
+        out = product(left, split(spread))
+        out_real += [out[:side, m * side : (m + 1) * side] for m in range(group)]
+        out_imaginary += [out[side:, m * side : (m + 1) * side] for m in range(group)]
+    return out_real, out_imaginary
 
 
 def times(ar, ai, br, bi):
@@ -179,9 +180,9 @@
         right = jnp.where(inner, pltpu.roll(imaginary[:, cols - side :], half, 1), real[:, cols - side :])
         with_even[layer] = jnp.where(even_col(), right, left)
         with_odd[layer] = jnp.where(even_col(), left, right)
-    unused, col = place_of(scan, rows, cols, half)
-    column[...] = jnp.full(column.shape, col.astype(jnp.float32))
-    column_near[...] = jnp.full(column_near.shape, col.astype(jnp.float32))
+    col = (scan[:, 1:2] - (lax.axis_index(COL) * cols - half)).astype(jnp.float32)
+    column[...] = jnp.broadcast_to(col, column.shape)
+    column_near[...] = jnp.broadcast_to(col, column_near.shape)
 
 
 def partner_column(column, cols):
@@ -305,7 +306,21 @@
         centre[1, layer] = frame[imaginary, :, side : side + cols]
 
 
-def finish_kernel(centre, with_even, with_odd, out):
+def add_kernel(keep, message, out):
+    out[...] = keep[...] + message[0 : keep.shape[0], :]
+
+
+def sum_kernel(parts, copies):
+    total = parts[0]
+    for n in range(1, parts.shape[0]):
+        total = total + parts[n]
+    for n in range(copies.shape[0]):
+        copies[n] = total
+
+
+def finish_kernel(centre, with_even, with_odd, whole, out, probe_grad, total, sem, out_sem):
+    copy = pltpu.make_async_copy(whole, probe_grad.at[lax.axis_index("core")], sem)
+    copy.start()
     rows, cols = centre.shape[2], centre.shape[3]
     side = with_even.shape[2]
     half = side // 2
@@ -318,18 +333,30 @@
             if part:
                 left, right = pltpu.roll(left, half, 1), pltpu.roll(right, half, 1)
             value = centre[part, layer]
-            out[part, layer, :, 0:side] = value[:, :side] + jnp.where(inner, left, zero)
-            out[part, layer, :, cols - side :] = value[:, cols - side :] + jnp.where(inner, zero, right)
-
-
-def call(kernel, out_shape, n_scalars, n_in, scratch=(), cost=None):
+            total[part, layer, :, 0:side] = value[:, :side] + jnp.where(inner, left, zero)
+            total[part, layer, :, cols - side :] = value[:, cols - side :] + jnp.where(inner, zero, right)
+    out_copy = pltpu.make_async_copy(total, out, out_sem)
+    out_copy.start()
+    copy.wait()
+    out_copy.wait()
+
+
+def other_half_kernel(facing, half_done, probe_grad, sem):
+    copy = pltpu.make_async_copy(facing, probe_grad.at[1 - lax.axis_index("core")], sem)
+    copy.start()
+    copy.wait()
+
+
+def call(kernel, out_shape, n_scalars, n_in, scratch=(), cost=None, n_far=0, out_far=(), aliases=None):
     many = isinstance(out_shape, (list, tuple))
     vmem = pl.BlockSpec(memory_space=pltpu.VMEM)
+    far = pl.BlockSpec(memory_space=pltpu.HBM)
     return pl.pallas_call(
         kernel,
         out_shape=out_shape,
-        in_specs=[pl.BlockSpec(memory_space=pltpu.SMEM)] * n_scalars + [vmem] * n_in,
-        out_specs=[vmem] * len(out_shape) if many else vmem,
+        in_specs=[pl.BlockSpec(memory_space=pltpu.SMEM)] * n_scalars + [vmem] * n_in + [far] * n_far,
+        out_specs=[far if n in out_far else vmem for n in range(len(out_shape))] if many else vmem,
+        input_output_aliases=aliases or {},
         scratch_shapes=list(scratch),
         compiler_params=pltpu.CompilerParams(vmem_limit_bytes=VMEM_LIMIT),
         cost_estimate=cost,
@@ -347,7 +374,6 @@
     rows, cols = obj_field.shape[2], obj_field.shape[3]
     n_row, n_col = lax.axis_size(ROW), lax.axis_size(COL)
     f32 = jnp.float32
-    core = lax.axis_index("core")
     scan = scan_pos.reshape(2)
     live = live_count.reshape(1)
     swap = [(0, 1), (1, 0)]
@@ -361,8 +387,8 @@
 
     edge = shape(2, rows, side)
     to_even, to_odd, column, column_near = call(
-        edges_kernel, [edge, edge, shape(136, side), shape(8, side)], 1, 1
-    )(scan, obj_field)
+        edges_kernel, [edge, edge, shape(136, side), shape(8, side)], 0, 2
+    )(scan.reshape(1, 2), obj_field)
     column = lax.ppermute(column, ROW, pairs)
     with_even = lax.ppermute(to_even, COL, even_pairs)
     with_odd = lax.ppermute(to_odd, COL, odd_pairs)
@@ -400,7 +426,7 @@
     n_z = lax.axis_size(("zh", "zl"))
     total = modes * side
     chunk = total // n_yx
-    summed = keep + from_core[:total]
+    summed = call(add_kernel, shape(total, side), 0, 2)(keep, from_core)
     spread = lax.all_to_all(summed.reshape(n_yx, chunk, side), ("y", "x"), 0, 0)
 
     centre, grad_even, grad_odd = call(
@@ -410,21 +436,34 @@
         3,
         [pltpu.VMEM((4, rows, cols + 2 * side), f32)],
     )(scan, own_strip, from_core, from_beyond)
-    part = jnp.sum(spread, axis=0)
-    part = lax.all_to_all(jnp.broadcast_to(part, (n_z, chunk, side)), ("zh", "zl"), 0, 0)
-    part = jnp.sum(part, axis=0)
+    part = call(sum_kernel, shape(n_z, chunk, side), 0, 1)(spread)
+    part = lax.all_to_all(part, ("zh", "zl"), 0, 0)
+    part = call(sum_kernel, shape(n_yx, chunk, side), 0, 1)(part)
+    part, grad_even, grad_odd = lax.optimization_barrier((part, grad_even, grad_odd))
     got_even = lax.ppermute(grad_even, COL, even_pairs)
-    part = jnp.broadcast_to(part, (n_yx, chunk, side))
-    part, got_even, grad_odd = lax.optimization_barrier((part, got_even, grad_odd))
     got_odd = lax.ppermute(grad_odd, COL, odd_pairs)
     whole = lax.all_to_all(part, ("y", "x"), 0, 0)
-    whole, got_odd = lax.optimization_barrier((whole, got_odd))
+    whole, got_even, got_odd = lax.optimization_barrier((whole, got_even, got_odd))
     whole = whole.reshape(modes, side, side)
     facing = lax.ppermute(whole, "core", swap)
-    first = core == 0
-    probe_grad = jnp.stack([jnp.where(first, whole, facing), jnp.where(first, facing, whole)])
-
-    obj_grad = call(finish_kernel, shape(2, 2, rows, cols), 0, 3)(centre, got_even, got_odd)
+    obj_grad, probe_grad = call(
+        finish_kernel,
+        [shape(2, 2, rows, cols), shape(2, modes, side, side)],
+        0,
+        4,
+        [pltpu.VMEM((2, 2, rows, cols), f32), pltpu.SemaphoreType.DMA, pltpu.SemaphoreType.DMA],
+        out_far=(0, 1),
+    )(centre, got_even, got_odd, whole)
+    (probe_grad,) = call(
+        other_half_kernel,
+        [shape(2, modes, side, side)],
+        0,
+        1,
+        [pltpu.SemaphoreType.DMA],
+        n_far=1,
+        out_far=(0,),
+        aliases={1: 0},
+    )(facing, probe_grad)
     return (obj_grad, probe_grad)
 
 

time: 108 us -> 105 us (0.972)
  starting transfers between devices: 65.9 us -> 63.8 us
  other arithmetic: 1.67 us -> 0 us
  Pallas kernels: 8.32 us -> 9.72 us
  local copies, waits for them, and re-layouts: 2.98 us -> 1.62 us
    all_to_all x1, waiting for transfers between devices: 9.92 us -> 5.51 us  [body(): whole = lax.all_to_all(part, ('y', 'x'), 0, 0)]
    all_to_all x1, waiting for transfers between devices: 2.91 us -> 6.18 us  [body(): part = lax.all_to_all(part, ('zh', 'zl'), 0, 0)]
    pallas_call x2 -> x6, Pallas kernels: 1.46 us -> 3.79 us  [the longest x1 0.84 us: body(): call(finish_kernel, [shape(2, 2, rows, cols), shape(2, modes, side, side)...]
    ppermute x1, waiting for transfers between devices: 0.01 us -> 2.14 us  [body(): got_even = lax.ppermute(grad_even, COL, even_pairs)]
    all_to_all x1, starting transfers between devices: 6.09 us -> 4.37 us  [body(): whole = lax.all_to_all(part, ('y', 'x'), 0, 0)]
    broadcast_in_dim x2 -> x0, local copies, waits for them, and re-layouts: 1.36 us -> none  [the longest x1 0.72 us: body(): part = jnp.broadcast_to(part, (n_yx, chunk, side))]
  transfers between devices with their start and end apart: 14 -> 14, of which waited for: 7 -> 8; matrix products, arithmetic and copies ran while one was open for 1% -> 0% of each run, Pallas kernels for 3% -> 4%
where the time goes in v6:
time: 105 us
  starting transfers between devices  63.8 us (61%)
  waiting for transfers between devices  27.9 us (27%)
  Pallas kernels  9.72 us (9%)
  local copies, waits for them, and re-layouts  1.62 us (2%)
  between operations  1.53 us (1%)
    all_to_all x1, starting transfers between devices, body(): spread = lax.all_to_all(summed.reshape(n_yx, chunk, side), ('y', 'x'), 0, 0)  18.8 us
    ppermute x1, starting transfers between devices, body(): column = lax.ppermute(column, ROW, pairs)  12 us
    all_to_all x1, waiting for transfers between devices, body(): spread = lax.all_to_all(summed.reshape(n_yx, chunk, side), ('y', 'x'), 0, 0)  8.39 us
    all_to_all x1, waiting for transfers between devices, body(): part = lax.all_to_all(part, ('zh', 'zl'), 0, 0)  6.18 us
    ppermute x1, starting transfers between devices, body(): facing = lax.ppermute(whole, 'core', swap)  5.87 us
    all_to_all x1, waiting for transfers between devices, body(): whole = lax.all_to_all(part, ('y', 'x'), 0, 0)  5.51 us
    all_to_all x1, starting transfers between devices, body(): whole = lax.all_to_all(part, ('y', 'x'), 0, 0)  4.37 us
    pallas_call x1, Pallas kernels, body(): call(main_kernel, [shape(modes * side, side), shape(modes * side + strip...  3.74 us
  transfers between devices with their start and end apart: 14, of which 8 were waited for; matrix products, arithmetic and copies ran while one was open for 0% of the time, Pallas kernels for 4%

profile of v6, /device:TPU:1, one launch (start us, length us, event | category | flops | bytes accessed | tf_op | source)
XLA Modules:
  0.0 104.7 jit_solution(15621415784344483598)
XLA Ops:
  1.3 0.9 copy-done.2
  2.4 12.0 %collective-permute-start = (f32[136,128]{1,0:T(8,128)S(1)}, f32[136,128]{1,0:T(8,128)S(1)}, u32[]{:S(2)}, u32[]{:S(2)}) collective-permute-start(f32[136,128]{1,0:T(8,128)S(1)} %get-tuple-element.26), channel_id=1, source_target_pairs={{16,32},{48,64},{80,96},{112,128},{144,160},{176,192},{208,224},{2... | collective-permute-start | bytes 208904 | tf_op jit(solution)/shard_map/ppermute | solution.py:392
  14.4 3.1 %collective-permute-start.1 = (f32[2,64,128]{2,1,0:T(8,128)S(1)}, f32[2,64,128]{2,1,0:T(8,128)S(1)}, u32[]{:S(2)}, u32[]{:S(2)}) collective-permute-start(f32[2,64,128]{2,1,0:T(8,128)S(1)} %get-tuple-element.27), channel_id=1, source_target_pairs={{0,1},{2,3},{4,5},{6,7},{8,9},{10,11},{12,13},{14,15},{1,0},{3,2},... | collective-permute-start | bytes 196616 | tf_op jit(solution)/shard_map/ppermute | solution.py:393
  18.2 2.1 %collective-permute-start.3 = (f32[8,128]{1,0:T(8,128)S(1)}, f32[8,128]{1,0:T(8,128)S(1)}, u32[]{:S(2)}, u32[]{:S(2)}) collective-permute-start(f32[8,128]{1,0:T(8,128)S(1)} %get-tuple-element.30), channel_id=1, source_target_pairs={{0,16},{16,0},{1,17},{17,1},{2,18},{18,2},{3,19},{19,3},{4,20},{20... | collective-permute-start | bytes 12296 | tf_op jit(solution)/shard_map/ppermute | solution.py:395
  21.0 3.5 %collective-permute-start.5 = (f32[264,128]{1,0:T(8,128)S(1)}, f32[264,128]{1,0:T(8,128)S(1)}, u32[]{:S(2)}, u32[]{:S(2)}) collective-permute-start(f32[264,128]{1,0:T(8,128)S(1)} %get-tuple-element.31), channel_id=1, source_target_pairs={{16,32},{48,64},{80,96},{112,128},{144,160},{176,192},{208,224},{2... | collective-permute-start | bytes 405512 | tf_op jit(solution)/shard_map/ppermute | solution.py:399
  24.8 1.9 %collective-permute-start.4 = (f32[256,128]{1,0:T(8,128)S(1)}, f32[256,128]{1,0:T(8,128)S(1)}, u32[]{:S(2)}, u32[]{:S(2)}) collective-permute-start(f32[256,128]{1,0:T(8,128)S(1)} %shard_map.80), channel_id=1, source_target_pairs={{0,16},{16,0},{1,17},{17,1},{2,18},{18,2},{3,19},{19,3},{4,20},{20... | collective-permute-start | bytes 393224 | tf_op jit(solution)/shard_map/ppermute | solution.py:401
  28.1 3.3 %collective-permute-done.5.beyond = f32[264,128]{1,0:T(8,128)S(1)} collective-permute-done((f32[264,128]{1,0:T(8,128)S(1)}, f32[264,128]{1,0:T(8,128)S(1)}, u32[]{:S(2)}, u32[]{:S(2)}) %collective-permute-start.5) | collective-permute-done | bytes 135200 | tf_op jit(solution)/shard_map/ppermute | solution.py:399
  31.4 3.7 %shard_map.81 = (f32[512,128]{1,0:T(8,128)S(1)}, f32[776,128]{1,0:T(8,128)S(1)}, f32[264,128]{1,0:T(8,128)S(1)}, f32[256,128]{1,0:T(8,128)S(1)}) custom-call(s32[2]{0:T(128)S(1)} %bitcast.10, s32[1]{0:T(128)} %bitcast.5.live, f32[256,128]{1,0:T(8,128)S(1)} %shard_map.79.near, f32[256,128]{1,0:T(8,128)S(1)} %collective-permute-done.4.other, ...), custom_call_target="tpu_custom_call" | custom-call | tf_op jit(solution)/shard_map/pallas_call | solution.py:409
  35.1 1.9 %collective-permute-start.6 = (f32[776,128]{1,0:T(8,128)S(1)}, f32[776,128]{1,0:T(8,128)S(1)}, u32[]{:S(2)}, u32[]{:S(2)}) collective-permute-start(f32[776,128]{1,0:T(8,128)S(1)} %get-tuple-element.36), channel_id=1, source_target_pairs={{0,16},{16,0},{1,17},{17,1},{2,18},{18,2},{3,19},{19,3},{4,20},{20... | collective-permute-start | bytes 1191944 | tf_op jit(solution)/shard_map/ppermute | solution.py:422
  37.1 1.7 %collective-permute-done.6.from_core.message = f32[776,128]{1,0:T(8,128)S(1)} collective-permute-done((f32[776,128]{1,0:T(8,128)S(1)}, f32[776,128]{1,0:T(8,128)S(1)}, u32[]{:S(2)}, u32[]{:S(2)}) %collective-permute-start.6) | collective-permute-done | bytes 397344 | tf_op jit(solution)/shard_map/ppermute | solution.py:422
  38.8 0.7 shard_map.83
  39.5 18.8 %all-to-all-start = ((f32[32,16,128]{2,1,0:T(8,128)}), f32[32,16,128]{2,1,0:T(8,128)S(1)}, u32[]{:S(2)}, u32[]{:S(2)}) async-start(f32[32,16,128]{2,1,0:T(8,128)} %bitcast.3), calls=%async_computation | async-start | bytes 524288 | tf_op jit(solution)/shard_map/all_to_all | solution.py:430
  58.3 3.4 %collective-permute-start.7 = (f32[264,128]{1,0:T(8,128)S(1)}, f32[264,128]{1,0:T(8,128)S(1)}, u32[]{:S(2)}, u32[]{:S(2)}) collective-permute-start(f32[264,128]{1,0:T(8,128)S(1)} %get-tuple-element.37), channel_id=1, source_target_pairs={{16,32},{48,64},{80,96},{112,128},{144,160},{176,192},{208,224},{2... | collective-permute-start | bytes 405512 | tf_op jit(solution)/shard_map/ppermute | solution.py:423
  61.7 8.4 %all-to-all-done.parts = f32[32,16,128]{2,1,0:T(8,128)S(1)} async-done(((f32[32,16,128]{2,1,0:T(8,128)}), f32[32,16,128]{2,1,0:T(8,128)S(1)}, u32[]{:S(2)}, u32[]{:S(2)}) %all-to-all-start) | async-done | bytes 262176 | tf_op jit(solution)/shard_map/all_to_all | solution.py:430
  70.8 3.4 %all-to-all-start.1 = ((f32[8,16,128]{2,1,0:T(8,128)}), f32[8,16,128]{2,1,0:T(8,128)S(1)}, u32[]{:S(2)}, u32[]{:S(2)}) async-start(f32[8,16,128]{2,1,0:T(8,128)} %shard_map.84), calls=%async_computation.1 | async-start | bytes 131072 | tf_op jit(solution)/shard_map/all_to_all | solution.py:440
  74.2 1.0 shard_map.82
  75.1 6.2 %all-to-all-done.1.parts = f32[8,16,128]{2,1,0:T(8,128)S(1)} async-done(((f32[8,16,128]{2,1,0:T(8,128)}), f32[8,16,128]{2,1,0:T(8,128)S(1)}, u32[]{:S(2)}, u32[]{:S(2)}) %all-to-all-start.1) | async-done | bytes 65568 | tf_op jit(solution)/shard_map/all_to_all | solution.py:440
  81.3 0.7 shard_map.85
  82.0 4.4 %all-to-all-start.2 = ((f32[32,16,128]{2,1,0:T(8,128)}), f32[32,16,128]{2,1,0:T(8,128)S(1)}, u32[]{:S(2)}, u32[]{:S(2)}) async-start(f32[32,16,128]{2,1,0:T(8,128)} %shard_map.85), calls=%async_computation.2 | async-start | bytes 524288 | tf_op jit(solution)/shard_map/all_to_all | solution.py:445
  86.4 2.2 %collective-permute-start.8 = (f32[2,64,128]{2,1,0:T(8,128)S(1)}, f32[2,64,128]{2,1,0:T(8,128)S(1)}, u32[]{:S(2)}, u32[]{:S(2)}) collective-permute-start(f32[2,64,128]{2,1,0:T(8,128)S(1)} %get-tuple-element.43), channel_id=1, source_target_pairs={{0,1},{2,3},{4,5},{6,7},{8,9},{10,11},{12,13},{14,15},{1,0},{3,2},... | collective-permute-start | bytes 196616 | tf_op jit(solution)/shard_map/ppermute | solution.py:443
  89.3 2.1 %collective-permute-done.8.with_even = f32[2,64,128]{2,1,0:T(8,128)S(1)} collective-permute-done((f32[2,64,128]{2,1,0:T(8,128)S(1)}, f32[2,64,128]{2,1,0:T(8,128)S(1)}, u32[]{:S(2)}, u32[]{:S(2)}) %collective-permute-start.8) | collective-permute-done | bytes 65568 | tf_op jit(solution)/shard_map/ppermute | solution.py:443
  91.4 5.5 %all-to-all-done.2 = f32[32,16,128]{2,1,0:T(8,128)S(1)} async-done(((f32[32,16,128]{2,1,0:T(8,128)}), f32[32,16,128]{2,1,0:T(8,128)S(1)}, u32[]{:S(2)}, u32[]{:S(2)}) %all-to-all-start.2) | async-done | bytes 262176 | tf_op jit(solution)/shard_map/all_to_all | solution.py:445
  96.9 5.9 %collective-permute-start.10 = (f32[4,128,128]{2,1,0:T(8,128)S(1)}, f32[4,128,128]{2,1,0:T(8,128)S(1)}, u32[]{:S(2)}, u32[]{:S(2)}) collective-permute-start(f32[4,128,128]{2,1,0:T(8,128)S(1)} %bitcast.6), channel_id=1, source_target_pairs={{0,16},{16,0},{1,17},{17,1},{2,18},{18,2},{3,19},{19,3},{4,20},{20... | collective-permute-start | bytes 786440 | tf_op jit(solution)/shard_map/ppermute | solution.py:448
  102.8 0.8 shard_map.86
  (27 shorter events, 5.5 us)
Async XLA Ops:
  0.6 0.7 copy-start.5
  1.3 0.9 copy-start.2
  2.2 18.5 %copy-start.3 = (f32[2,2,64,256]{3,2,1,0:T(8,128)S(1)}, f32[2,2,64,256]{3,2,1,0:T(8,128)}, u32[]{:S(2)}) copy-start(f32[2,2,64,256]{3,2,1,0:T(8,128)} %own.3) | copy-start | bytes 786436
  2.4 18.4 %collective-permute-start = (f32[136,128]{1,0:T(8,128)S(1)}, f32[136,128]{1,0:T(8,128)S(1)}, u32[]{:S(2)}, u32[]{:S(2)}) collective-permute-start(f32[136,128]{1,0:T(8,128)S(1)} %get-tuple-element.26), channel_id=1, source_target_pairs={{16,32},{48,64},{80,96},{112,128},{144,160},{176,192},{208,224},{2... | collective-permute-start | bytes 208904 | tf_op jit(solution)/shard_map/ppermute | solution.py:392
  14.4 6.3 %collective-permute-start.1 = (f32[2,64,128]{2,1,0:T(8,128)S(1)}, f32[2,64,128]{2,1,0:T(8,128)S(1)}, u32[]{:S(2)}, u32[]{:S(2)}) collective-permute-start(f32[2,64,128]{2,1,0:T(8,128)S(1)} %get-tuple-element.27), channel_id=1, source_target_pairs={{0,1},{2,3},{4,5},{6,7},{8,9},{10,11},{12,13},{14,15},{1,0},{3,2},... | collective-permute-start | bytes 196616 | tf_op jit(solution)/shard_map/ppermute | solution.py:393
  17.5 3.2 %collective-permute-start.2 = (f32[2,64,128]{2,1,0:T(8,128)S(1)}, f32[2,64,128]{2,1,0:T(8,128)S(1)}, u32[]{:S(2)}, u32[]{:S(2)}) collective-permute-start(f32[2,64,128]{2,1,0:T(8,128)S(1)} %get-tuple-element.28), channel_id=1, source_target_pairs={{1,2},{3,4},{5,6},{7,8},{9,10},{11,12},{13,14},{2,1},{4,3},{6,5},{... | collective-permute-start | bytes 196616 | tf_op jit(solution)/shard_map/ppermute | solution.py:394
  18.2 9.2 %copy-start = (f32[2,4,128,128]{3,2,1,0:T(8,128)S(1)}, f32[2,4,128,128]{3,2,1,0:T(8,128)}, u32[]{:S(2)}) copy-start(f32[2,4,128,128]{3,2,1,0:T(8,128)} %probe.3) | copy-start | bytes 1572868
  18.2 6.3 %collective-permute-start.3 = (f32[8,128]{1,0:T(8,128)S(1)}, f32[8,128]{1,0:T(8,128)S(1)}, u32[]{:S(2)}, u32[]{:S(2)}) collective-permute-start(f32[8,128]{1,0:T(8,128)S(1)} %get-tuple-element.30), channel_id=1, source_target_pairs={{0,16},{16,0},{1,17},{17,1},{2,18},{18,2},{3,19},{19,3},{4,20},{20... | collective-permute-start | bytes 12296 | tf_op jit(solution)/shard_map/ppermute | solution.py:395
  21.0 6.4 %copy-start.1 = (bf16[12,128,128]{2,1,0:T(8,128)(2,1)S(1)}, bf16[12,128,128]{2,1,0:T(8,128)(2,1)}, u32[]{:S(2)}) copy-start(bf16[12,128,128]{2,1,0:T(8,128)(2,1)} %constant.2.clone.tabs) | copy-start | bytes 1179652
  21.0 10.4 %collective-permute-start.5 = (f32[264,128]{1,0:T(8,128)S(1)}, f32[264,128]{1,0:T(8,128)S(1)}, u32[]{:S(2)}, u32[]{:S(2)}) collective-permute-start(f32[264,128]{1,0:T(8,128)S(1)} %get-tuple-element.31), channel_id=1, source_target_pairs={{16,32},{48,64},{80,96},{112,128},{144,160},{176,192},{208,224},{2... | collective-permute-start | bytes 405512 | tf_op jit(solution)/shard_map/ppermute | solution.py:399
  24.5 2.9 %copy-start.4 = (f32[1,1,1,128,128]{4,3,2,1,0:T(8,128)S(1)}, f32[1,1,1,128,128]{4,3,2,1,0:T(8,128)}, u32[]{:S(2)}) copy-start(f32[1,1,1,128,128]{4,3,2,1,0:T(8,128)} %pattern.3) | copy-start | bytes 196612
  24.8 3.3 %collective-permute-start.4 = (f32[256,128]{1,0:T(8,128)S(1)}, f32[256,128]{1,0:T(8,128)S(1)}, u32[]{:S(2)}, u32[]{:S(2)}) collective-permute-start(f32[256,128]{1,0:T(8,128)S(1)} %shard_map.80), channel_id=1, source_target_pairs={{0,16},{16,0},{1,17},{17,1},{2,18},{18,2},{3,19},{19,3},{4,20},{20... | collective-permute-start | bytes 393224 | tf_op jit(solution)/shard_map/ppermute | solution.py:401
  35.1 3.6 %collective-permute-start.6 = (f32[776,128]{1,0:T(8,128)S(1)}, f32[776,128]{1,0:T(8,128)S(1)}, u32[]{:S(2)}, u32[]{:S(2)}) collective-permute-start(f32[776,128]{1,0:T(8,128)S(1)} %get-tuple-element.36), channel_id=1, source_target_pairs={{0,16},{16,0},{1,17},{17,1},{2,18},{18,2},{3,19},{19,3},{4,20},{20... | collective-permute-start | bytes 1191944 | tf_op jit(solution)/shard_map/ppermute | solution.py:422
  39.5 30.6 %all-to-all-start = ((f32[32,16,128]{2,1,0:T(8,128)}), f32[32,16,128]{2,1,0:T(8,128)S(1)}, u32[]{:S(2)}, u32[]{:S(2)}) async-start(f32[32,16,128]{2,1,0:T(8,128)} %bitcast.3), calls=%async_computation | async-start | bytes 524288 | tf_op jit(solution)/shard_map/all_to_all | solution.py:430
  58.3 15.9 %collective-permute-start.7 = (f32[264,128]{1,0:T(8,128)S(1)}, f32[264,128]{1,0:T(8,128)S(1)}, u32[]{:S(2)}, u32[]{:S(2)}) collective-permute-start(f32[264,128]{1,0:T(8,128)S(1)} %get-tuple-element.37), channel_id=1, source_target_pairs={{16,32},{48,64},{80,96},{112,128},{144,160},{176,192},{208,224},{2... | collective-permute-start | bytes 405512 | tf_op jit(solution)/shard_map/ppermute | solution.py:423
  70.8 10.5 %all-to-all-start.1 = ((f32[8,16,128]{2,1,0:T(8,128)}), f32[8,16,128]{2,1,0:T(8,128)S(1)}, u32[]{:S(2)}, u32[]{:S(2)}) async-start(f32[8,16,128]{2,1,0:T(8,128)} %shard_map.84), calls=%async_computation.1 | async-start | bytes 131072 | tf_op jit(solution)/shard_map/all_to_all | solution.py:440
  82.0 14.9 %all-to-all-start.2 = ((f32[32,16,128]{2,1,0:T(8,128)}), f32[32,16,128]{2,1,0:T(8,128)S(1)}, u32[]{:S(2)}, u32[]{:S(2)}) async-start(f32[32,16,128]{2,1,0:T(8,128)} %shard_map.85), calls=%async_computation.2 | async-start | bytes 524288 | tf_op jit(solution)/shard_map/all_to_all | solution.py:445
  86.4 5.0 %collective-permute-start.8 = (f32[2,64,128]{2,1,0:T(8,128)S(1)}, f32[2,64,128]{2,1,0:T(8,128)S(1)}, u32[]{:S(2)}, u32[]{:S(2)}) collective-permute-start(f32[2,64,128]{2,1,0:T(8,128)S(1)} %get-tuple-element.43), channel_id=1, source_target_pairs={{0,1},{2,3},{4,5},{6,7},{8,9},{10,11},{12,13},{14,15},{1,0},{3,2},... | collective-permute-start | bytes 196616 | tf_op jit(solution)/shard_map/ppermute | solution.py:443
  88.6 2.8 %collective-permute-start.9 = (f32[2,64,128]{2,1,0:T(8,128)S(1)}, f32[2,64,128]{2,1,0:T(8,128)S(1)}, u32[]{:S(2)}, u32[]{:S(2)}) collective-permute-start(f32[2,64,128]{2,1,0:T(8,128)S(1)} %get-tuple-element.44), channel_id=1, source_target_pairs={{1,2},{3,4},{5,6},{7,8},{9,10},{11,12},{13,14},{2,1},{4,3},{6,5},{... | collective-permute-start | bytes 196616 | tf_op jit(solution)/shard_map/ppermute | solution.py:444
  96.9 7.0 %collective-permute-start.10 = (f32[4,128,128]{2,1,0:T(8,128)S(1)}, f32[4,128,128]{2,1,0:T(8,128)S(1)}, u32[]{:S(2)}, u32[]{:S(2)}) collective-permute-start(f32[4,128,128]{2,1,0:T(8,128)S(1)} %bitcast.6), channel_id=1, source_target_pairs={{0,16},{16,0},{1,17},{17,1},{2,18},{18,2},{3,19},{19,3},{4,20},{20... | collective-permute-start | bytes 786440 | tf_op jit(solution)/shard_map/ppermute | solution.py:448

commit v7 on v6

--- a/solution.py
+++ b/solution.py
@@ -169,7 +169,14 @@
     return pltpu.roll(wide, lax.rem(2 * side - step, 2 * side), 1)[:, :side]
 
 
-def edges_kernel(scan, own, with_even, with_odd, column, column_near):
+def column_kernel(scan, column, column_near):
+    half = column.shape[1] // 2
+    col = (scan[:, 1:2] - (lax.axis_index(COL) * TILE_COLS - half)).astype(jnp.float32)
+    column[...] = jnp.broadcast_to(col, column.shape)
+    column_near[...] = jnp.broadcast_to(col, column_near.shape)
+
+
+def edges_kernel(own, with_even, with_odd):
     rows, cols = own.shape[2], own.shape[3]
     side = with_even.shape[2]
     half = side // 2
@@ -180,9 +187,6 @@
         right = jnp.where(inner, pltpu.roll(imaginary[:, cols - side :], half, 1), real[:, cols - side :])
         with_even[layer] = jnp.where(even_col(), right, left)
         with_odd[layer] = jnp.where(even_col(), left, right)
-    col = (scan[:, 1:2] - (lax.axis_index(COL) * cols - half)).astype(jnp.float32)
-    column[...] = jnp.broadcast_to(col, column.shape)
-    column_near[...] = jnp.broadcast_to(col, column_near.shape)
 
 
 def partner_column(column, cols):
@@ -386,9 +390,10 @@
         return jax.ShapeDtypeStruct(dims, f32)
 
     edge = shape(2, rows, side)
-    to_even, to_odd, column, column_near = call(
-        edges_kernel, [edge, edge, shape(136, side), shape(8, side)], 0, 2
-    )(scan.reshape(1, 2), obj_field)
+    column, column_near = call(column_kernel, [shape(136, side), shape(8, side)], 0, 1)(
+        scan.reshape(1, 2)
+    )
+    to_even, to_odd = call(edges_kernel, [edge, edge], 0, 1)(obj_field)
     column = lax.ppermute(column, ROW, pairs)
     with_even = lax.ppermute(to_even, COL, even_pairs)
     with_odd = lax.ppermute(to_odd, COL, odd_pairs)
@@ -439,8 +444,8 @@
     part = call(sum_kernel, shape(n_z, chunk, side), 0, 1)(spread)
     part = lax.all_to_all(part, ("zh", "zl"), 0, 0)
     part = call(sum_kernel, shape(n_yx, chunk, side), 0, 1)(part)
-    part, grad_even, grad_odd = lax.optimization_barrier((part, grad_even, grad_odd))
     got_even = lax.ppermute(grad_even, COL, even_pairs)
+    part, got_even, grad_odd = lax.optimization_barrier((part, got_even, grad_odd))
     got_odd = lax.ppermute(grad_odd, COL, odd_pairs)
     whole = lax.all_to_all(part, ("y", "x"), 0, 0)
     whole, got_even, got_odd = lax.optimization_barrier((whole, got_even, got_odd))

time: 105 us -> 105 us (level)
    all_to_all x1, waiting for transfers between devices: 5.51 us -> 9.72 us  [body(): whole = lax.all_to_all(part, ('y', 'x'), 0, 0)]
    all_to_all x1, waiting for transfers between devices: 6.18 us -> 2.91 us  [body(): part = lax.all_to_all(part, ('zh', 'zl'), 0, 0)]
    ppermute x1, waiting for transfers between devices: 2.14 us -> 0.01 us  [body(): got_even = lax.ppermute(grad_even, COL, even_pairs)]
    ppermute x1, starting transfers between devices: 2.19 us -> 3.26 us  [body(): got_even = lax.ppermute(grad_even, COL, even_pairs)]
  transfers between devices with their start and end apart: 14 -> 14, of which waited for: 8 -> 6; matrix products, arithmetic and copies ran while one was open for 0% -> 0% of each run, Pallas kernels for 4% -> 4%
where the time goes in v7:
time: 105 us; the launch traced here: 104 us
  starting transfers between devices  64.1 us (61%)
  waiting for transfers between devices  27.3 us (26%)
  Pallas kernels  9.79 us (9%)
  local copies, waits for them, and re-layouts  1.61 us (2%)
  between operations  1.56 us (1%)
    all_to_all x1, starting transfers between devices, body(): spread = lax.all_to_all(summed.reshape(n_yx, chunk, side), ('y', 'x'), 0, 0)  18.6 us
    ppermute x1, starting transfers between devices, body(): column = lax.ppermute(column, ROW, pairs)  12 us
    all_to_all x1, waiting for transfers between devices, body(): whole = lax.all_to_all(part, ('y', 'x'), 0, 0)  9.72 us
    all_to_all x1, waiting for transfers between devices, body(): spread = lax.all_to_all(summed.reshape(n_yx, chunk, side), ('y', 'x'), 0, 0)  8.72 us
    ppermute x1, starting transfers between devices, body(): facing = lax.ppermute(whole, 'core', swap)  5.65 us
    all_to_all x1, starting transfers between devices, body(): whole = lax.all_to_all(part, ('y', 'x'), 0, 0)  5.27 us
    ppermute x1, waiting for transfers between devices, body(): beyond = lax.ppermute(to_beyond, ROW, pairs)  3.96 us
    pallas_call x1, Pallas kernels, body(): call(main_kernel, [shape(modes * side, side), shape(modes * side + strip...  3.75 us
  transfers between devices with their start and end apart: 14, of which 6 were waited for; matrix products, arithmetic and copies ran while one was open for 0% of the time, Pallas kernels for 4%

profile of v7, /device:TPU:1, one launch (start us, length us, event | category | flops | bytes accessed | tf_op | source)
XLA Modules:
  0.0 104.4 jit_solution(15819921654947468289)
XLA Ops:
  1.4 12.0 %collective-permute-start = (f32[136,128]{1,0:T(8,128)S(1)}, f32[136,128]{1,0:T(8,128)S(1)}, u32[]{:S(2)}, u32[]{:S(2)}) collective-permute-start(f32[136,128]{1,0:T(8,128)S(1)} %get-tuple-element.26), channel_id=1, source_target_pairs={{16,32},{48,64},{80,96},{112,128},{144,160},{176,192},{208,224},{2... | collective-permute-start | bytes 208904 | tf_op jit(solution)/shard_map/ppermute | solution.py:397
  13.4 0.9 copy-done.2
  14.4 3.1 %collective-permute-start.1 = (f32[2,64,128]{2,1,0:T(8,128)S(1)}, f32[2,64,128]{2,1,0:T(8,128)S(1)}, u32[]{:S(2)}, u32[]{:S(2)}) collective-permute-start(f32[2,64,128]{2,1,0:T(8,128)S(1)} %get-tuple-element.27), channel_id=1, source_target_pairs={{0,1},{2,3},{4,5},{6,7},{8,9},{10,11},{12,13},{14,15},{1,0},{3,2},... | collective-permute-start | bytes 196616 | tf_op jit(solution)/shard_map/ppermute | solution.py:398
  18.2 2.1 %collective-permute-start.3 = (f32[8,128]{1,0:T(8,128)S(1)}, f32[8,128]{1,0:T(8,128)S(1)}, u32[]{:S(2)}, u32[]{:S(2)}) collective-permute-start(f32[8,128]{1,0:T(8,128)S(1)} %get-tuple-element.30), channel_id=1, source_target_pairs={{0,16},{16,0},{1,17},{17,1},{2,18},{18,2},{3,19},{19,3},{4,20},{20... | collective-permute-start | bytes 12296 | tf_op jit(solution)/shard_map/ppermute | solution.py:400
  20.6 2.8 %collective-permute-start.5 = (f32[264,128]{1,0:T(8,128)S(1)}, f32[264,128]{1,0:T(8,128)S(1)}, u32[]{:S(2)}, u32[]{:S(2)}) collective-permute-start(f32[264,128]{1,0:T(8,128)S(1)} %get-tuple-element.31), channel_id=1, source_target_pairs={{16,32},{48,64},{80,96},{112,128},{144,160},{176,192},{208,224},{2... | collective-permute-start | bytes 405512 | tf_op jit(solution)/shard_map/ppermute | solution.py:404
  23.7 1.9 %collective-permute-start.4 = (f32[256,128]{1,0:T(8,128)S(1)}, f32[256,128]{1,0:T(8,128)S(1)}, u32[]{:S(2)}, u32[]{:S(2)}) collective-permute-start(f32[256,128]{1,0:T(8,128)S(1)} %shard_map.81), channel_id=1, source_target_pairs={{0,16},{16,0},{1,17},{17,1},{2,18},{18,2},{3,19},{19,3},{4,20},{20... | collective-permute-start | bytes 393224 | tf_op jit(solution)/shard_map/ppermute | solution.py:406
  27.0 4.0 %collective-permute-done.5.beyond = f32[264,128]{1,0:T(8,128)S(1)} collective-permute-done((f32[264,128]{1,0:T(8,128)S(1)}, f32[264,128]{1,0:T(8,128)S(1)}, u32[]{:S(2)}, u32[]{:S(2)}) %collective-permute-start.5) | collective-permute-done | bytes 135200 | tf_op jit(solution)/shard_map/ppermute | solution.py:404
  31.0 3.7 %shard_map.82 = (f32[512,128]{1,0:T(8,128)S(1)}, f32[776,128]{1,0:T(8,128)S(1)}, f32[264,128]{1,0:T(8,128)S(1)}, f32[256,128]{1,0:T(8,128)S(1)}) custom-call(s32[2]{0:T(128)S(1)} %bitcast.10, s32[1]{0:T(128)} %bitcast.5.live, f32[256,128]{1,0:T(8,128)S(1)} %shard_map.80.near, f32[256,128]{1,0:T(8,128)S(1)} %collective-permute-done.4.other, ...), custom_call_target="tpu_custom_call" | custom-call | tf_op jit(solution)/shard_map/pallas_call | solution.py:414
  34.8 1.9 %collective-permute-start.6 = (f32[776,128]{1,0:T(8,128)S(1)}, f32[776,128]{1,0:T(8,128)S(1)}, u32[]{:S(2)}, u32[]{:S(2)}) collective-permute-start(f32[776,128]{1,0:T(8,128)S(1)} %get-tuple-element.36), channel_id=1, source_target_pairs={{0,16},{16,0},{1,17},{17,1},{2,18},{18,2},{3,19},{19,3},{4,20},{20... | collective-permute-start | bytes 1191944 | tf_op jit(solution)/shard_map/ppermute | solution.py:427
  36.7 1.7 %collective-permute-done.6.from_core.message = f32[776,128]{1,0:T(8,128)S(1)} collective-permute-done((f32[776,128]{1,0:T(8,128)S(1)}, f32[776,128]{1,0:T(8,128)S(1)}, u32[]{:S(2)}, u32[]{:S(2)}) %collective-permute-start.6) | collective-permute-done | bytes 397344 | tf_op jit(solution)/shard_map/ppermute | solution.py:427
  38.4 0.7 shard_map.84
  39.1 18.6 %all-to-all-start = ((f32[32,16,128]{2,1,0:T(8,128)}), f32[32,16,128]{2,1,0:T(8,128)S(1)}, u32[]{:S(2)}, u32[]{:S(2)}) async-start(f32[32,16,128]{2,1,0:T(8,128)} %bitcast.3), calls=%async_computation | async-start | bytes 524288 | tf_op jit(solution)/shard_map/all_to_all | solution.py:435
  57.7 2.9 %collective-permute-start.7 = (f32[264,128]{1,0:T(8,128)S(1)}, f32[264,128]{1,0:T(8,128)S(1)}, u32[]{:S(2)}, u32[]{:S(2)}) collective-permute-start(f32[264,128]{1,0:T(8,128)S(1)} %get-tuple-element.37), channel_id=1, source_target_pairs={{16,32},{48,64},{80,96},{112,128},{144,160},{176,192},{208,224},{2... | collective-permute-start | bytes 405512 | tf_op jit(solution)/shard_map/ppermute | solution.py:428
  60.6 8.7 %all-to-all-done.parts = f32[32,16,128]{2,1,0:T(8,128)S(1)} async-done(((f32[32,16,128]{2,1,0:T(8,128)}), f32[32,16,128]{2,1,0:T(8,128)S(1)}, u32[]{:S(2)}, u32[]{:S(2)}) %all-to-all-start) | async-done | bytes 262176 | tf_op jit(solution)/shard_map/all_to_all | solution.py:435
  70.0 3.4 %all-to-all-start.1 = ((f32[8,16,128]{2,1,0:T(8,128)}), f32[8,16,128]{2,1,0:T(8,128)S(1)}, u32[]{:S(2)}, u32[]{:S(2)}) async-start(f32[8,16,128]{2,1,0:T(8,128)} %shard_map.85), calls=%async_computation.1 | async-start | bytes 131072 | tf_op jit(solution)/shard_map/all_to_all | solution.py:445
  73.4 0.9 shard_map.83
  74.3 3.3 %collective-permute-start.8 = (f32[2,64,128]{2,1,0:T(8,128)S(1)}, f32[2,64,128]{2,1,0:T(8,128)S(1)}, u32[]{:S(2)}, u32[]{:S(2)}) collective-permute-start(f32[2,64,128]{2,1,0:T(8,128)S(1)} %get-tuple-element.40), channel_id=1, source_target_pairs={{0,1},{2,3},{4,5},{6,7},{8,9},{10,11},{12,13},{14,15},{1,0},{3,2},... | collective-permute-start | bytes 196616 | tf_op jit(solution)/shard_map/ppermute | solution.py:447
  77.6 2.9 %all-to-all-done.1.parts = f32[8,16,128]{2,1,0:T(8,128)S(1)} async-done(((f32[8,16,128]{2,1,0:T(8,128)}), f32[8,16,128]{2,1,0:T(8,128)S(1)}, u32[]{:S(2)}, u32[]{:S(2)}) %all-to-all-start.1) | async-done | bytes 65568 | tf_op jit(solution)/shard_map/all_to_all | solution.py:445
  80.5 0.7 shard_map.86
  81.2 5.3 %all-to-all-start.2 = ((f32[32,16,128]{2,1,0:T(8,128)}), f32[32,16,128]{2,1,0:T(8,128)S(1)}, u32[]{:S(2)}, u32[]{:S(2)}) async-start(f32[32,16,128]{2,1,0:T(8,128)} %shard_map.86), calls=%async_computation.2 | async-start | bytes 524288 | tf_op jit(solution)/shard_map/all_to_all | solution.py:450
  87.2 9.7 %all-to-all-done.2 = f32[32,16,128]{2,1,0:T(8,128)S(1)} async-done(((f32[32,16,128]{2,1,0:T(8,128)}), f32[32,16,128]{2,1,0:T(8,128)S(1)}, u32[]{:S(2)}, u32[]{:S(2)}) %all-to-all-start.2) | async-done | bytes 262176 | tf_op jit(solution)/shard_map/all_to_all | solution.py:450
  96.9 5.7 %collective-permute-start.10 = (f32[4,128,128]{2,1,0:T(8,128)S(1)}, f32[4,128,128]{2,1,0:T(8,128)S(1)}, u32[]{:S(2)}, u32[]{:S(2)}) collective-permute-start(f32[4,128,128]{2,1,0:T(8,128)S(1)} %bitcast.6), channel_id=1, source_target_pairs={{0,16},{16,0},{1,17},{17,1},{2,18},{18,2},{3,19},{19,3},{4,20},{20... | collective-permute-start | bytes 786440 | tf_op jit(solution)/shard_map/ppermute | solution.py:453
  102.6 0.8 shard_map.87
  103.7 0.7 shard_map.88
  (26 shorter events, 4.4 us)
Async XLA Ops:
  0.6 0.7 copy-start.4
  1.4 19.0 %collective-permute-start = (f32[136,128]{1,0:T(8,128)S(1)}, f32[136,128]{1,0:T(8,128)S(1)}, u32[]{:S(2)}, u32[]{:S(2)}) collective-permute-start(f32[136,128]{1,0:T(8,128)S(1)} %get-tuple-element.26), channel_id=1, source_target_pairs={{16,32},{48,64},{80,96},{112,128},{144,160},{176,192},{208,224},{2... | collective-permute-start | bytes 208904 | tf_op jit(solution)/shard_map/ppermute | solution.py:397
  13.4 1.0 copy-start.2
  14.4 5.9 %collective-permute-start.1 = (f32[2,64,128]{2,1,0:T(8,128)S(1)}, f32[2,64,128]{2,1,0:T(8,128)S(1)}, u32[]{:S(2)}, u32[]{:S(2)}) collective-permute-start(f32[2,64,128]{2,1,0:T(8,128)S(1)} %get-tuple-element.27), channel_id=1, source_target_pairs={{0,1},{2,3},{4,5},{6,7},{8,9},{10,11},{12,13},{14,15},{1,0},{3,2},... | collective-permute-start | bytes 196616 | tf_op jit(solution)/shard_map/ppermute | solution.py:398
  17.6 2.8 %collective-permute-start.2 = (f32[2,64,128]{2,1,0:T(8,128)S(1)}, f32[2,64,128]{2,1,0:T(8,128)S(1)}, u32[]{:S(2)}, u32[]{:S(2)}) collective-permute-start(f32[2,64,128]{2,1,0:T(8,128)S(1)} %get-tuple-element.28), channel_id=1, source_target_pairs={{1,2},{3,4},{5,6},{7,8},{9,10},{11,12},{13,14},{2,1},{4,3},{6,5},{... | collective-permute-start | bytes 196616 | tf_op jit(solution)/shard_map/ppermute | solution.py:399
  18.2 8.1 %copy-start = (f32[2,4,128,128]{3,2,1,0:T(8,128)S(1)}, f32[2,4,128,128]{3,2,1,0:T(8,128)}, u32[]{:S(2)}) copy-start(f32[2,4,128,128]{3,2,1,0:T(8,128)} %probe.3) | copy-start | bytes 1572868
  18.2 5.2 %collective-permute-start.3 = (f32[8,128]{1,0:T(8,128)S(1)}, f32[8,128]{1,0:T(8,128)S(1)}, u32[]{:S(2)}, u32[]{:S(2)}) collective-permute-start(f32[8,128]{1,0:T(8,128)S(1)} %get-tuple-element.30), channel_id=1, source_target_pairs={{0,16},{16,0},{1,17},{17,1},{2,18},{18,2},{3,19},{19,3},{4,20},{20... | collective-permute-start | bytes 12296 | tf_op jit(solution)/shard_map/ppermute | solution.py:400
  20.6 5.7 %copy-start.1 = (bf16[12,128,128]{2,1,0:T(8,128)(2,1)S(1)}, bf16[12,128,128]{2,1,0:T(8,128)(2,1)}, u32[]{:S(2)}) copy-start(bf16[12,128,128]{2,1,0:T(8,128)(2,1)} %constant.2.clone.tabs) | copy-start | bytes 1179652
  20.6 10.4 %collective-permute-start.5 = (f32[264,128]{1,0:T(8,128)S(1)}, f32[264,128]{1,0:T(8,128)S(1)}, u32[]{:S(2)}, u32[]{:S(2)}) collective-permute-start(f32[264,128]{1,0:T(8,128)S(1)} %get-tuple-element.31), channel_id=1, source_target_pairs={{16,32},{48,64},{80,96},{112,128},{144,160},{176,192},{208,224},{2... | collective-permute-start | bytes 405512 | tf_op jit(solution)/shard_map/ppermute | solution.py:404
  23.4 2.9 %copy-start.3 = (f32[1,1,1,128,128]{4,3,2,1,0:T(8,128)S(1)}, f32[1,1,1,128,128]{4,3,2,1,0:T(8,128)}, u32[]{:S(2)}) copy-start(f32[1,1,1,128,128]{4,3,2,1,0:T(8,128)} %pattern.3) | copy-start | bytes 196612
  23.7 3.3 %collective-permute-start.4 = (f32[256,128]{1,0:T(8,128)S(1)}, f32[256,128]{1,0:T(8,128)S(1)}, u32[]{:S(2)}, u32[]{:S(2)}) collective-permute-start(f32[256,128]{1,0:T(8,128)S(1)} %shard_map.81), channel_id=1, source_target_pairs={{0,16},{16,0},{1,17},{17,1},{2,18},{18,2},{3,19},{19,3},{4,20},{20... | collective-permute-start | bytes 393224 | tf_op jit(solution)/shard_map/ppermute | solution.py:406
  34.8 3.6 %collective-permute-start.6 = (f32[776,128]{1,0:T(8,128)S(1)}, f32[776,128]{1,0:T(8,128)S(1)}, u32[]{:S(2)}, u32[]{:S(2)}) collective-permute-start(f32[776,128]{1,0:T(8,128)S(1)} %get-tuple-element.36), channel_id=1, source_target_pairs={{0,16},{16,0},{1,17},{17,1},{2,18},{18,2},{3,19},{19,3},{4,20},{20... | collective-permute-start | bytes 1191944 | tf_op jit(solution)/shard_map/ppermute | solution.py:427
  39.1 30.2 %all-to-all-start = ((f32[32,16,128]{2,1,0:T(8,128)}), f32[32,16,128]{2,1,0:T(8,128)S(1)}, u32[]{:S(2)}, u32[]{:S(2)}) async-start(f32[32,16,128]{2,1,0:T(8,128)} %bitcast.3), calls=%async_computation | async-start | bytes 524288 | tf_op jit(solution)/shard_map/all_to_all | solution.py:435
  57.7 15.6 %collective-permute-start.7 = (f32[264,128]{1,0:T(8,128)S(1)}, f32[264,128]{1,0:T(8,128)S(1)}, u32[]{:S(2)}, u32[]{:S(2)}) collective-permute-start(f32[264,128]{1,0:T(8,128)S(1)} %get-tuple-element.37), channel_id=1, source_target_pairs={{16,32},{48,64},{80,96},{112,128},{144,160},{176,192},{208,224},{2... | collective-permute-start | bytes 405512 | tf_op jit(solution)/shard_map/ppermute | solution.py:428
  70.0 10.5 %all-to-all-start.1 = ((f32[8,16,128]{2,1,0:T(8,128)}), f32[8,16,128]{2,1,0:T(8,128)S(1)}, u32[]{:S(2)}, u32[]{:S(2)}) async-start(f32[8,16,128]{2,1,0:T(8,128)} %shard_map.85), calls=%async_computation.1 | async-start | bytes 131072 | tf_op jit(solution)/shard_map/all_to_all | solution.py:445
  74.3 6.9 %collective-permute-start.8 = (f32[2,64,128]{2,1,0:T(8,128)S(1)}, f32[2,64,128]{2,1,0:T(8,128)S(1)}, u32[]{:S(2)}, u32[]{:S(2)}) collective-permute-start(f32[2,64,128]{2,1,0:T(8,128)S(1)} %get-tuple-element.40), channel_id=1, source_target_pairs={{0,1},{2,3},{4,5},{6,7},{8,9},{10,11},{12,13},{14,15},{1,0},{3,2},... | collective-permute-start | bytes 196616 | tf_op jit(solution)/shard_map/ppermute | solution.py:447
  81.2 15.7 %all-to-all-start.2 = ((f32[32,16,128]{2,1,0:T(8,128)}), f32[32,16,128]{2,1,0:T(8,128)S(1)}, u32[]{:S(2)}, u32[]{:S(2)}) async-start(f32[32,16,128]{2,1,0:T(8,128)} %shard_map.86), calls=%async_computation.2 | async-start | bytes 524288 | tf_op jit(solution)/shard_map/all_to_all | solution.py:450
  86.5 0.7 collective-permute-start.9
  96.9 6.8 %collective-permute-start.10 = (f32[4,128,128]{2,1,0:T(8,128)S(1)}, f32[4,128,128]{2,1,0:T(8,128)S(1)}, u32[]{:S(2)}, u32[]{:S(2)}) collective-permute-start(f32[4,128,128]{2,1,0:T(8,128)S(1)} %bitcast.6), channel_id=1, source_target_pairs={{0,16},{16,0},{1,17},{17,1},{2,18},{18,2},{3,19},{19,3},{4,20},{20... | collective-permute-start | bytes 786440 | tf_op jit(solution)/shard_map/ppermute | solution.py:453

commit v8 on v7

--- a/solution.py
+++ b/solution.py
@@ -390,9 +390,10 @@
         return jax.ShapeDtypeStruct(dims, f32)
 
     edge = shape(2, rows, side)
-    column, column_near = call(column_kernel, [shape(136, side), shape(8, side)], 0, 1)(
-        scan.reshape(1, 2)
-    )
+    large = pl.CostEstimate(flops=4_000_000_000, bytes_accessed=0, transcendentals=0)
+    column, column_near = call(
+        column_kernel, [shape(136, side), shape(8, side)], 0, 1, cost=large
+    )(scan.reshape(1, 2))
     to_even, to_odd = call(edges_kernel, [edge, edge], 0, 1)(obj_field)
     column = lax.ppermute(column, ROW, pairs)
     with_even = lax.ppermute(to_even, COL, even_pairs)

time: 105 us -> 105 us (level)
  starting transfers between devices: 64.1 us -> 65.3 us
  transfers between devices with their start and end apart: 14 -> 14, of which waited for: 6 -> 7; matrix products, arithmetic and copies ran while one was open for 0% -> 0% of each run, Pallas kernels for 4% -> 4%
where the time goes in v8:
time: 105 us; the launch traced here: 104 us
  starting transfers between devices  65.3 us (62%)
  waiting for transfers between devices  27.1 us (26%)
  Pallas kernels  9.79 us (9%)
  between operations  1.54 us (1%)
    all_to_all x1, starting transfers between devices, body(): spread = lax.all_to_all(summed.reshape(n_yx, chunk, side), ('y', 'x'), 0, 0)  18.6 us
    ppermute x1, starting transfers between devices, body(): column = lax.ppermute(column, ROW, pairs)  12 us
    all_to_all x1, waiting for transfers between devices, body(): whole = lax.all_to_all(part, ('y', 'x'), 0, 0)  9.78 us
    all_to_all x1, waiting for transfers between devices, body(): spread = lax.all_to_all(summed.reshape(n_yx, chunk, side), ('y', 'x'), 0, 0)  8.35 us
    ppermute x1, starting transfers between devices, body(): facing = lax.ppermute(whole, 'core', swap)  5.6 us
    all_to_all x1, starting transfers between devices, body(): whole = lax.all_to_all(part, ('y', 'x'), 0, 0)  5.46 us
    pallas_call x1, Pallas kernels, body(): call(main_kernel, [shape(modes * side, side), shape(modes * side + strip...  3.75 us
    ppermute x1, waiting for transfers between devices, body(): beyond = lax.ppermute(to_beyond, ROW, pairs)  3.53 us
  transfers between devices with their start and end apart: 14, of which 7 were waited for; matrix products, arithmetic and copies ran while one was open for 0% of the time, Pallas kernels for 4%

profile of v8, /device:TPU:1, one launch (start us, length us, event | category | flops | bytes accessed | tf_op | source)
XLA Modules:
  0.0 104.5 jit_solution(17665539318720662135)
XLA Ops:
  1.4 12.0 %collective-permute-start = (f32[136,128]{1,0:T(8,128)S(1)}, f32[136,128]{1,0:T(8,128)S(1)}, u32[]{:S(2)}, u32[]{:S(2)}) collective-permute-start(f32[136,128]{1,0:T(8,128)S(1)} %get-tuple-element.26), channel_id=1, source_target_pairs={{16,32},{48,64},{80,96},{112,128},{144,160},{176,192},{208,224},{2... | collective-permute-start | bytes 208904 | tf_op jit(solution)/shard_map/ppermute | solution.py:398
  13.5 3.1 %collective-permute-start.1 = (f32[2,64,128]{2,1,0:T(8,128)S(1)}, f32[2,64,128]{2,1,0:T(8,128)S(1)}, u32[]{:S(2)}, u32[]{:S(2)}) collective-permute-start(f32[2,64,128]{2,1,0:T(8,128)S(1)} %get-tuple-element.27), channel_id=1, source_target_pairs={{0,1},{2,3},{4,5},{6,7},{8,9},{10,11},{12,13},{14,15},{1,0},{3,2},... | collective-permute-start | bytes 196616 | tf_op jit(solution)/shard_map/ppermute | solution.py:399
  17.3 2.1 %collective-permute-start.3 = (f32[8,128]{1,0:T(8,128)S(1)}, f32[8,128]{1,0:T(8,128)S(1)}, u32[]{:S(2)}, u32[]{:S(2)}) collective-permute-start(f32[8,128]{1,0:T(8,128)S(1)} %get-tuple-element.30), channel_id=1, source_target_pairs={{0,16},{16,0},{1,17},{17,1},{2,18},{18,2},{3,19},{19,3},{4,20},{20... | collective-permute-start | bytes 12296 | tf_op jit(solution)/shard_map/ppermute | solution.py:401
  20.2 3.2 %collective-permute-start.5 = (f32[264,128]{1,0:T(8,128)S(1)}, f32[264,128]{1,0:T(8,128)S(1)}, u32[]{:S(2)}, u32[]{:S(2)}) collective-permute-start(f32[264,128]{1,0:T(8,128)S(1)} %get-tuple-element.31), channel_id=1, source_target_pairs={{16,32},{48,64},{80,96},{112,128},{144,160},{176,192},{208,224},{2... | collective-permute-start | bytes 405512 | tf_op jit(solution)/shard_map/ppermute | solution.py:405
  23.8 1.9 %collective-permute-start.4 = (f32[256,128]{1,0:T(8,128)S(1)}, f32[256,128]{1,0:T(8,128)S(1)}, u32[]{:S(2)}, u32[]{:S(2)}) collective-permute-start(f32[256,128]{1,0:T(8,128)S(1)} %shard_map.81), channel_id=1, source_target_pairs={{0,16},{16,0},{1,17},{17,1},{2,18},{18,2},{3,19},{19,3},{4,20},{20... | collective-permute-start | bytes 393224 | tf_op jit(solution)/shard_map/ppermute | solution.py:407
  26.4 0.7 shard_map.80.near
  27.1 3.5 %collective-permute-done.5.beyond = f32[264,128]{1,0:T(8,128)S(1)} collective-permute-done((f32[264,128]{1,0:T(8,128)S(1)}, f32[264,128]{1,0:T(8,128)S(1)}, u32[]{:S(2)}, u32[]{:S(2)}) %collective-permute-start.5) | collective-permute-done | bytes 135200 | tf_op jit(solution)/shard_map/ppermute | solution.py:405
  30.6 3.7 %shard_map.82 = (f32[512,128]{1,0:T(8,128)S(1)}, f32[776,128]{1,0:T(8,128)S(1)}, f32[264,128]{1,0:T(8,128)S(1)}, f32[256,128]{1,0:T(8,128)S(1)}) custom-call(s32[2]{0:T(128)S(1)} %bitcast.10, s32[1]{0:T(128)} %bitcast.5.live, f32[256,128]{1,0:T(8,128)S(1)} %shard_map.80.near, f32[256,128]{1,0:T(8,128)S(1)} %collective-permute-done.4.other, ...), custom_call_target="tpu_custom_call" | custom-call | tf_op jit(solution)/shard_map/pallas_call | solution.py:415
  34.4 1.9 %collective-permute-start.6 = (f32[776,128]{1,0:T(8,128)S(1)}, f32[776,128]{1,0:T(8,128)S(1)}, u32[]{:S(2)}, u32[]{:S(2)}) collective-permute-start(f32[776,128]{1,0:T(8,128)S(1)} %get-tuple-element.36), channel_id=1, source_target_pairs={{0,16},{16,0},{1,17},{17,1},{2,18},{18,2},{3,19},{19,3},{4,20},{20... | collective-permute-start | bytes 1191944 | tf_op jit(solution)/shard_map/ppermute | solution.py:428
  36.3 1.7 %collective-permute-done.6.from_core.message = f32[776,128]{1,0:T(8,128)S(1)} collective-permute-done((f32[776,128]{1,0:T(8,128)S(1)}, f32[776,128]{1,0:T(8,128)S(1)}, u32[]{:S(2)}, u32[]{:S(2)}) %collective-permute-start.6) | collective-permute-done | bytes 397344 | tf_op jit(solution)/shard_map/ppermute | solution.py:428
  38.0 0.7 shard_map.84
  38.7 18.6 %all-to-all-start = ((f32[32,16,128]{2,1,0:T(8,128)}), f32[32,16,128]{2,1,0:T(8,128)S(1)}, u32[]{:S(2)}, u32[]{:S(2)}) async-start(f32[32,16,128]{2,1,0:T(8,128)} %bitcast.3), calls=%async_computation | async-start | bytes 524288 | tf_op jit(solution)/shard_map/all_to_all | solution.py:436
  57.4 3.5 %collective-permute-start.7 = (f32[264,128]{1,0:T(8,128)S(1)}, f32[264,128]{1,0:T(8,128)S(1)}, u32[]{:S(2)}, u32[]{:S(2)}) collective-permute-start(f32[264,128]{1,0:T(8,128)S(1)} %get-tuple-element.37), channel_id=1, source_target_pairs={{16,32},{48,64},{80,96},{112,128},{144,160},{176,192},{208,224},{2... | collective-permute-start | bytes 405512 | tf_op jit(solution)/shard_map/ppermute | solution.py:429
  60.8 8.4 %all-to-all-done.parts = f32[32,16,128]{2,1,0:T(8,128)S(1)} async-done(((f32[32,16,128]{2,1,0:T(8,128)}), f32[32,16,128]{2,1,0:T(8,128)S(1)}, u32[]{:S(2)}, u32[]{:S(2)}) %all-to-all-start) | async-done | bytes 262176 | tf_op jit(solution)/shard_map/all_to_all | solution.py:436
  69.9 3.4 %all-to-all-start.1 = ((f32[8,16,128]{2,1,0:T(8,128)}), f32[8,16,128]{2,1,0:T(8,128)S(1)}, u32[]{:S(2)}, u32[]{:S(2)}) async-start(f32[8,16,128]{2,1,0:T(8,128)} %shard_map.85), calls=%async_computation.1 | async-start | bytes 131072 | tf_op jit(solution)/shard_map/all_to_all | solution.py:446
  73.2 1.0 shard_map.83
  74.2 3.3 %collective-permute-start.8 = (f32[2,64,128]{2,1,0:T(8,128)S(1)}, f32[2,64,128]{2,1,0:T(8,128)S(1)}, u32[]{:S(2)}, u32[]{:S(2)}) collective-permute-start(f32[2,64,128]{2,1,0:T(8,128)S(1)} %get-tuple-element.40), channel_id=1, source_target_pairs={{0,1},{2,3},{4,5},{6,7},{8,9},{10,11},{12,13},{14,15},{1,0},{3,2},... | collective-permute-start | bytes 196616 | tf_op jit(solution)/shard_map/ppermute | solution.py:448
  77.5 2.9 %all-to-all-done.1.parts = f32[8,16,128]{2,1,0:T(8,128)S(1)} async-done(((f32[8,16,128]{2,1,0:T(8,128)}), f32[8,16,128]{2,1,0:T(8,128)S(1)}, u32[]{:S(2)}, u32[]{:S(2)}) %all-to-all-start.1) | async-done | bytes 65568 | tf_op jit(solution)/shard_map/all_to_all | solution.py:446
  80.4 0.7 shard_map.86
  81.1 5.5 %all-to-all-start.2 = ((f32[32,16,128]{2,1,0:T(8,128)}), f32[32,16,128]{2,1,0:T(8,128)S(1)}, u32[]{:S(2)}, u32[]{:S(2)}) async-start(f32[32,16,128]{2,1,0:T(8,128)} %shard_map.86), calls=%async_computation.2 | async-start | bytes 524288 | tf_op jit(solution)/shard_map/all_to_all | solution.py:451
  87.3 9.8 %all-to-all-done.2 = f32[32,16,128]{2,1,0:T(8,128)S(1)} async-done(((f32[32,16,128]{2,1,0:T(8,128)}), f32[32,16,128]{2,1,0:T(8,128)S(1)}, u32[]{:S(2)}, u32[]{:S(2)}) %all-to-all-start.2) | async-done | bytes 262176 | tf_op jit(solution)/shard_map/all_to_all | solution.py:451
  97.0 5.6 %collective-permute-start.10 = (f32[4,128,128]{2,1,0:T(8,128)S(1)}, f32[4,128,128]{2,1,0:T(8,128)S(1)}, u32[]{:S(2)}, u32[]{:S(2)}) collective-permute-start(f32[4,128,128]{2,1,0:T(8,128)S(1)} %bitcast.6), channel_id=1, source_target_pairs={{0,16},{16,0},{1,17},{17,1},{2,18},{18,2},{3,19},{19,3},{4,20},{20... | collective-permute-start | bytes 786440 | tf_op jit(solution)/shard_map/ppermute | solution.py:454
  102.6 0.8 shard_map.87
  103.8 0.7 shard_map.88
  (26 shorter events, 4.3 us)
Async XLA Ops:
  0.6 0.7 copy-start.4
  1.3 12.1 %copy-start.2 = (f32[2,2,64,256]{3,2,1,0:T(8,128)S(1)}, f32[2,2,64,256]{3,2,1,0:T(8,128)}, u32[]{:S(2)}) copy-start(f32[2,2,64,256]{3,2,1,0:T(8,128)} %own.3) | copy-start | bytes 786436
  1.4 18.6 %collective-permute-start = (f32[136,128]{1,0:T(8,128)S(1)}, f32[136,128]{1,0:T(8,128)S(1)}, u32[]{:S(2)}, u32[]{:S(2)}) collective-permute-start(f32[136,128]{1,0:T(8,128)S(1)} %get-tuple-element.26), channel_id=1, source_target_pairs={{16,32},{48,64},{80,96},{112,128},{144,160},{176,192},{208,224},{2... | collective-permute-start | bytes 208904 | tf_op jit(solution)/shard_map/ppermute | solution.py:398
  13.5 6.4 %collective-permute-start.1 = (f32[2,64,128]{2,1,0:T(8,128)S(1)}, f32[2,64,128]{2,1,0:T(8,128)S(1)}, u32[]{:S(2)}, u32[]{:S(2)}) collective-permute-start(f32[2,64,128]{2,1,0:T(8,128)S(1)} %get-tuple-element.27), channel_id=1, source_target_pairs={{0,1},{2,3},{4,5},{6,7},{8,9},{10,11},{12,13},{14,15},{1,0},{3,2},... | collective-permute-start | bytes 196616 | tf_op jit(solution)/shard_map/ppermute | solution.py:399
  16.6 3.3 %collective-permute-start.2 = (f32[2,64,128]{2,1,0:T(8,128)S(1)}, f32[2,64,128]{2,1,0:T(8,128)S(1)}, u32[]{:S(2)}, u32[]{:S(2)}) collective-permute-start(f32[2,64,128]{2,1,0:T(8,128)S(1)} %get-tuple-element.28), channel_id=1, source_target_pairs={{1,2},{3,4},{5,6},{7,8},{9,10},{11,12},{13,14},{2,1},{4,3},{6,5},{... | collective-permute-start | bytes 196616 | tf_op jit(solution)/shard_map/ppermute | solution.py:400
  17.3 9.1 %copy-start = (f32[2,4,128,128]{3,2,1,0:T(8,128)S(1)}, f32[2,4,128,128]{3,2,1,0:T(8,128)}, u32[]{:S(2)}) copy-start(f32[2,4,128,128]{3,2,1,0:T(8,128)} %probe.3) | copy-start | bytes 1572868
  17.3 6.2 %collective-permute-start.3 = (f32[8,128]{1,0:T(8,128)S(1)}, f32[8,128]{1,0:T(8,128)S(1)}, u32[]{:S(2)}, u32[]{:S(2)}) collective-permute-start(f32[8,128]{1,0:T(8,128)S(1)} %get-tuple-element.30), channel_id=1, source_target_pairs={{0,16},{16,0},{1,17},{17,1},{2,18},{18,2},{3,19},{19,3},{4,20},{20... | collective-permute-start | bytes 12296 | tf_op jit(solution)/shard_map/ppermute | solution.py:401
  20.2 6.1 %copy-start.1 = (bf16[12,128,128]{2,1,0:T(8,128)(2,1)S(1)}, bf16[12,128,128]{2,1,0:T(8,128)(2,1)}, u32[]{:S(2)}) copy-start(bf16[12,128,128]{2,1,0:T(8,128)(2,1)} %constant.2.clone.tabs) | copy-start | bytes 1179652
  20.2 10.4 %collective-permute-start.5 = (f32[264,128]{1,0:T(8,128)S(1)}, f32[264,128]{1,0:T(8,128)S(1)}, u32[]{:S(2)}, u32[]{:S(2)}) collective-permute-start(f32[264,128]{1,0:T(8,128)S(1)} %get-tuple-element.31), channel_id=1, source_target_pairs={{16,32},{48,64},{80,96},{112,128},{144,160},{176,192},{208,224},{2... | collective-permute-start | bytes 405512 | tf_op jit(solution)/shard_map/ppermute | solution.py:405
  23.5 2.9 %copy-start.3 = (f32[1,1,1,128,128]{4,3,2,1,0:T(8,128)S(1)}, f32[1,1,1,128,128]{4,3,2,1,0:T(8,128)}, u32[]{:S(2)}) copy-start(f32[1,1,1,128,128]{4,3,2,1,0:T(8,128)} %pattern.3) | copy-start | bytes 196612
  23.8 3.3 %collective-permute-start.4 = (f32[256,128]{1,0:T(8,128)S(1)}, f32[256,128]{1,0:T(8,128)S(1)}, u32[]{:S(2)}, u32[]{:S(2)}) collective-permute-start(f32[256,128]{1,0:T(8,128)S(1)} %shard_map.81), channel_id=1, source_target_pairs={{0,16},{16,0},{1,17},{17,1},{2,18},{18,2},{3,19},{19,3},{4,20},{20... | collective-permute-start | bytes 393224 | tf_op jit(solution)/shard_map/ppermute | solution.py:407
  34.4 3.6 %collective-permute-start.6 = (f32[776,128]{1,0:T(8,128)S(1)}, f32[776,128]{1,0:T(8,128)S(1)}, u32[]{:S(2)}, u32[]{:S(2)}) collective-permute-start(f32[776,128]{1,0:T(8,128)S(1)} %get-tuple-element.36), channel_id=1, source_target_pairs={{0,16},{16,0},{1,17},{17,1},{2,18},{18,2},{3,19},{19,3},{4,20},{20... | collective-permute-start | bytes 1191944 | tf_op jit(solution)/shard_map/ppermute | solution.py:428
  38.7 30.5 %all-to-all-start = ((f32[32,16,128]{2,1,0:T(8,128)}), f32[32,16,128]{2,1,0:T(8,128)S(1)}, u32[]{:S(2)}, u32[]{:S(2)}) async-start(f32[32,16,128]{2,1,0:T(8,128)} %bitcast.3), calls=%async_computation | async-start | bytes 524288 | tf_op jit(solution)/shard_map/all_to_all | solution.py:436
  57.4 15.9 %collective-permute-start.7 = (f32[264,128]{1,0:T(8,128)S(1)}, f32[264,128]{1,0:T(8,128)S(1)}, u32[]{:S(2)}, u32[]{:S(2)}) collective-permute-start(f32[264,128]{1,0:T(8,128)S(1)} %get-tuple-element.37), channel_id=1, source_target_pairs={{16,32},{48,64},{80,96},{112,128},{144,160},{176,192},{208,224},{2... | collective-permute-start | bytes 405512 | tf_op jit(solution)/shard_map/ppermute | solution.py:429
  69.9 10.5 %all-to-all-start.1 = ((f32[8,16,128]{2,1,0:T(8,128)}), f32[8,16,128]{2,1,0:T(8,128)S(1)}, u32[]{:S(2)}, u32[]{:S(2)}) async-start(f32[8,16,128]{2,1,0:T(8,128)} %shard_map.85), calls=%async_computation.1 | async-start | bytes 131072 | tf_op jit(solution)/shard_map/all_to_all | solution.py:446
  74.2 6.9 %collective-permute-start.8 = (f32[2,64,128]{2,1,0:T(8,128)S(1)}, f32[2,64,128]{2,1,0:T(8,128)S(1)}, u32[]{:S(2)}, u32[]{:S(2)}) collective-permute-start(f32[2,64,128]{2,1,0:T(8,128)S(1)} %get-tuple-element.40), channel_id=1, source_target_pairs={{0,1},{2,3},{4,5},{6,7},{8,9},{10,11},{12,13},{14,15},{1,0},{3,2},... | collective-permute-start | bytes 196616 | tf_op jit(solution)/shard_map/ppermute | solution.py:448
  81.1 15.9 %all-to-all-start.2 = ((f32[32,16,128]{2,1,0:T(8,128)}), f32[32,16,128]{2,1,0:T(8,128)S(1)}, u32[]{:S(2)}, u32[]{:S(2)}) async-start(f32[32,16,128]{2,1,0:T(8,128)} %shard_map.86), calls=%async_computation.2 | async-start | bytes 524288 | tf_op jit(solution)/shard_map/all_to_all | solution.py:451
  86.6 0.7 collective-permute-start.9
  97.0 6.7 %collective-permute-start.10 = (f32[4,128,128]{2,1,0:T(8,128)S(1)}, f32[4,128,128]{2,1,0:T(8,128)S(1)}, u32[]{:S(2)}, u32[]{:S(2)}) collective-permute-start(f32[4,128,128]{2,1,0:T(8,128)S(1)} %bitcast.6), channel_id=1, source_target_pairs={{0,16},{16,0},{1,17},{17,1},{2,18},{18,2},{3,19},{19,3},{4,20},{20... | collective-permute-start | bytes 786440 | tf_op jit(solution)/shard_map/ppermute | solution.py:454

commit v9 on v8

--- a/solution.py
+++ b/solution.py
@@ -428,12 +428,12 @@
     from_core = lax.ppermute(message_core, "core", swap)
     from_beyond = lax.ppermute(message_beyond, ROW, pairs)
 
-    n_yx = lax.axis_size(("y", "x"))
+    n_yx = lax.axis_size(("x", "y"))
     n_z = lax.axis_size(("zh", "zl"))
     total = modes * side
     chunk = total // n_yx
     summed = call(add_kernel, shape(total, side), 0, 2)(keep, from_core)
-    spread = lax.all_to_all(summed.reshape(n_yx, chunk, side), ("y", "x"), 0, 0)
+    spread = lax.all_to_all(summed.reshape(n_yx, chunk, side), ("x", "y"), 0, 0)
 
     centre, grad_even, grad_odd = call(
         merge_kernel,
@@ -448,7 +448,7 @@
     got_even = lax.ppermute(grad_even, COL, even_pairs)
     part, got_even, grad_odd = lax.optimization_barrier((part, got_even, grad_odd))
     got_odd = lax.ppermute(grad_odd, COL, odd_pairs)
-    whole = lax.all_to_all(part, ("y", "x"), 0, 0)
+    whole = lax.all_to_all(part, ("x", "y"), 0, 0)
     whole, got_even, got_odd = lax.optimization_barrier((whole, got_even, got_odd))
     whole = whole.reshape(modes, side, side)
     facing = lax.ppermute(whole, "core", swap)

time: 105 us -> 104 us (level)
  waiting for transfers between devices: 27.1 us -> 24.8 us
  starting transfers between devices: 65.3 us -> 66.9 us
    all_to_all x2, waiting for transfers between devices: 18.1 us -> 15.8 us  [the longest x1 9.19 us: body(): whole = lax.all_to_all(part, ('x', 'y'), 0, 0)]
    all_to_all x2, starting transfers between devices: 24.1 us -> 25.8 us  [the longest x1 18.6 us: body(): spread = lax.all_to_all(summed.reshape(n_yx, chunk, side), ('x', 'y'), 0, 0)]
where the time goes in v9:
time: 104 us
  starting transfers between devices  66.9 us (64%)
  waiting for transfers between devices  24.8 us (24%)
  Pallas kernels  9.79 us (9%)
  between operations  1.54 us (1%)
    all_to_all x1, starting transfers between devices, body(): spread = lax.all_to_all(summed.reshape(n_yx, chunk, side), ('x', 'y'), 0, 0)  18.6 us
    ppermute x1, starting transfers between devices, body(): column = lax.ppermute(column, ROW, pairs)  12 us
    all_to_all x1, waiting for transfers between devices, body(): whole = lax.all_to_all(part, ('x', 'y'), 0, 0)  9.19 us
    all_to_all x1, starting transfers between devices, body(): whole = lax.all_to_all(part, ('x', 'y'), 0, 0)  7.19 us
    all_to_all x1, waiting for transfers between devices, body(): spread = lax.all_to_all(summed.reshape(n_yx, chunk, side), ('x', 'y'), 0, 0)  6.63 us
    ppermute x1, starting transfers between devices, body(): facing = lax.ppermute(whole, 'core', swap)  5.38 us
    pallas_call x1, Pallas kernels, body(): call(main_kernel, [shape(modes * side, side), shape(modes * side + strip...  3.74 us
    ppermute x1, waiting for transfers between devices, body(): beyond = lax.ppermute(to_beyond, ROW, pairs)  3.53 us
  transfers between devices with their start and end apart: 14, of which 7 were waited for; matrix products, arithmetic and copies ran while one was open for 0% of the time, Pallas kernels for 4%

profile of v9, /device:TPU:1, one launch (start us, length us, event | category | flops | bytes accessed | tf_op | source)
XLA Modules:
  0.0 103.7 jit_solution(6857245971570633198)
XLA Ops:
  1.4 12.0 %collective-permute-start = (f32[136,128]{1,0:T(8,128)S(1)}, f32[136,128]{1,0:T(8,128)S(1)}, u32[]{:S(2)}, u32[]{:S(2)}) collective-permute-start(f32[136,128]{1,0:T(8,128)S(1)} %get-tuple-element.26), channel_id=1, source_target_pairs={{16,32},{48,64},{80,96},{112,128},{144,160},{176,192},{208,224},{2... | collective-permute-start | bytes 208904 | tf_op jit(solution)/shard_map/ppermute | solution.py:398
  13.5 3.1 %collective-permute-start.1 = (f32[2,64,128]{2,1,0:T(8,128)S(1)}, f32[2,64,128]{2,1,0:T(8,128)S(1)}, u32[]{:S(2)}, u32[]{:S(2)}) collective-permute-start(f32[2,64,128]{2,1,0:T(8,128)S(1)} %get-tuple-element.27), channel_id=1, source_target_pairs={{0,1},{2,3},{4,5},{6,7},{8,9},{10,11},{12,13},{14,15},{1,0},{3,2},... | collective-permute-start | bytes 196616 | tf_op jit(solution)/shard_map/ppermute | solution.py:399
  17.3 2.1 %collective-permute-start.3 = (f32[8,128]{1,0:T(8,128)S(1)}, f32[8,128]{1,0:T(8,128)S(1)}, u32[]{:S(2)}, u32[]{:S(2)}) collective-permute-start(f32[8,128]{1,0:T(8,128)S(1)} %get-tuple-element.30), channel_id=1, source_target_pairs={{0,16},{16,0},{1,17},{17,1},{2,18},{18,2},{3,19},{19,3},{4,20},{20... | collective-permute-start | bytes 12296 | tf_op jit(solution)/shard_map/ppermute | solution.py:401
  20.2 3.2 %collective-permute-start.5 = (f32[264,128]{1,0:T(8,128)S(1)}, f32[264,128]{1,0:T(8,128)S(1)}, u32[]{:S(2)}, u32[]{:S(2)}) collective-permute-start(f32[264,128]{1,0:T(8,128)S(1)} %get-tuple-element.31), channel_id=1, source_target_pairs={{16,32},{48,64},{80,96},{112,128},{144,160},{176,192},{208,224},{2... | collective-permute-start | bytes 405512 | tf_op jit(solution)/shard_map/ppermute | solution.py:405
  23.8 1.9 %collective-permute-start.4 = (f32[256,128]{1,0:T(8,128)S(1)}, f32[256,128]{1,0:T(8,128)S(1)}, u32[]{:S(2)}, u32[]{:S(2)}) collective-permute-start(f32[256,128]{1,0:T(8,128)S(1)} %shard_map.81), channel_id=1, source_target_pairs={{0,16},{16,0},{1,17},{17,1},{2,18},{18,2},{3,19},{19,3},{4,20},{20... | collective-permute-start | bytes 393224 | tf_op jit(solution)/shard_map/ppermute | solution.py:407
  26.4 0.7 shard_map.80.near
  27.1 3.5 %collective-permute-done.5.beyond = f32[264,128]{1,0:T(8,128)S(1)} collective-permute-done((f32[264,128]{1,0:T(8,128)S(1)}, f32[264,128]{1,0:T(8,128)S(1)}, u32[]{:S(2)}, u32[]{:S(2)}) %collective-permute-start.5) | collective-permute-done | bytes 135200 | tf_op jit(solution)/shard_map/ppermute | solution.py:405
  30.6 3.7 %shard_map.82 = (f32[512,128]{1,0:T(8,128)S(1)}, f32[776,128]{1,0:T(8,128)S(1)}, f32[264,128]{1,0:T(8,128)S(1)}, f32[256,128]{1,0:T(8,128)S(1)}) custom-call(s32[2]{0:T(128)S(1)} %bitcast.10, s32[1]{0:T(128)} %bitcast.5.live, f32[256,128]{1,0:T(8,128)S(1)} %shard_map.80.near, f32[256,128]{1,0:T(8,128)S(1)} %collective-permute-done.4.other, ...), custom_call_target="tpu_custom_call" | custom-call | tf_op jit(solution)/shard_map/pallas_call | solution.py:415
  34.3 1.9 %collective-permute-start.6 = (f32[776,128]{1,0:T(8,128)S(1)}, f32[776,128]{1,0:T(8,128)S(1)}, u32[]{:S(2)}, u32[]{:S(2)}) collective-permute-start(f32[776,128]{1,0:T(8,128)S(1)} %get-tuple-element.36), channel_id=1, source_target_pairs={{0,16},{16,0},{1,17},{17,1},{2,18},{18,2},{3,19},{19,3},{4,20},{20... | collective-permute-start | bytes 1191944 | tf_op jit(solution)/shard_map/ppermute | solution.py:428
  36.3 1.7 %collective-permute-done.6.from_core.message = f32[776,128]{1,0:T(8,128)S(1)} collective-permute-done((f32[776,128]{1,0:T(8,128)S(1)}, f32[776,128]{1,0:T(8,128)S(1)}, u32[]{:S(2)}, u32[]{:S(2)}) %collective-permute-start.6) | collective-permute-done | bytes 397344 | tf_op jit(solution)/shard_map/ppermute | solution.py:428
  38.0 0.7 shard_map.84
  38.7 18.6 %all-to-all-start = ((f32[32,16,128]{2,1,0:T(8,128)}), f32[32,16,128]{2,1,0:T(8,128)S(1)}, u32[]{:S(2)}, u32[]{:S(2)}) async-start(f32[32,16,128]{2,1,0:T(8,128)} %bitcast.3), calls=%async_computation | async-start | bytes 524288 | tf_op jit(solution)/shard_map/all_to_all | solution.py:436
  57.4 3.5 %collective-permute-start.7 = (f32[264,128]{1,0:T(8,128)S(1)}, f32[264,128]{1,0:T(8,128)S(1)}, u32[]{:S(2)}, u32[]{:S(2)}) collective-permute-start(f32[264,128]{1,0:T(8,128)S(1)} %get-tuple-element.37), channel_id=1, source_target_pairs={{16,32},{48,64},{80,96},{112,128},{144,160},{176,192},{208,224},{2... | collective-permute-start | bytes 405512 | tf_op jit(solution)/shard_map/ppermute | solution.py:429
  60.8 6.6 %all-to-all-done.parts = f32[32,16,128]{2,1,0:T(8,128)S(1)} async-done(((f32[32,16,128]{2,1,0:T(8,128)}), f32[32,16,128]{2,1,0:T(8,128)S(1)}, u32[]{:S(2)}, u32[]{:S(2)}) %all-to-all-start) | async-done | bytes 262176 | tf_op jit(solution)/shard_map/all_to_all | solution.py:436
  68.1 3.4 %all-to-all-start.1 = ((f32[8,16,128]{2,1,0:T(8,128)}), f32[8,16,128]{2,1,0:T(8,128)S(1)}, u32[]{:S(2)}, u32[]{:S(2)}) async-start(f32[8,16,128]{2,1,0:T(8,128)} %shard_map.85), calls=%async_computation.1 | async-start | bytes 131072 | tf_op jit(solution)/shard_map/all_to_all | solution.py:446
  71.5 0.9 shard_map.83
  72.5 3.3 %collective-permute-start.8 = (f32[2,64,128]{2,1,0:T(8,128)S(1)}, f32[2,64,128]{2,1,0:T(8,128)S(1)}, u32[]{:S(2)}, u32[]{:S(2)}) collective-permute-start(f32[2,64,128]{2,1,0:T(8,128)S(1)} %get-tuple-element.40), channel_id=1, source_target_pairs={{0,1},{2,3},{4,5},{6,7},{8,9},{10,11},{12,13},{14,15},{1,0},{3,2},... | collective-permute-start | bytes 196616 | tf_op jit(solution)/shard_map/ppermute | solution.py:448
  75.7 2.9 %all-to-all-done.1.parts = f32[8,16,128]{2,1,0:T(8,128)S(1)} async-done(((f32[8,16,128]{2,1,0:T(8,128)}), f32[8,16,128]{2,1,0:T(8,128)S(1)}, u32[]{:S(2)}, u32[]{:S(2)}) %all-to-all-start.1) | async-done | bytes 65568 | tf_op jit(solution)/shard_map/all_to_all | solution.py:446
  78.6 0.7 shard_map.86
  79.4 7.2 %all-to-all-start.2 = ((f32[32,16,128]{2,1,0:T(8,128)}), f32[32,16,128]{2,1,0:T(8,128)S(1)}, u32[]{:S(2)}, u32[]{:S(2)}) async-start(f32[32,16,128]{2,1,0:T(8,128)} %shard_map.86), calls=%async_computation.2 | async-start | bytes 524288 | tf_op jit(solution)/shard_map/all_to_all | solution.py:451
  87.3 9.2 %all-to-all-done.2 = f32[32,16,128]{2,1,0:T(8,128)S(1)} async-done(((f32[32,16,128]{2,1,0:T(8,128)}), f32[32,16,128]{2,1,0:T(8,128)S(1)}, u32[]{:S(2)}, u32[]{:S(2)}) %all-to-all-start.2) | async-done | bytes 262176 | tf_op jit(solution)/shard_map/all_to_all | solution.py:451
  96.4 5.4 %collective-permute-start.10 = (f32[4,128,128]{2,1,0:T(8,128)S(1)}, f32[4,128,128]{2,1,0:T(8,128)S(1)}, u32[]{:S(2)}, u32[]{:S(2)}) collective-permute-start(f32[4,128,128]{2,1,0:T(8,128)S(1)} %bitcast.6), channel_id=1, source_target_pairs={{0,16},{16,0},{1,17},{17,1},{2,18},{18,2},{3,19},{19,3},{4,20},{20... | collective-permute-start | bytes 786440 | tf_op jit(solution)/shard_map/ppermute | solution.py:454
  101.8 0.8 shard_map.87
  103.0 0.7 shard_map.88
  (26 shorter events, 4.3 us)
Async XLA Ops:
  0.6 0.7 copy-start.4
  1.3 12.1 %copy-start.2 = (f32[2,2,64,256]{3,2,1,0:T(8,128)S(1)}, f32[2,2,64,256]{3,2,1,0:T(8,128)}, u32[]{:S(2)}) copy-start(f32[2,2,64,256]{3,2,1,0:T(8,128)} %own.3) | copy-start | bytes 786436
  1.4 18.6 %collective-permute-start = (f32[136,128]{1,0:T(8,128)S(1)}, f32[136,128]{1,0:T(8,128)S(1)}, u32[]{:S(2)}, u32[]{:S(2)}) collective-permute-start(f32[136,128]{1,0:T(8,128)S(1)} %get-tuple-element.26), channel_id=1, source_target_pairs={{16,32},{48,64},{80,96},{112,128},{144,160},{176,192},{208,224},{2... | collective-permute-start | bytes 208904 | tf_op jit(solution)/shard_map/ppermute | solution.py:398
  13.5 6.4 %collective-permute-start.1 = (f32[2,64,128]{2,1,0:T(8,128)S(1)}, f32[2,64,128]{2,1,0:T(8,128)S(1)}, u32[]{:S(2)}, u32[]{:S(2)}) collective-permute-start(f32[2,64,128]{2,1,0:T(8,128)S(1)} %get-tuple-element.27), channel_id=1, source_target_pairs={{0,1},{2,3},{4,5},{6,7},{8,9},{10,11},{12,13},{14,15},{1,0},{3,2},... | collective-permute-start | bytes 196616 | tf_op jit(solution)/shard_map/ppermute | solution.py:399
  16.6 3.3 %collective-permute-start.2 = (f32[2,64,128]{2,1,0:T(8,128)S(1)}, f32[2,64,128]{2,1,0:T(8,128)S(1)}, u32[]{:S(2)}, u32[]{:S(2)}) collective-permute-start(f32[2,64,128]{2,1,0:T(8,128)S(1)} %get-tuple-element.28), channel_id=1, source_target_pairs={{1,2},{3,4},{5,6},{7,8},{9,10},{11,12},{13,14},{2,1},{4,3},{6,5},{... | collective-permute-start | bytes 196616 | tf_op jit(solution)/shard_map/ppermute | solution.py:400
  17.3 9.1 %copy-start = (f32[2,4,128,128]{3,2,1,0:T(8,128)S(1)}, f32[2,4,128,128]{3,2,1,0:T(8,128)}, u32[]{:S(2)}) copy-start(f32[2,4,128,128]{3,2,1,0:T(8,128)} %probe.3) | copy-start | bytes 1572868
  17.3 6.2 %collective-permute-start.3 = (f32[8,128]{1,0:T(8,128)S(1)}, f32[8,128]{1,0:T(8,128)S(1)}, u32[]{:S(2)}, u32[]{:S(2)}) collective-permute-start(f32[8,128]{1,0:T(8,128)S(1)} %get-tuple-element.30), channel_id=1, source_target_pairs={{0,16},{16,0},{1,17},{17,1},{2,18},{18,2},{3,19},{19,3},{4,20},{20... | collective-permute-start | bytes 12296 | tf_op jit(solution)/shard_map/ppermute | solution.py:401
  20.2 6.1 %copy-start.1 = (bf16[12,128,128]{2,1,0:T(8,128)(2,1)S(1)}, bf16[12,128,128]{2,1,0:T(8,128)(2,1)}, u32[]{:S(2)}) copy-start(bf16[12,128,128]{2,1,0:T(8,128)(2,1)} %constant.2.clone.tabs) | copy-start | bytes 1179652
  20.2 10.4 %collective-permute-start.5 = (f32[264,128]{1,0:T(8,128)S(1)}, f32[264,128]{1,0:T(8,128)S(1)}, u32[]{:S(2)}, u32[]{:S(2)}) collective-permute-start(f32[264,128]{1,0:T(8,128)S(1)} %get-tuple-element.31), channel_id=1, source_target_pairs={{16,32},{48,64},{80,96},{112,128},{144,160},{176,192},{208,224},{2... | collective-permute-start | bytes 405512 | tf_op jit(solution)/shard_map/ppermute | solution.py:405
  23.5 2.9 %copy-start.3 = (f32[1,1,1,128,128]{4,3,2,1,0:T(8,128)S(1)}, f32[1,1,1,128,128]{4,3,2,1,0:T(8,128)}, u32[]{:S(2)}) copy-start(f32[1,1,1,128,128]{4,3,2,1,0:T(8,128)} %pattern.3) | copy-start | bytes 196612
  23.8 3.3 %collective-permute-start.4 = (f32[256,128]{1,0:T(8,128)S(1)}, f32[256,128]{1,0:T(8,128)S(1)}, u32[]{:S(2)}, u32[]{:S(2)}) collective-permute-start(f32[256,128]{1,0:T(8,128)S(1)} %shard_map.81), channel_id=1, source_target_pairs={{0,16},{16,0},{1,17},{17,1},{2,18},{18,2},{3,19},{19,3},{4,20},{20... | collective-permute-start | bytes 393224 | tf_op jit(solution)/shard_map/ppermute | solution.py:407
  34.3 3.6 %collective-permute-start.6 = (f32[776,128]{1,0:T(8,128)S(1)}, f32[776,128]{1,0:T(8,128)S(1)}, u32[]{:S(2)}, u32[]{:S(2)}) collective-permute-start(f32[776,128]{1,0:T(8,128)S(1)} %get-tuple-element.36), channel_id=1, source_target_pairs={{0,16},{16,0},{1,17},{17,1},{2,18},{18,2},{3,19},{19,3},{4,20},{20... | collective-permute-start | bytes 1191944 | tf_op jit(solution)/shard_map/ppermute | solution.py:428
  38.7 28.8 %all-to-all-start = ((f32[32,16,128]{2,1,0:T(8,128)}), f32[32,16,128]{2,1,0:T(8,128)S(1)}, u32[]{:S(2)}, u32[]{:S(2)}) async-start(f32[32,16,128]{2,1,0:T(8,128)} %bitcast.3), calls=%async_computation | async-start | bytes 524288 | tf_op jit(solution)/shard_map/all_to_all | solution.py:436
  57.4 14.1 %collective-permute-start.7 = (f32[264,128]{1,0:T(8,128)S(1)}, f32[264,128]{1,0:T(8,128)S(1)}, u32[]{:S(2)}, u32[]{:S(2)}) collective-permute-start(f32[264,128]{1,0:T(8,128)S(1)} %get-tuple-element.37), channel_id=1, source_target_pairs={{16,32},{48,64},{80,96},{112,128},{144,160},{176,192},{208,224},{2... | collective-permute-start | bytes 405512 | tf_op jit(solution)/shard_map/ppermute | solution.py:429
  68.1 10.5 %all-to-all-start.1 = ((f32[8,16,128]{2,1,0:T(8,128)}), f32[8,16,128]{2,1,0:T(8,128)S(1)}, u32[]{:S(2)}, u32[]{:S(2)}) async-start(f32[8,16,128]{2,1,0:T(8,128)} %shard_map.85), calls=%async_computation.1 | async-start | bytes 131072 | tf_op jit(solution)/shard_map/all_to_all | solution.py:446
  72.5 6.9 %collective-permute-start.8 = (f32[2,64,128]{2,1,0:T(8,128)S(1)}, f32[2,64,128]{2,1,0:T(8,128)S(1)}, u32[]{:S(2)}, u32[]{:S(2)}) collective-permute-start(f32[2,64,128]{2,1,0:T(8,128)S(1)} %get-tuple-element.40), channel_id=1, source_target_pairs={{0,1},{2,3},{4,5},{6,7},{8,9},{10,11},{12,13},{14,15},{1,0},{3,2},... | collective-permute-start | bytes 196616 | tf_op jit(solution)/shard_map/ppermute | solution.py:448
  79.4 17.1 %all-to-all-start.2 = ((f32[32,16,128]{2,1,0:T(8,128)}), f32[32,16,128]{2,1,0:T(8,128)S(1)}, u32[]{:S(2)}, u32[]{:S(2)}) async-start(f32[32,16,128]{2,1,0:T(8,128)} %shard_map.86), calls=%async_computation.2 | async-start | bytes 524288 | tf_op jit(solution)/shard_map/all_to_all | solution.py:451
  86.6 0.7 collective-permute-start.9
  96.4 6.5 %collective-permute-start.10 = (f32[4,128,128]{2,1,0:T(8,128)S(1)}, f32[4,128,128]{2,1,0:T(8,128)S(1)}, u32[]{:S(2)}, u32[]{:S(2)}) collective-permute-start(f32[4,128,128]{2,1,0:T(8,128)S(1)} %bitcast.6), channel_id=1, source_target_pairs={{0,16},{16,0},{1,17},{17,1},{2,18},{18,2},{3,19},{19,3},{4,20},{20... | collective-permute-start | bytes 786440 | tf_op jit(solution)/shard_map/ppermute | solution.py:454

commit v10 on v9

--- a/solution.py
+++ b/solution.py
@@ -15,6 +15,7 @@
 LOSS_WEIGHT = 0.125
 ROW = ("y", "zh", "core")
 COL = ("x", "zl")
+EVERY = ("y", "zh", "core", "x", "zl")
 VMEM_LIMIT = 48 * 1024 * 1024
 TILE_COLS = 256
 
@@ -369,6 +370,24 @@
 
 def both_ways(pairs):
     return pairs + [(j, i) for i, j in pairs]
+
+
+def peer_groups():
+    sizes = {axis: lax.axis_size(axis) for axis in EVERY}
+    n_x, n_y, n_z = sizes["x"], sizes["y"], sizes["zh"] * sizes["zl"]
+
+    def index(x, y, z, core):
+        at = {"x": x, "y": y, "zh": z // sizes["zl"], "zl": z % sizes["zl"], "core": core}
+        flat = 0
+        for axis in EVERY:
+            flat = flat * sizes[axis] + at[axis]
+        return flat
+
+    planes = [[index(x, y, z, 0) for x in range(n_x) for y in range(n_y)] for z in range(n_z)]
+    planes += [[index(x, y, z, 1) for x in range(n_x) for z in range(n_z)] for y in range(n_y)]
+    lines = [[index(x, y, z, 0) for z in range(n_z)] for x in range(n_x) for y in range(n_y)]
+    lines += [[index(x, y, z, 1) for y in range(n_y)] for x in range(n_x) for z in range(n_z)]
+    return planes, lines
 
 
 def body(obj_field, probe, scan_pos, live_count, patterns):
@@ -433,7 +452,10 @@
     total = modes * side
     chunk = total // n_yx
     summed = call(add_kernel, shape(total, side), 0, 2)(keep, from_core)
-    spread = lax.all_to_all(summed.reshape(n_yx, chunk, side), ("x", "y"), 0, 0)
+    planes, lines = peer_groups()
+    spread = lax.all_to_all(
+        summed.reshape(n_yx, chunk, side), EVERY, 0, 0, axis_index_groups=planes
+    )
 
     centre, grad_even, grad_odd = call(
         merge_kernel,
@@ -443,12 +465,12 @@
         [pltpu.VMEM((4, rows, cols + 2 * side), f32)],
     )(scan, own_strip, from_core, from_beyond)
     part = call(sum_kernel, shape(n_z, chunk, side), 0, 1)(spread)
-    part = lax.all_to_all(part, ("zh", "zl"), 0, 0)
+    part = lax.all_to_all(part, EVERY, 0, 0, axis_index_groups=lines)
     part = call(sum_kernel, shape(n_yx, chunk, side), 0, 1)(part)
     got_even = lax.ppermute(grad_even, COL, even_pairs)
     part, got_even, grad_odd = lax.optimization_barrier((part, got_even, grad_odd))
     got_odd = lax.ppermute(grad_odd, COL, odd_pairs)
-    whole = lax.all_to_all(part, ("x", "y"), 0, 0)
+    whole = lax.all_to_all(part, EVERY, 0, 0, axis_index_groups=planes)
     whole, got_even, got_odd = lax.optimization_barrier((whole, got_even, got_odd))
     whole = whole.reshape(modes, side, side)
     facing = lax.ppermute(whole, "core", swap)

time: 104 us -> 103 us (level)
  waiting for transfers between devices: 24.8 us -> 19.8 us
  starting transfers between devices: 66.9 us -> 70.2 us
    all_to_all x3, waiting for transfers between devices: 18.7 us -> 13.7 us  [the longest x1 9.22 us: body(): whole = lax.all_to_all(part, EVERY, 0, 0, axis_index_groups=planes)]
    ppermute x1, starting transfers between devices: 3.47 us -> 8.19 us  [body(): from_beyond = lax.ppermute(message_beyond, ROW, pairs)]
    all_to_all x3, starting transfers between devices: 29.2 us -> 27.3 us  [the longest x1 13.9 us: body(): lax.all_to_all(summed.reshape(n_yx, chunk, side), EVERY, 0, 0, axis_index...]
where the time goes in v10:
time: 103 us; the launch traced here: 102 us
  starting transfers between devices  70.2 us (68%)
  waiting for transfers between devices  19.8 us (19%)
  Pallas kernels  9.79 us (10%)
  between operations  1.53 us (1%)
    all_to_all x1, starting transfers between devices, body(): lax.all_to_all(summed.reshape(n_yx, chunk, side), EVERY, 0, 0, axis_index...  13.9 us
    ppermute x1, starting transfers between devices, body(): column = lax.ppermute(column, ROW, pairs)  12 us
    all_to_all x1, waiting for transfers between devices, body(): whole = lax.all_to_all(part, EVERY, 0, 0, axis_index_groups=planes)  9.22 us
    ppermute x1, starting transfers between devices, body(): from_beyond = lax.ppermute(message_beyond, ROW, pairs)  8.19 us
    all_to_all x1, starting transfers between devices, body(): part = lax.all_to_all(part, EVERY, 0, 0, axis_index_groups=lines)  7.19 us
    all_to_all x1, starting transfers between devices, body(): whole = lax.all_to_all(part, EVERY, 0, 0, axis_index_groups=planes)  6.19 us
    ppermute x1, starting transfers between devices, body(): facing = lax.ppermute(whole, 'core', swap)  5.82 us
    pallas_call x1, Pallas kernels, body(): call(main_kernel, [shape(modes * side, side), shape(modes * side + strip...  3.74 us
  transfers between devices with their start and end apart: 14, of which 7 were waited for; matrix products, arithmetic and copies ran while one was open for 0% of the time, Pallas kernels for 4%

profile of v10, /device:TPU:1, one launch (start us, length us, event | category | flops | bytes accessed | tf_op | source)
XLA Modules:
  0.0 102.0 jit_solution(11502935586305034407)
XLA Ops:
  1.4 12.0 %collective-permute-start = (f32[136,128]{1,0:T(8,128)S(1)}, f32[136,128]{1,0:T(8,128)S(1)}, u32[]{:S(2)}, u32[]{:S(2)}) collective-permute-start(f32[136,128]{1,0:T(8,128)S(1)} %get-tuple-element.26), channel_id=1, source_target_pairs={{16,32},{48,64},{80,96},{112,128},{144,160},{176,192},{208,224},{2... | collective-permute-start | bytes 208904 | tf_op jit(solution)/shard_map/ppermute | solution.py:417
  13.5 3.1 %collective-permute-start.1 = (f32[2,64,128]{2,1,0:T(8,128)S(1)}, f32[2,64,128]{2,1,0:T(8,128)S(1)}, u32[]{:S(2)}, u32[]{:S(2)}) collective-permute-start(f32[2,64,128]{2,1,0:T(8,128)S(1)} %get-tuple-element.27), channel_id=1, source_target_pairs={{0,1},{2,3},{4,5},{6,7},{8,9},{10,11},{12,13},{14,15},{1,0},{3,2},... | collective-permute-start | bytes 196616 | tf_op jit(solution)/shard_map/ppermute | solution.py:418
  17.3 2.1 %collective-permute-start.3 = (f32[8,128]{1,0:T(8,128)S(1)}, f32[8,128]{1,0:T(8,128)S(1)}, u32[]{:S(2)}, u32[]{:S(2)}) collective-permute-start(f32[8,128]{1,0:T(8,128)S(1)} %get-tuple-element.30), channel_id=1, source_target_pairs={{0,16},{16,0},{1,17},{17,1},{2,18},{18,2},{3,19},{19,3},{4,20},{20... | collective-permute-start | bytes 12296 | tf_op jit(solution)/shard_map/ppermute | solution.py:420
  20.2 3.2 %collective-permute-start.5 = (f32[264,128]{1,0:T(8,128)S(1)}, f32[264,128]{1,0:T(8,128)S(1)}, u32[]{:S(2)}, u32[]{:S(2)}) collective-permute-start(f32[264,128]{1,0:T(8,128)S(1)} %get-tuple-element.31), channel_id=1, source_target_pairs={{16,32},{48,64},{80,96},{112,128},{144,160},{176,192},{208,224},{2... | collective-permute-start | bytes 405512 | tf_op jit(solution)/shard_map/ppermute | solution.py:424
  23.8 1.9 %collective-permute-start.4 = (f32[256,128]{1,0:T(8,128)S(1)}, f32[256,128]{1,0:T(8,128)S(1)}, u32[]{:S(2)}, u32[]{:S(2)}) collective-permute-start(f32[256,128]{1,0:T(8,128)S(1)} %shard_map.81), channel_id=1, source_target_pairs={{0,16},{16,0},{1,17},{17,1},{2,18},{18,2},{3,19},{19,3},{4,20},{20... | collective-permute-start | bytes 393224 | tf_op jit(solution)/shard_map/ppermute | solution.py:426
  26.4 0.7 shard_map.80.near
  27.1 3.5 %collective-permute-done.5.beyond = f32[264,128]{1,0:T(8,128)S(1)} collective-permute-done((f32[264,128]{1,0:T(8,128)S(1)}, f32[264,128]{1,0:T(8,128)S(1)}, u32[]{:S(2)}, u32[]{:S(2)}) %collective-permute-start.5) | collective-permute-done | bytes 135200 | tf_op jit(solution)/shard_map/ppermute | solution.py:424
  30.6 3.7 %shard_map.82 = (f32[512,128]{1,0:T(8,128)S(1)}, f32[776,128]{1,0:T(8,128)S(1)}, f32[264,128]{1,0:T(8,128)S(1)}, f32[256,128]{1,0:T(8,128)S(1)}) custom-call(s32[2]{0:T(128)S(1)} %bitcast.10, s32[1]{0:T(128)} %bitcast.5.live, f32[256,128]{1,0:T(8,128)S(1)} %shard_map.80.near, f32[256,128]{1,0:T(8,128)S(1)} %collective-permute-done.4.other, ...), custom_call_target="tpu_custom_call" | custom-call | tf_op jit(solution)/shard_map/pallas_call | solution.py:434
  34.3 1.9 %collective-permute-start.6 = (f32[776,128]{1,0:T(8,128)S(1)}, f32[776,128]{1,0:T(8,128)S(1)}, u32[]{:S(2)}, u32[]{:S(2)}) collective-permute-start(f32[776,128]{1,0:T(8,128)S(1)} %get-tuple-element.36), channel_id=1, source_target_pairs={{0,16},{16,0},{1,17},{17,1},{2,18},{18,2},{3,19},{19,3},{4,20},{20... | collective-permute-start | bytes 1191944 | tf_op jit(solution)/shard_map/ppermute | solution.py:447
  36.3 1.7 %collective-permute-done.6.from_core.message = f32[776,128]{1,0:T(8,128)S(1)} collective-permute-done((f32[776,128]{1,0:T(8,128)S(1)}, f32[776,128]{1,0:T(8,128)S(1)}, u32[]{:S(2)}, u32[]{:S(2)}) %collective-permute-start.6) | collective-permute-done | bytes 397344 | tf_op jit(solution)/shard_map/ppermute | solution.py:447
  38.0 0.7 shard_map.84
  38.7 13.9 %all-to-all-start = ((f32[32,16,128]{2,1,0:T(8,128)}), f32[32,16,128]{2,1,0:T(8,128)S(1)}, u32[]{:S(2)}, u32[]{:S(2)}) async-start(f32[32,16,128]{2,1,0:T(8,128)} %bitcast.3), calls=%async_computation | async-start | bytes 524288 | tf_op jit(solution)/shard_map/all_to_all | solution.py:456
  52.6 8.2 %collective-permute-start.7 = (f32[264,128]{1,0:T(8,128)S(1)}, f32[264,128]{1,0:T(8,128)S(1)}, u32[]{:S(2)}, u32[]{:S(2)}) collective-permute-start(f32[264,128]{1,0:T(8,128)S(1)} %get-tuple-element.37), channel_id=1, source_target_pairs={{16,32},{48,64},{80,96},{112,128},{144,160},{176,192},{208,224},{2... | collective-permute-start | bytes 405512 | tf_op jit(solution)/shard_map/ppermute | solution.py:448
  60.8 1.5 %all-to-all-done.parts = f32[32,16,128]{2,1,0:T(8,128)S(1)} async-done(((f32[32,16,128]{2,1,0:T(8,128)}), f32[32,16,128]{2,1,0:T(8,128)S(1)}, u32[]{:S(2)}, u32[]{:S(2)}) %all-to-all-start) | async-done | bytes 262176 | tf_op jit(solution)/shard_map/all_to_all | solution.py:456
  63.0 7.2 %all-to-all-start.1 = ((f32[8,16,128]{2,1,0:T(8,128)}), f32[8,16,128]{2,1,0:T(8,128)S(1)}, u32[]{:S(2)}, u32[]{:S(2)}) async-start(f32[8,16,128]{2,1,0:T(8,128)} %shard_map.85), calls=%async_computation.1 | async-start | bytes 131072 | tf_op jit(solution)/shard_map/all_to_all | solution.py:468
  70.2 1.0 shard_map.83
  71.2 3.3 %collective-permute-start.8 = (f32[2,64,128]{2,1,0:T(8,128)S(1)}, f32[2,64,128]{2,1,0:T(8,128)S(1)}, u32[]{:S(2)}, u32[]{:S(2)}) collective-permute-start(f32[2,64,128]{2,1,0:T(8,128)S(1)} %get-tuple-element.40), channel_id=1, source_target_pairs={{0,1},{2,3},{4,5},{6,7},{8,9},{10,11},{12,13},{14,15},{1,0},{3,2},... | collective-permute-start | bytes 196616 | tf_op jit(solution)/shard_map/ppermute | solution.py:470
  74.6 2.9 %all-to-all-done.1.parts = f32[8,16,128]{2,1,0:T(8,128)S(1)} async-done(((f32[8,16,128]{2,1,0:T(8,128)}), f32[8,16,128]{2,1,0:T(8,128)S(1)}, u32[]{:S(2)}, u32[]{:S(2)}) %all-to-all-start.1) | async-done | bytes 65568 | tf_op jit(solution)/shard_map/all_to_all | solution.py:468
  77.5 0.7 shard_map.86
  78.2 6.2 %all-to-all-start.2 = ((f32[32,16,128]{2,1,0:T(8,128)}), f32[32,16,128]{2,1,0:T(8,128)S(1)}, u32[]{:S(2)}, u32[]{:S(2)}) async-start(f32[32,16,128]{2,1,0:T(8,128)} %shard_map.86), calls=%async_computation.2 | async-start | bytes 524288 | tf_op jit(solution)/shard_map/all_to_all | solution.py:473
  85.1 9.2 %all-to-all-done.2 = f32[32,16,128]{2,1,0:T(8,128)S(1)} async-done(((f32[32,16,128]{2,1,0:T(8,128)}), f32[32,16,128]{2,1,0:T(8,128)S(1)}, u32[]{:S(2)}, u32[]{:S(2)}) %all-to-all-start.2) | async-done | bytes 262176 | tf_op jit(solution)/shard_map/all_to_all | solution.py:473
  94.3 5.8 %collective-permute-start.10 = (f32[4,128,128]{2,1,0:T(8,128)S(1)}, f32[4,128,128]{2,1,0:T(8,128)S(1)}, u32[]{:S(2)}, u32[]{:S(2)}) collective-permute-start(f32[4,128,128]{2,1,0:T(8,128)S(1)} %bitcast.6), channel_id=1, source_target_pairs={{0,16},{16,0},{1,17},{17,1},{2,18},{18,2},{3,19},{19,3},{4,20},{20... | collective-permute-start | bytes 786440 | tf_op jit(solution)/shard_map/ppermute | solution.py:476
  100.1 0.8 shard_map.87
  101.3 0.7 shard_map.88
  (26 shorter events, 4.3 us)
Async XLA Ops:
  0.6 0.7 copy-start.4
  1.3 12.1 %copy-start.2 = (f32[2,2,64,256]{3,2,1,0:T(8,128)S(1)}, f32[2,2,64,256]{3,2,1,0:T(8,128)}, u32[]{:S(2)}) copy-start(f32[2,2,64,256]{3,2,1,0:T(8,128)} %own.3) | copy-start | bytes 786436
  1.4 18.6 %collective-permute-start = (f32[136,128]{1,0:T(8,128)S(1)}, f32[136,128]{1,0:T(8,128)S(1)}, u32[]{:S(2)}, u32[]{:S(2)}) collective-permute-start(f32[136,128]{1,0:T(8,128)S(1)} %get-tuple-element.26), channel_id=1, source_target_pairs={{16,32},{48,64},{80,96},{112,128},{144,160},{176,192},{208,224},{2... | collective-permute-start | bytes 208904 | tf_op jit(solution)/shard_map/ppermute | solution.py:417
  13.5 6.4 %collective-permute-start.1 = (f32[2,64,128]{2,1,0:T(8,128)S(1)}, f32[2,64,128]{2,1,0:T(8,128)S(1)}, u32[]{:S(2)}, u32[]{:S(2)}) collective-permute-start(f32[2,64,128]{2,1,0:T(8,128)S(1)} %get-tuple-element.27), channel_id=1, source_target_pairs={{0,1},{2,3},{4,5},{6,7},{8,9},{10,11},{12,13},{14,15},{1,0},{3,2},... | collective-permute-start | bytes 196616 | tf_op jit(solution)/shard_map/ppermute | solution.py:418
  16.6 3.3 %collective-permute-start.2 = (f32[2,64,128]{2,1,0:T(8,128)S(1)}, f32[2,64,128]{2,1,0:T(8,128)S(1)}, u32[]{:S(2)}, u32[]{:S(2)}) collective-permute-start(f32[2,64,128]{2,1,0:T(8,128)S(1)} %get-tuple-element.28), channel_id=1, source_target_pairs={{1,2},{3,4},{5,6},{7,8},{9,10},{11,12},{13,14},{2,1},{4,3},{6,5},{... | collective-permute-start | bytes 196616 | tf_op jit(solution)/shard_map/ppermute | solution.py:419
  17.3 9.1 %copy-start = (f32[2,4,128,128]{3,2,1,0:T(8,128)S(1)}, f32[2,4,128,128]{3,2,1,0:T(8,128)}, u32[]{:S(2)}) copy-start(f32[2,4,128,128]{3,2,1,0:T(8,128)} %probe.3) | copy-start | bytes 1572868
  17.3 6.2 %collective-permute-start.3 = (f32[8,128]{1,0:T(8,128)S(1)}, f32[8,128]{1,0:T(8,128)S(1)}, u32[]{:S(2)}, u32[]{:S(2)}) collective-permute-start(f32[8,128]{1,0:T(8,128)S(1)} %get-tuple-element.30), channel_id=1, source_target_pairs={{0,16},{16,0},{1,17},{17,1},{2,18},{18,2},{3,19},{19,3},{4,20},{20... | collective-permute-start | bytes 12296 | tf_op jit(solution)/shard_map/ppermute | solution.py:420
  20.2 6.1 %copy-start.1 = (bf16[12,128,128]{2,1,0:T(8,128)(2,1)S(1)}, bf16[12,128,128]{2,1,0:T(8,128)(2,1)}, u32[]{:S(2)}) copy-start(bf16[12,128,128]{2,1,0:T(8,128)(2,1)} %constant.2.clone.tabs) | copy-start | bytes 1179652
  20.2 10.4 %collective-permute-start.5 = (f32[264,128]{1,0:T(8,128)S(1)}, f32[264,128]{1,0:T(8,128)S(1)}, u32[]{:S(2)}, u32[]{:S(2)}) collective-permute-start(f32[264,128]{1,0:T(8,128)S(1)} %get-tuple-element.31), channel_id=1, source_target_pairs={{16,32},{48,64},{80,96},{112,128},{144,160},{176,192},{208,224},{2... | collective-permute-start | bytes 405512 | tf_op jit(solution)/shard_map/ppermute | solution.py:424
  23.5 2.9 %copy-start.3 = (f32[1,1,1,128,128]{4,3,2,1,0:T(8,128)S(1)}, f32[1,1,1,128,128]{4,3,2,1,0:T(8,128)}, u32[]{:S(2)}) copy-start(f32[1,1,1,128,128]{4,3,2,1,0:T(8,128)} %pattern.3) | copy-start | bytes 196612
  23.8 3.3 %collective-permute-start.4 = (f32[256,128]{1,0:T(8,128)S(1)}, f32[256,128]{1,0:T(8,128)S(1)}, u32[]{:S(2)}, u32[]{:S(2)}) collective-permute-start(f32[256,128]{1,0:T(8,128)S(1)} %shard_map.81), channel_id=1, source_target_pairs={{0,16},{16,0},{1,17},{17,1},{2,18},{18,2},{3,19},{19,3},{4,20},{20... | collective-permute-start | bytes 393224 | tf_op jit(solution)/shard_map/ppermute | solution.py:426
  34.3 3.6 %collective-permute-start.6 = (f32[776,128]{1,0:T(8,128)S(1)}, f32[776,128]{1,0:T(8,128)S(1)}, u32[]{:S(2)}, u32[]{:S(2)}) collective-permute-start(f32[776,128]{1,0:T(8,128)S(1)} %get-tuple-element.36), channel_id=1, source_target_pairs={{0,16},{16,0},{1,17},{17,1},{2,18},{18,2},{3,19},{19,3},{4,20},{20... | collective-permute-start | bytes 1191944 | tf_op jit(solution)/shard_map/ppermute | solution.py:447
  38.7 23.7 %all-to-all-start = ((f32[32,16,128]{2,1,0:T(8,128)}), f32[32,16,128]{2,1,0:T(8,128)S(1)}, u32[]{:S(2)}, u32[]{:S(2)}) async-start(f32[32,16,128]{2,1,0:T(8,128)} %bitcast.3), calls=%async_computation | async-start | bytes 524288 | tf_op jit(solution)/shard_map/all_to_all | solution.py:456
  52.6 17.6 %collective-permute-start.7 = (f32[264,128]{1,0:T(8,128)S(1)}, f32[264,128]{1,0:T(8,128)S(1)}, u32[]{:S(2)}, u32[]{:S(2)}) collective-permute-start(f32[264,128]{1,0:T(8,128)S(1)} %get-tuple-element.37), channel_id=1, source_target_pairs={{16,32},{48,64},{80,96},{112,128},{144,160},{176,192},{208,224},{2... | collective-permute-start | bytes 405512 | tf_op jit(solution)/shard_map/ppermute | solution.py:448
  63.0 14.4 %all-to-all-start.1 = ((f32[8,16,128]{2,1,0:T(8,128)}), f32[8,16,128]{2,1,0:T(8,128)S(1)}, u32[]{:S(2)}, u32[]{:S(2)}) async-start(f32[8,16,128]{2,1,0:T(8,128)} %shard_map.85), calls=%async_computation.1 | async-start | bytes 131072 | tf_op jit(solution)/shard_map/all_to_all | solution.py:468
  71.2 7.0 %collective-permute-start.8 = (f32[2,64,128]{2,1,0:T(8,128)S(1)}, f32[2,64,128]{2,1,0:T(8,128)S(1)}, u32[]{:S(2)}, u32[]{:S(2)}) collective-permute-start(f32[2,64,128]{2,1,0:T(8,128)S(1)} %get-tuple-element.40), channel_id=1, source_target_pairs={{0,1},{2,3},{4,5},{6,7},{8,9},{10,11},{12,13},{14,15},{1,0},{3,2},... | collective-permute-start | bytes 196616 | tf_op jit(solution)/shard_map/ppermute | solution.py:470
  78.2 16.1 %all-to-all-start.2 = ((f32[32,16,128]{2,1,0:T(8,128)}), f32[32,16,128]{2,1,0:T(8,128)S(1)}, u32[]{:S(2)}, u32[]{:S(2)}) async-start(f32[32,16,128]{2,1,0:T(8,128)} %shard_map.86), calls=%async_computation.2 | async-start | bytes 524288 | tf_op jit(solution)/shard_map/all_to_all | solution.py:473
  84.4 0.7 collective-permute-start.9
  94.3 7.0 %collective-permute-start.10 = (f32[4,128,128]{2,1,0:T(8,128)S(1)}, f32[4,128,128]{2,1,0:T(8,128)S(1)}, u32[]{:S(2)}, u32[]{:S(2)}) collective-permute-start(f32[4,128,128]{2,1,0:T(8,128)S(1)} %bitcast.6), channel_id=1, source_target_pairs={{0,16},{16,0},{1,17},{17,1},{2,18},{18,2},{3,19},{19,3},{4,20},{20... | collective-permute-start | bytes 786440 | tf_op jit(solution)/shard_map/ppermute | solution.py:476

commit v11 on v10

--- a/solution.py
+++ b/solution.py
@@ -411,7 +411,7 @@
     edge = shape(2, rows, side)
     large = pl.CostEstimate(flops=4_000_000_000, bytes_accessed=0, transcendentals=0)
     column, column_near = call(
-        column_kernel, [shape(136, side), shape(8, side)], 0, 1, cost=large
+        column_kernel, [shape(8, side), shape(8, side)], 0, 1, cost=large
     )(scan.reshape(1, 2))
     to_even, to_odd = call(edges_kernel, [edge, edge], 0, 1)(obj_field)
     column = lax.ppermute(column, ROW, pairs)

time: 103 us -> 103 us (level)
  waiting for transfers between devices: 19.8 us -> 15.6 us
  starting transfers between devices: 70.2 us -> 74 us
    ppermute x1, starting transfers between devices: 3.23 us -> 6.86 us  [body(): beyond = lax.ppermute(to_beyond, ROW, pairs)]
    ppermute x1, waiting for transfers between devices: 3.52 us -> 0.01 us  [body(): beyond = lax.ppermute(to_beyond, ROW, pairs)]
    ppermute x1, starting transfers between devices: 3.1 us -> 4.83 us  [body(): with_even = lax.ppermute(to_even, COL, even_pairs)]
    all_to_all x1, starting transfers between devices: 13.9 us -> 15.5 us  [body(): lax.all_to_all(summed.reshape(n_yx, chunk, side), EVERY, 0, 0, axis_index...]
    ppermute x1, starting transfers between devices: 12 us -> 10.6 us  [body(): column = lax.ppermute(column, ROW, pairs)]
    all_to_all x1, starting transfers between devices: 6.19 us -> 4.89 us  [body(): whole = lax.all_to_all(part, EVERY, 0, 0, axis_index_groups=planes)]
  transfers between devices with their start and end apart: 14 -> 14, of which waited for: 7 -> 5; matrix products, arithmetic and copies ran while one was open for 0% -> 0% of each run, Pallas kernels for 4% -> 4%
where the time goes in v11:
time: 103 us; the launch traced here: 102 us
  starting transfers between devices  74 us (72%)
  waiting for transfers between devices  15.6 us (15%)
  Pallas kernels  9.8 us (10%)
  between operations  1.58 us (2%)
    all_to_all x1, starting transfers between devices, body(): lax.all_to_all(summed.reshape(n_yx, chunk, side), EVERY, 0, 0, axis_index...  15.5 us
    ppermute x1, starting transfers between devices, body(): column = lax.ppermute(column, ROW, pairs)  10.6 us
    all_to_all x1, waiting for transfers between devices, body(): whole = lax.all_to_all(part, EVERY, 0, 0, axis_index_groups=planes)  9.17 us
    ppermute x1, starting transfers between devices, body(): from_beyond = lax.ppermute(message_beyond, ROW, pairs)  7.55 us
    ppermute x1, starting transfers between devices, body(): beyond = lax.ppermute(to_beyond, ROW, pairs)  6.86 us
    all_to_all x1, starting transfers between devices, body(): part = lax.all_to_all(part, EVERY, 0, 0, axis_index_groups=lines)  6.38 us
    ppermute x1, starting transfers between devices, body(): facing = lax.ppermute(whole, 'core', swap)  6.11 us
    all_to_all x1, starting transfers between devices, body(): whole = lax.all_to_all(part, EVERY, 0, 0, axis_index_groups=planes)  4.89 us
  transfers between devices with their start and end apart: 14, of which 5 were waited for; matrix products, arithmetic and copies ran while one was open for 0% of the time, Pallas kernels for 4%

profile of v11, /device:TPU:1, one launch (start us, length us, event | category | flops | bytes accessed | tf_op | source)
XLA Modules:
  0.0 101.9 jit_solution(4260101764246395445)
XLA Ops:
  0.6 0.9 copy-done.2
  1.7 4.8 %collective-permute-start.1 = (f32[2,64,128]{2,1,0:T(8,128)S(1)}, f32[2,64,128]{2,1,0:T(8,128)S(1)}, u32[]{:S(2)}, u32[]{:S(2)}) collective-permute-start(f32[2,64,128]{2,1,0:T(8,128)S(1)} %get-tuple-element.27), channel_id=1, source_target_pairs={{0,1},{2,3},{4,5},{6,7},{8,9},{10,11},{12,13},{14,15},{1,0},{3,2},... | collective-permute-start | bytes 196616 | tf_op jit(solution)/shard_map/ppermute | solution.py:418
  7.3 10.6 %collective-permute-start = (f32[8,128]{1,0:T(8,128)S(1)}, f32[8,128]{1,0:T(8,128)S(1)}, u32[]{:S(2)}, u32[]{:S(2)}) collective-permute-start(f32[8,128]{1,0:T(8,128)S(1)} %get-tuple-element.26), channel_id=1, source_target_pairs={{16,32},{48,64},{80,96},{112,128},{144,160},{176,192},{208,224},{2... | collective-permute-start | bytes 12296 | tf_op jit(solution)/shard_map/ppermute | solution.py:417
  17.9 2.1 %collective-permute-start.3 = (f32[8,128]{1,0:T(8,128)S(1)}, f32[8,128]{1,0:T(8,128)S(1)}, u32[]{:S(2)}, u32[]{:S(2)}) collective-permute-start(f32[8,128]{1,0:T(8,128)S(1)} %get-tuple-element.30), channel_id=1, source_target_pairs={{0,16},{16,0},{1,17},{17,1},{2,18},{18,2},{3,19},{19,3},{4,20},{20... | collective-permute-start | bytes 12296 | tf_op jit(solution)/shard_map/ppermute | solution.py:420
  20.3 6.9 %collective-permute-start.5 = (f32[264,128]{1,0:T(8,128)S(1)}, f32[264,128]{1,0:T(8,128)S(1)}, u32[]{:S(2)}, u32[]{:S(2)}) collective-permute-start(f32[264,128]{1,0:T(8,128)S(1)} %get-tuple-element.31), channel_id=1, source_target_pairs={{16,32},{48,64},{80,96},{112,128},{144,160},{176,192},{208,224},{2... | collective-permute-start | bytes 405512 | tf_op jit(solution)/shard_map/ppermute | solution.py:424
  27.5 1.9 %collective-permute-start.4 = (f32[256,128]{1,0:T(8,128)S(1)}, f32[256,128]{1,0:T(8,128)S(1)}, u32[]{:S(2)}, u32[]{:S(2)}) collective-permute-start(f32[256,128]{1,0:T(8,128)S(1)} %shard_map.81), channel_id=1, source_target_pairs={{0,16},{16,0},{1,17},{17,1},{2,18},{18,2},{3,19},{19,3},{4,20},{20... | collective-permute-start | bytes 393224 | tf_op jit(solution)/shard_map/ppermute | solution.py:426
  30.1 0.7 shard_map.80.near
  30.8 3.7 %shard_map.82 = (f32[512,128]{1,0:T(8,128)S(1)}, f32[776,128]{1,0:T(8,128)S(1)}, f32[264,128]{1,0:T(8,128)S(1)}, f32[256,128]{1,0:T(8,128)S(1)}) custom-call(s32[2]{0:T(128)S(1)} %bitcast.10, s32[1]{0:T(128)} %bitcast.5.live, f32[256,128]{1,0:T(8,128)S(1)} %shard_map.80.near, f32[256,128]{1,0:T(8,128)S(1)} %collective-permute-done.4.other, ...), custom_call_target="tpu_custom_call" | custom-call | tf_op jit(solution)/shard_map/pallas_call | solution.py:434
  34.5 2.4 %collective-permute-start.6 = (f32[776,128]{1,0:T(8,128)S(1)}, f32[776,128]{1,0:T(8,128)S(1)}, u32[]{:S(2)}, u32[]{:S(2)}) collective-permute-start(f32[776,128]{1,0:T(8,128)S(1)} %get-tuple-element.36), channel_id=1, source_target_pairs={{0,16},{16,0},{1,17},{17,1},{2,18},{18,2},{3,19},{19,3},{4,20},{20... | collective-permute-start | bytes 1191944 | tf_op jit(solution)/shard_map/ppermute | solution.py:447
  37.0 1.3 %collective-permute-done.6.from_core.message = f32[776,128]{1,0:T(8,128)S(1)} collective-permute-done((f32[776,128]{1,0:T(8,128)S(1)}, f32[776,128]{1,0:T(8,128)S(1)}, u32[]{:S(2)}, u32[]{:S(2)}) %collective-permute-start.6) | collective-permute-done | bytes 397344 | tf_op jit(solution)/shard_map/ppermute | solution.py:447
  38.3 0.7 shard_map.84
  39.0 15.5 %all-to-all-start = ((f32[32,16,128]{2,1,0:T(8,128)}), f32[32,16,128]{2,1,0:T(8,128)S(1)}, u32[]{:S(2)}, u32[]{:S(2)}) async-start(f32[32,16,128]{2,1,0:T(8,128)} %bitcast.3), calls=%async_computation | async-start | bytes 524288 | tf_op jit(solution)/shard_map/all_to_all | solution.py:456
  54.6 7.5 %collective-permute-start.7 = (f32[264,128]{1,0:T(8,128)S(1)}, f32[264,128]{1,0:T(8,128)S(1)}, u32[]{:S(2)}, u32[]{:S(2)}) collective-permute-start(f32[264,128]{1,0:T(8,128)S(1)} %get-tuple-element.37), channel_id=1, source_target_pairs={{16,32},{48,64},{80,96},{112,128},{144,160},{176,192},{208,224},{2... | collective-permute-start | bytes 405512 | tf_op jit(solution)/shard_map/ppermute | solution.py:448
  62.1 2.1 %all-to-all-done.parts = f32[32,16,128]{2,1,0:T(8,128)S(1)} async-done(((f32[32,16,128]{2,1,0:T(8,128)}), f32[32,16,128]{2,1,0:T(8,128)S(1)}, u32[]{:S(2)}, u32[]{:S(2)}) %all-to-all-start) | async-done | bytes 262176 | tf_op jit(solution)/shard_map/all_to_all | solution.py:456
  64.9 6.4 %all-to-all-start.1 = ((f32[8,16,128]{2,1,0:T(8,128)}), f32[8,16,128]{2,1,0:T(8,128)S(1)}, u32[]{:S(2)}, u32[]{:S(2)}) async-start(f32[8,16,128]{2,1,0:T(8,128)} %shard_map.85), calls=%async_computation.1 | async-start | bytes 131072 | tf_op jit(solution)/shard_map/all_to_all | solution.py:468
  71.3 0.9 shard_map.83
  72.2 3.6 %collective-permute-start.8 = (f32[2,64,128]{2,1,0:T(8,128)S(1)}, f32[2,64,128]{2,1,0:T(8,128)S(1)}, u32[]{:S(2)}, u32[]{:S(2)}) collective-permute-start(f32[2,64,128]{2,1,0:T(8,128)S(1)} %get-tuple-element.40), channel_id=1, source_target_pairs={{0,1},{2,3},{4,5},{6,7},{8,9},{10,11},{12,13},{14,15},{1,0},{3,2},... | collective-permute-start | bytes 196616 | tf_op jit(solution)/shard_map/ppermute | solution.py:470
  75.8 2.7 %all-to-all-done.1.parts = f32[8,16,128]{2,1,0:T(8,128)S(1)} async-done(((f32[8,16,128]{2,1,0:T(8,128)}), f32[8,16,128]{2,1,0:T(8,128)S(1)}, u32[]{:S(2)}, u32[]{:S(2)}) %all-to-all-start.1) | async-done | bytes 65568 | tf_op jit(solution)/shard_map/all_to_all | solution.py:468
  78.5 0.7 shard_map.86
  79.2 4.9 %all-to-all-start.2 = ((f32[32,16,128]{2,1,0:T(8,128)}), f32[32,16,128]{2,1,0:T(8,128)S(1)}, u32[]{:S(2)}, u32[]{:S(2)}) async-start(f32[32,16,128]{2,1,0:T(8,128)} %shard_map.86), calls=%async_computation.2 | async-start | bytes 524288 | tf_op jit(solution)/shard_map/all_to_all | solution.py:473
  84.8 9.2 %all-to-all-done.2 = f32[32,16,128]{2,1,0:T(8,128)S(1)} async-done(((f32[32,16,128]{2,1,0:T(8,128)}), f32[32,16,128]{2,1,0:T(8,128)S(1)}, u32[]{:S(2)}, u32[]{:S(2)}) %all-to-all-start.2) | async-done | bytes 262176 | tf_op jit(solution)/shard_map/all_to_all | solution.py:473
  94.0 6.1 %collective-permute-start.10 = (f32[4,128,128]{2,1,0:T(8,128)S(1)}, f32[4,128,128]{2,1,0:T(8,128)S(1)}, u32[]{:S(2)}, u32[]{:S(2)}) collective-permute-start(f32[4,128,128]{2,1,0:T(8,128)S(1)} %bitcast.6), channel_id=1, source_target_pairs={{0,16},{16,0},{1,17},{17,1},{2,18},{18,2},{3,19},{19,3},{4,20},{20... | collective-permute-start | bytes 786440 | tf_op jit(solution)/shard_map/ppermute | solution.py:476
  100.1 0.8 shard_map.87
  101.2 0.7 shard_map.88
  (28 shorter events, 3.1 us)
Async XLA Ops:
  0.6 1.0 copy-start.2
  1.7 18.3 %collective-permute-start.1 = (f32[2,64,128]{2,1,0:T(8,128)S(1)}, f32[2,64,128]{2,1,0:T(8,128)S(1)}, u32[]{:S(2)}, u32[]{:S(2)}) collective-permute-start(f32[2,64,128]{2,1,0:T(8,128)S(1)} %get-tuple-element.27), channel_id=1, source_target_pairs={{0,1},{2,3},{4,5},{6,7},{8,9},{10,11},{12,13},{14,15},{1,0},{3,2},... | collective-permute-start | bytes 196616 | tf_op jit(solution)/shard_map/ppermute | solution.py:418
  6.5 0.7 copy-start.5
  6.5 13.4 %collective-permute-start.2 = (f32[2,64,128]{2,1,0:T(8,128)S(1)}, f32[2,64,128]{2,1,0:T(8,128)S(1)}, u32[]{:S(2)}, u32[]{:S(2)}) collective-permute-start(f32[2,64,128]{2,1,0:T(8,128)S(1)} %get-tuple-element.28), channel_id=1, source_target_pairs={{1,2},{3,4},{5,6},{7,8},{9,10},{11,12},{13,14},{2,1},{4,3},{6,5},{... | collective-permute-start | bytes 196616 | tf_op jit(solution)/shard_map/ppermute | solution.py:419
  7.2 12.8 %copy-start.3 = (f32[2,2,64,256]{3,2,1,0:T(8,128)S(1)}, f32[2,2,64,256]{3,2,1,0:T(8,128)}, u32[]{:S(2)}) copy-start(f32[2,2,64,256]{3,2,1,0:T(8,128)} %own.3) | copy-start | bytes 786436
  7.3 12.6 %collective-permute-start = (f32[8,128]{1,0:T(8,128)S(1)}, f32[8,128]{1,0:T(8,128)S(1)}, u32[]{:S(2)}, u32[]{:S(2)}) collective-permute-start(f32[8,128]{1,0:T(8,128)S(1)} %get-tuple-element.26), channel_id=1, source_target_pairs={{16,32},{48,64},{80,96},{112,128},{144,160},{176,192},{208,224},{2... | collective-permute-start | bytes 12296 | tf_op jit(solution)/shard_map/ppermute | solution.py:417
  17.9 12.2 %copy-start = (f32[2,4,128,128]{3,2,1,0:T(8,128)S(1)}, f32[2,4,128,128]{3,2,1,0:T(8,128)}, u32[]{:S(2)}) copy-start(f32[2,4,128,128]{3,2,1,0:T(8,128)} %probe.3) | copy-start | bytes 1572868
  17.9 9.3 %collective-permute-start.3 = (f32[8,128]{1,0:T(8,128)S(1)}, f32[8,128]{1,0:T(8,128)S(1)}, u32[]{:S(2)}, u32[]{:S(2)}) collective-permute-start(f32[8,128]{1,0:T(8,128)S(1)} %get-tuple-element.30), channel_id=1, source_target_pairs={{0,16},{16,0},{1,17},{17,1},{2,18},{18,2},{3,19},{19,3},{4,20},{20... | collective-permute-start | bytes 12296 | tf_op jit(solution)/shard_map/ppermute | solution.py:420
  20.3 9.8 %copy-start.1 = (bf16[12,128,128]{2,1,0:T(8,128)(2,1)S(1)}, bf16[12,128,128]{2,1,0:T(8,128)(2,1)}, u32[]{:S(2)}) copy-start(bf16[12,128,128]{2,1,0:T(8,128)(2,1)} %constant.2.clone.tabs) | copy-start | bytes 1179652
  20.3 10.5 %collective-permute-start.5 = (f32[264,128]{1,0:T(8,128)S(1)}, f32[264,128]{1,0:T(8,128)S(1)}, u32[]{:S(2)}, u32[]{:S(2)}) collective-permute-start(f32[264,128]{1,0:T(8,128)S(1)} %get-tuple-element.31), channel_id=1, source_target_pairs={{16,32},{48,64},{80,96},{112,128},{144,160},{176,192},{208,224},{2... | collective-permute-start | bytes 405512 | tf_op jit(solution)/shard_map/ppermute | solution.py:424
  27.2 2.9 %copy-start.4 = (f32[1,1,1,128,128]{4,3,2,1,0:T(8,128)S(1)}, f32[1,1,1,128,128]{4,3,2,1,0:T(8,128)}, u32[]{:S(2)}) copy-start(f32[1,1,1,128,128]{4,3,2,1,0:T(8,128)} %pattern.3) | copy-start | bytes 196612
  27.5 3.3 %collective-permute-start.4 = (f32[256,128]{1,0:T(8,128)S(1)}, f32[256,128]{1,0:T(8,128)S(1)}, u32[]{:S(2)}, u32[]{:S(2)}) collective-permute-start(f32[256,128]{1,0:T(8,128)S(1)} %shard_map.81), channel_id=1, source_target_pairs={{0,16},{16,0},{1,17},{17,1},{2,18},{18,2},{3,19},{19,3},{4,20},{20... | collective-permute-start | bytes 393224 | tf_op jit(solution)/shard_map/ppermute | solution.py:426
  34.5 3.8 %collective-permute-start.6 = (f32[776,128]{1,0:T(8,128)S(1)}, f32[776,128]{1,0:T(8,128)S(1)}, u32[]{:S(2)}, u32[]{:S(2)}) collective-permute-start(f32[776,128]{1,0:T(8,128)S(1)} %get-tuple-element.36), channel_id=1, source_target_pairs={{0,16},{16,0},{1,17},{17,1},{2,18},{18,2},{3,19},{19,3},{4,20},{20... | collective-permute-start | bytes 1191944 | tf_op jit(solution)/shard_map/ppermute | solution.py:447
  39.0 25.2 %all-to-all-start = ((f32[32,16,128]{2,1,0:T(8,128)}), f32[32,16,128]{2,1,0:T(8,128)S(1)}, u32[]{:S(2)}, u32[]{:S(2)}) async-start(f32[32,16,128]{2,1,0:T(8,128)} %bitcast.3), calls=%async_computation | async-start | bytes 524288 | tf_op jit(solution)/shard_map/all_to_all | solution.py:456
  54.6 16.7 %collective-permute-start.7 = (f32[264,128]{1,0:T(8,128)S(1)}, f32[264,128]{1,0:T(8,128)S(1)}, u32[]{:S(2)}, u32[]{:S(2)}) collective-permute-start(f32[264,128]{1,0:T(8,128)S(1)} %get-tuple-element.37), channel_id=1, source_target_pairs={{16,32},{48,64},{80,96},{112,128},{144,160},{176,192},{208,224},{2... | collective-permute-start | bytes 405512 | tf_op jit(solution)/shard_map/ppermute | solution.py:448
  64.9 13.6 %all-to-all-start.1 = ((f32[8,16,128]{2,1,0:T(8,128)}), f32[8,16,128]{2,1,0:T(8,128)S(1)}, u32[]{:S(2)}, u32[]{:S(2)}) async-start(f32[8,16,128]{2,1,0:T(8,128)} %shard_map.85), calls=%async_computation.1 | async-start | bytes 131072 | tf_op jit(solution)/shard_map/all_to_all | solution.py:468
  72.2 7.0 %collective-permute-start.8 = (f32[2,64,128]{2,1,0:T(8,128)S(1)}, f32[2,64,128]{2,1,0:T(8,128)S(1)}, u32[]{:S(2)}, u32[]{:S(2)}) collective-permute-start(f32[2,64,128]{2,1,0:T(8,128)S(1)} %get-tuple-element.40), channel_id=1, source_target_pairs={{0,1},{2,3},{4,5},{6,7},{8,9},{10,11},{12,13},{14,15},{1,0},{3,2},... | collective-permute-start | bytes 196616 | tf_op jit(solution)/shard_map/ppermute | solution.py:470
  79.2 14.8 %all-to-all-start.2 = ((f32[32,16,128]{2,1,0:T(8,128)}), f32[32,16,128]{2,1,0:T(8,128)S(1)}, u32[]{:S(2)}, u32[]{:S(2)}) async-start(f32[32,16,128]{2,1,0:T(8,128)} %shard_map.86), calls=%async_computation.2 | async-start | bytes 524288 | tf_op jit(solution)/shard_map/all_to_all | solution.py:473
  84.1 0.7 collective-permute-start.9
  94.0 7.3 %collective-permute-start.10 = (f32[4,128,128]{2,1,0:T(8,128)S(1)}, f32[4,128,128]{2,1,0:T(8,128)S(1)}, u32[]{:S(2)}, u32[]{:S(2)}) collective-permute-start(f32[4,128,128]{2,1,0:T(8,128)S(1)} %bitcast.6), channel_id=1, source_target_pairs={{0,16},{16,0},{1,17},{17,1},{2,18},{18,2},{3,19},{19,3},{4,20},{20... | collective-permute-start | bytes 786440 | tf_op jit(solution)/shard_map/ppermute | solution.py:476

commit v12 on v10

--- a/solution.py
+++ b/solution.py
@@ -384,7 +384,7 @@
         return flat
 
     planes = [[index(x, y, z, 0) for x in range(n_x) for y in range(n_y)] for z in range(n_z)]
-    planes += [[index(x, y, z, 1) for x in range(n_x) for z in range(n_z)] for y in range(n_y)]
+    planes += [[index(x, y, z, 1) for z in range(n_z) for x in range(n_x)] for y in range(n_y)]
     lines = [[index(x, y, z, 0) for z in range(n_z)] for x in range(n_x) for y in range(n_y)]
     lines += [[index(x, y, z, 1) for y in range(n_y)] for x in range(n_x) for z in range(n_z)]
     return planes, lines

time: 103 us -> 103 us (level)
  starting transfers between devices: 70.2 us -> 68.3 us
  waiting for transfers between devices: 19.8 us -> 21.6 us
where the time goes in v12:
time: 103 us; the launch traced here: 102 us
  starting transfers between devices  68.3 us (66%)
  waiting for transfers between devices  21.6 us (21%)
  Pallas kernels  9.79 us (10%)
  between operations  1.53 us (1%)
    all_to_all x1, starting transfers between devices, body(): lax.all_to_all(summed.reshape(n_yx, chunk, side), EVERY, 0, 0, axis_index...  13.9 us
    ppermute x1, starting transfers between devices, body(): column = lax.ppermute(column, ROW, pairs)  12 us
    all_to_all x1, waiting for transfers between devices, body(): whole = lax.all_to_all(part, EVERY, 0, 0, axis_index_groups=planes)  9.72 us
    ppermute x1, starting transfers between devices, body(): from_beyond = lax.ppermute(message_beyond, ROW, pairs)  8.19 us
    all_to_all x1, starting transfers between devices, body(): part = lax.all_to_all(part, EVERY, 0, 0, axis_index_groups=lines)  7.03 us
    all_to_all x1, starting transfers between devices, body(): whole = lax.all_to_all(part, EVERY, 0, 0, axis_index_groups=planes)  5.68 us
    ppermute x1, starting transfers between devices, body(): facing = lax.ppermute(whole, 'core', swap)  5.31 us
    pallas_call x1, Pallas kernels, body(): call(main_kernel, [shape(modes * side, side), shape(modes * side + strip...  3.75 us
  transfers between devices with their start and end apart: 14, of which 7 were waited for; matrix products, arithmetic and copies ran while one was open for 0% of the time, Pallas kernels for 4%

profile of v12, /device:TPU:1, one launch (start us, length us, event | category | flops | bytes accessed | tf_op | source)
XLA Modules:
  0.0 102.0 jit_solution(12658957225814829301)
XLA Ops:
  1.4 12.0 %collective-permute-start = (f32[136,128]{1,0:T(8,128)S(1)}, f32[136,128]{1,0:T(8,128)S(1)}, u32[]{:S(2)}, u32[]{:S(2)}) collective-permute-start(f32[136,128]{1,0:T(8,128)S(1)} %get-tuple-element.26), channel_id=1, source_target_pairs={{16,32},{48,64},{80,96},{112,128},{144,160},{176,192},{208,224},{2... | collective-permute-start | bytes 208904 | tf_op jit(solution)/shard_map/ppermute | solution.py:417
  13.5 3.1 %collective-permute-start.1 = (f32[2,64,128]{2,1,0:T(8,128)S(1)}, f32[2,64,128]{2,1,0:T(8,128)S(1)}, u32[]{:S(2)}, u32[]{:S(2)}) collective-permute-start(f32[2,64,128]{2,1,0:T(8,128)S(1)} %get-tuple-element.27), channel_id=1, source_target_pairs={{0,1},{2,3},{4,5},{6,7},{8,9},{10,11},{12,13},{14,15},{1,0},{3,2},... | collective-permute-start | bytes 196616 | tf_op jit(solution)/shard_map/ppermute | solution.py:418
  17.3 2.1 %collective-permute-start.3 = (f32[8,128]{1,0:T(8,128)S(1)}, f32[8,128]{1,0:T(8,128)S(1)}, u32[]{:S(2)}, u32[]{:S(2)}) collective-permute-start(f32[8,128]{1,0:T(8,128)S(1)} %get-tuple-element.30), channel_id=1, source_target_pairs={{0,16},{16,0},{1,17},{17,1},{2,18},{18,2},{3,19},{19,3},{4,20},{20... | collective-permute-start | bytes 12296 | tf_op jit(solution)/shard_map/ppermute | solution.py:420
  20.2 3.2 %collective-permute-start.5 = (f32[264,128]{1,0:T(8,128)S(1)}, f32[264,128]{1,0:T(8,128)S(1)}, u32[]{:S(2)}, u32[]{:S(2)}) collective-permute-start(f32[264,128]{1,0:T(8,128)S(1)} %get-tuple-element.31), channel_id=1, source_target_pairs={{16,32},{48,64},{80,96},{112,128},{144,160},{176,192},{208,224},{2... | collective-permute-start | bytes 405512 | tf_op jit(solution)/shard_map/ppermute | solution.py:424
  23.8 1.9 %collective-permute-start.4 = (f32[256,128]{1,0:T(8,128)S(1)}, f32[256,128]{1,0:T(8,128)S(1)}, u32[]{:S(2)}, u32[]{:S(2)}) collective-permute-start(f32[256,128]{1,0:T(8,128)S(1)} %shard_map.81), channel_id=1, source_target_pairs={{0,16},{16,0},{1,17},{17,1},{2,18},{18,2},{3,19},{19,3},{4,20},{20... | collective-permute-start | bytes 393224 | tf_op jit(solution)/shard_map/ppermute | solution.py:426
  26.4 0.7 shard_map.80.near
  27.1 3.5 %collective-permute-done.5.beyond = f32[264,128]{1,0:T(8,128)S(1)} collective-permute-done((f32[264,128]{1,0:T(8,128)S(1)}, f32[264,128]{1,0:T(8,128)S(1)}, u32[]{:S(2)}, u32[]{:S(2)}) %collective-permute-start.5) | collective-permute-done | bytes 135200 | tf_op jit(solution)/shard_map/ppermute | solution.py:424
  30.6 3.7 %shard_map.82 = (f32[512,128]{1,0:T(8,128)S(1)}, f32[776,128]{1,0:T(8,128)S(1)}, f32[264,128]{1,0:T(8,128)S(1)}, f32[256,128]{1,0:T(8,128)S(1)}) custom-call(s32[2]{0:T(128)S(1)} %bitcast.10, s32[1]{0:T(128)} %bitcast.5.live, f32[256,128]{1,0:T(8,128)S(1)} %shard_map.80.near, f32[256,128]{1,0:T(8,128)S(1)} %collective-permute-done.4.other, ...), custom_call_target="tpu_custom_call" | custom-call | tf_op jit(solution)/shard_map/pallas_call | solution.py:434
  34.4 1.9 %collective-permute-start.6 = (f32[776,128]{1,0:T(8,128)S(1)}, f32[776,128]{1,0:T(8,128)S(1)}, u32[]{:S(2)}, u32[]{:S(2)}) collective-permute-start(f32[776,128]{1,0:T(8,128)S(1)} %get-tuple-element.36), channel_id=1, source_target_pairs={{0,16},{16,0},{1,17},{17,1},{2,18},{18,2},{3,19},{19,3},{4,20},{20... | collective-permute-start | bytes 1191944 | tf_op jit(solution)/shard_map/ppermute | solution.py:447
  36.3 1.7 %collective-permute-done.6.from_core.message = f32[776,128]{1,0:T(8,128)S(1)} collective-permute-done((f32[776,128]{1,0:T(8,128)S(1)}, f32[776,128]{1,0:T(8,128)S(1)}, u32[]{:S(2)}, u32[]{:S(2)}) %collective-permute-start.6) | collective-permute-done | bytes 397344 | tf_op jit(solution)/shard_map/ppermute | solution.py:447
  38.0 0.7 shard_map.84
  38.7 13.9 %all-to-all-start = ((f32[32,16,128]{2,1,0:T(8,128)}), f32[32,16,128]{2,1,0:T(8,128)S(1)}, u32[]{:S(2)}, u32[]{:S(2)}) async-start(f32[32,16,128]{2,1,0:T(8,128)} %bitcast.3), calls=%async_computation | async-start | bytes 524288 | tf_op jit(solution)/shard_map/all_to_all | solution.py:456
  52.6 8.2 %collective-permute-start.7 = (f32[264,128]{1,0:T(8,128)S(1)}, f32[264,128]{1,0:T(8,128)S(1)}, u32[]{:S(2)}, u32[]{:S(2)}) collective-permute-start(f32[264,128]{1,0:T(8,128)S(1)} %get-tuple-element.37), channel_id=1, source_target_pairs={{16,32},{48,64},{80,96},{112,128},{144,160},{176,192},{208,224},{2... | collective-permute-start | bytes 405512 | tf_op jit(solution)/shard_map/ppermute | solution.py:448
  60.8 2.2 %all-to-all-done.parts = f32[32,16,128]{2,1,0:T(8,128)S(1)} async-done(((f32[32,16,128]{2,1,0:T(8,128)}), f32[32,16,128]{2,1,0:T(8,128)S(1)}, u32[]{:S(2)}, u32[]{:S(2)}) %all-to-all-start) | async-done | bytes 262176 | tf_op jit(solution)/shard_map/all_to_all | solution.py:456
  63.7 7.0 %all-to-all-start.1 = ((f32[8,16,128]{2,1,0:T(8,128)}), f32[8,16,128]{2,1,0:T(8,128)S(1)}, u32[]{:S(2)}, u32[]{:S(2)}) async-start(f32[8,16,128]{2,1,0:T(8,128)} %shard_map.85), calls=%async_computation.1 | async-start | bytes 131072 | tf_op jit(solution)/shard_map/all_to_all | solution.py:468
  70.8 0.9 shard_map.83
  71.7 2.6 %collective-permute-start.8 = (f32[2,64,128]{2,1,0:T(8,128)S(1)}, f32[2,64,128]{2,1,0:T(8,128)S(1)}, u32[]{:S(2)}, u32[]{:S(2)}) collective-permute-start(f32[2,64,128]{2,1,0:T(8,128)S(1)} %get-tuple-element.40), channel_id=1, source_target_pairs={{0,1},{2,3},{4,5},{6,7},{8,9},{10,11},{12,13},{14,15},{1,0},{3,2},... | collective-permute-start | bytes 196616 | tf_op jit(solution)/shard_map/ppermute | solution.py:470
  74.4 3.6 %all-to-all-done.1.parts = f32[8,16,128]{2,1,0:T(8,128)S(1)} async-done(((f32[8,16,128]{2,1,0:T(8,128)}), f32[8,16,128]{2,1,0:T(8,128)S(1)}, u32[]{:S(2)}, u32[]{:S(2)}) %all-to-all-start.1) | async-done | bytes 65568 | tf_op jit(solution)/shard_map/all_to_all | solution.py:468
  78.0 0.7 shard_map.86
  78.7 5.7 %all-to-all-start.2 = ((f32[32,16,128]{2,1,0:T(8,128)}), f32[32,16,128]{2,1,0:T(8,128)S(1)}, u32[]{:S(2)}, u32[]{:S(2)}) async-start(f32[32,16,128]{2,1,0:T(8,128)} %shard_map.86), calls=%async_computation.2 | async-start | bytes 524288 | tf_op jit(solution)/shard_map/all_to_all | solution.py:473
  85.1 9.7 %all-to-all-done.2 = f32[32,16,128]{2,1,0:T(8,128)S(1)} async-done(((f32[32,16,128]{2,1,0:T(8,128)}), f32[32,16,128]{2,1,0:T(8,128)S(1)}, u32[]{:S(2)}, u32[]{:S(2)}) %all-to-all-start.2) | async-done | bytes 262176 | tf_op jit(solution)/shard_map/all_to_all | solution.py:473
  94.8 5.3 %collective-permute-start.10 = (f32[4,128,128]{2,1,0:T(8,128)S(1)}, f32[4,128,128]{2,1,0:T(8,128)S(1)}, u32[]{:S(2)}, u32[]{:S(2)}) collective-permute-start(f32[4,128,128]{2,1,0:T(8,128)S(1)} %bitcast.6), channel_id=1, source_target_pairs={{0,16},{16,0},{1,17},{17,1},{2,18},{18,2},{3,19},{19,3},{4,20},{20... | collective-permute-start | bytes 786440 | tf_op jit(solution)/shard_map/ppermute | solution.py:476
  100.1 0.8 shard_map.87
  101.3 0.7 shard_map.88
  (26 shorter events, 4.3 us)
Async XLA Ops:
  0.6 0.7 copy-start.4
  1.3 12.1 %copy-start.2 = (f32[2,2,64,256]{3,2,1,0:T(8,128)S(1)}, f32[2,2,64,256]{3,2,1,0:T(8,128)}, u32[]{:S(2)}) copy-start(f32[2,2,64,256]{3,2,1,0:T(8,128)} %own.3) | copy-start | bytes 786436
  1.4 18.6 %collective-permute-start = (f32[136,128]{1,0:T(8,128)S(1)}, f32[136,128]{1,0:T(8,128)S(1)}, u32[]{:S(2)}, u32[]{:S(2)}) collective-permute-start(f32[136,128]{1,0:T(8,128)S(1)} %get-tuple-element.26), channel_id=1, source_target_pairs={{16,32},{48,64},{80,96},{112,128},{144,160},{176,192},{208,224},{2... | collective-permute-start | bytes 208904 | tf_op jit(solution)/shard_map/ppermute | solution.py:417
  13.5 6.4 %collective-permute-start.1 = (f32[2,64,128]{2,1,0:T(8,128)S(1)}, f32[2,64,128]{2,1,0:T(8,128)S(1)}, u32[]{:S(2)}, u32[]{:S(2)}) collective-permute-start(f32[2,64,128]{2,1,0:T(8,128)S(1)} %get-tuple-element.27), channel_id=1, source_target_pairs={{0,1},{2,3},{4,5},{6,7},{8,9},{10,11},{12,13},{14,15},{1,0},{3,2},... | collective-permute-start | bytes 196616 | tf_op jit(solution)/shard_map/ppermute | solution.py:418
  16.6 3.3 %collective-permute-start.2 = (f32[2,64,128]{2,1,0:T(8,128)S(1)}, f32[2,64,128]{2,1,0:T(8,128)S(1)}, u32[]{:S(2)}, u32[]{:S(2)}) collective-permute-start(f32[2,64,128]{2,1,0:T(8,128)S(1)} %get-tuple-element.28), channel_id=1, source_target_pairs={{1,2},{3,4},{5,6},{7,8},{9,10},{11,12},{13,14},{2,1},{4,3},{6,5},{... | collective-permute-start | bytes 196616 | tf_op jit(solution)/shard_map/ppermute | solution.py:419
  17.3 9.1 %copy-start = (f32[2,4,128,128]{3,2,1,0:T(8,128)S(1)}, f32[2,4,128,128]{3,2,1,0:T(8,128)}, u32[]{:S(2)}) copy-start(f32[2,4,128,128]{3,2,1,0:T(8,128)} %probe.3) | copy-start | bytes 1572868
  17.3 6.2 %collective-permute-start.3 = (f32[8,128]{1,0:T(8,128)S(1)}, f32[8,128]{1,0:T(8,128)S(1)}, u32[]{:S(2)}, u32[]{:S(2)}) collective-permute-start(f32[8,128]{1,0:T(8,128)S(1)} %get-tuple-element.30), channel_id=1, source_target_pairs={{0,16},{16,0},{1,17},{17,1},{2,18},{18,2},{3,19},{19,3},{4,20},{20... | collective-permute-start | bytes 12296 | tf_op jit(solution)/shard_map/ppermute | solution.py:420
  20.2 6.1 %copy-start.1 = (bf16[12,128,128]{2,1,0:T(8,128)(2,1)S(1)}, bf16[12,128,128]{2,1,0:T(8,128)(2,1)}, u32[]{:S(2)}) copy-start(bf16[12,128,128]{2,1,0:T(8,128)(2,1)} %constant.2.clone.tabs) | copy-start | bytes 1179652
  20.2 10.4 %collective-permute-start.5 = (f32[264,128]{1,0:T(8,128)S(1)}, f32[264,128]{1,0:T(8,128)S(1)}, u32[]{:S(2)}, u32[]{:S(2)}) collective-permute-start(f32[264,128]{1,0:T(8,128)S(1)} %get-tuple-element.31), channel_id=1, source_target_pairs={{16,32},{48,64},{80,96},{112,128},{144,160},{176,192},{208,224},{2... | collective-permute-start | bytes 405512 | tf_op jit(solution)/shard_map/ppermute | solution.py:424
  23.5 2.9 %copy-start.3 = (f32[1,1,1,128,128]{4,3,2,1,0:T(8,128)S(1)}, f32[1,1,1,128,128]{4,3,2,1,0:T(8,128)}, u32[]{:S(2)}) copy-start(f32[1,1,1,128,128]{4,3,2,1,0:T(8,128)} %pattern.3) | copy-start | bytes 196612
  23.8 3.3 %collective-permute-start.4 = (f32[256,128]{1,0:T(8,128)S(1)}, f32[256,128]{1,0:T(8,128)S(1)}, u32[]{:S(2)}, u32[]{:S(2)}) collective-permute-start(f32[256,128]{1,0:T(8,128)S(1)} %shard_map.81), channel_id=1, source_target_pairs={{0,16},{16,0},{1,17},{17,1},{2,18},{18,2},{3,19},{19,3},{4,20},{20... | collective-permute-start | bytes 393224 | tf_op jit(solution)/shard_map/ppermute | solution.py:426
  34.4 3.6 %collective-permute-start.6 = (f32[776,128]{1,0:T(8,128)S(1)}, f32[776,128]{1,0:T(8,128)S(1)}, u32[]{:S(2)}, u32[]{:S(2)}) collective-permute-start(f32[776,128]{1,0:T(8,128)S(1)} %get-tuple-element.36), channel_id=1, source_target_pairs={{0,16},{16,0},{1,17},{17,1},{2,18},{18,2},{3,19},{19,3},{4,20},{20... | collective-permute-start | bytes 1191944 | tf_op jit(solution)/shard_map/ppermute | solution.py:447
  38.7 24.3 %all-to-all-start = ((f32[32,16,128]{2,1,0:T(8,128)}), f32[32,16,128]{2,1,0:T(8,128)S(1)}, u32[]{:S(2)}, u32[]{:S(2)}) async-start(f32[32,16,128]{2,1,0:T(8,128)} %bitcast.3), calls=%async_computation | async-start | bytes 524288 | tf_op jit(solution)/shard_map/all_to_all | solution.py:456
  52.6 18.1 %collective-permute-start.7 = (f32[264,128]{1,0:T(8,128)S(1)}, f32[264,128]{1,0:T(8,128)S(1)}, u32[]{:S(2)}, u32[]{:S(2)}) collective-permute-start(f32[264,128]{1,0:T(8,128)S(1)} %get-tuple-element.37), channel_id=1, source_target_pairs={{16,32},{48,64},{80,96},{112,128},{144,160},{176,192},{208,224},{2... | collective-permute-start | bytes 405512 | tf_op jit(solution)/shard_map/ppermute | solution.py:448
  63.7 14.3 %all-to-all-start.1 = ((f32[8,16,128]{2,1,0:T(8,128)}), f32[8,16,128]{2,1,0:T(8,128)S(1)}, u32[]{:S(2)}, u32[]{:S(2)}) async-start(f32[8,16,128]{2,1,0:T(8,128)} %shard_map.85), calls=%async_computation.1 | async-start | bytes 131072 | tf_op jit(solution)/shard_map/all_to_all | solution.py:468
  71.7 7.0 %collective-permute-start.8 = (f32[2,64,128]{2,1,0:T(8,128)S(1)}, f32[2,64,128]{2,1,0:T(8,128)S(1)}, u32[]{:S(2)}, u32[]{:S(2)}) collective-permute-start(f32[2,64,128]{2,1,0:T(8,128)S(1)} %get-tuple-element.40), channel_id=1, source_target_pairs={{0,1},{2,3},{4,5},{6,7},{8,9},{10,11},{12,13},{14,15},{1,0},{3,2},... | collective-permute-start | bytes 196616 | tf_op jit(solution)/shard_map/ppermute | solution.py:470
  78.7 16.1 %all-to-all-start.2 = ((f32[32,16,128]{2,1,0:T(8,128)}), f32[32,16,128]{2,1,0:T(8,128)S(1)}, u32[]{:S(2)}, u32[]{:S(2)}) async-start(f32[32,16,128]{2,1,0:T(8,128)} %shard_map.86), calls=%async_computation.2 | async-start | bytes 524288 | tf_op jit(solution)/shard_map/all_to_all | solution.py:473
  84.4 0.7 collective-permute-start.9
  94.8 6.5 %collective-permute-start.10 = (f32[4,128,128]{2,1,0:T(8,128)S(1)}, f32[4,128,128]{2,1,0:T(8,128)S(1)}, u32[]{:S(2)}, u32[]{:S(2)}) collective-permute-start(f32[4,128,128]{2,1,0:T(8,128)S(1)} %bitcast.6), channel_id=1, source_target_pairs={{0,16},{16,0},{1,17},{17,1},{2,18},{18,2},{3,19},{19,3},{4,20},{20... | collective-permute-start | bytes 786440 | tf_op jit(solution)/shard_map/ppermute | solution.py:476

commit v13 on v10

--- a/solution.py
+++ b/solution.py
@@ -467,8 +467,8 @@
     part = call(sum_kernel, shape(n_z, chunk, side), 0, 1)(spread)
     part = lax.all_to_all(part, EVERY, 0, 0, axis_index_groups=lines)
     part = call(sum_kernel, shape(n_yx, chunk, side), 0, 1)(part)
+    part, grad_even, grad_odd = lax.optimization_barrier((part, grad_even, grad_odd))
     got_even = lax.ppermute(grad_even, COL, even_pairs)
-    part, got_even, grad_odd = lax.optimization_barrier((part, got_even, grad_odd))
     got_odd = lax.ppermute(grad_odd, COL, odd_pairs)
     whole = lax.all_to_all(part, EVERY, 0, 0, axis_index_groups=planes)
     whole, got_even, got_odd = lax.optimization_barrier((whole, got_even, got_odd))

time: 103 us -> 102 us (level)
  starting transfers between devices: 70.2 us -> 68.2 us
    all_to_all x1, waiting for transfers between devices: 9.22 us -> 4.55 us  [body(): whole = lax.all_to_all(part, EVERY, 0, 0, axis_index_groups=planes)]
    all_to_all x1, waiting for transfers between devices: 2.91 us -> 6.26 us  [body(): part = lax.all_to_all(part, EVERY, 0, 0, axis_index_groups=lines)]
    ppermute x1, waiting for transfers between devices: 0.01 us -> 2.26 us  [body(): got_even = lax.ppermute(grad_even, COL, even_pairs)]
    ppermute x1, starting transfers between devices: 5.82 us -> 3.99 us  [body(): facing = lax.ppermute(whole, 'core', swap)]
  transfers between devices with their start and end apart: 14 -> 14, of which waited for: 7 -> 8; matrix products, arithmetic and copies ran while one was open for 0% -> 0% of each run, Pallas kernels for 4% -> 4%
where the time goes in v13:
time: 102 us; the launch traced here: 101 us
  starting transfers between devices  68.2 us (67%)
  waiting for transfers between devices  20.7 us (20%)
  Pallas kernels  9.79 us (10%)
  between operations  1.52 us (1%)
    all_to_all x1, starting transfers between devices, body(): lax.all_to_all(summed.reshape(n_yx, chunk, side), EVERY, 0, 0, axis_index...  13.9 us
    ppermute x1, starting transfers between devices, body(): column = lax.ppermute(column, ROW, pairs)  12 us
    ppermute x1, starting transfers between devices, body(): from_beyond = lax.ppermute(message_beyond, ROW, pairs)  8.18 us
    all_to_all x1, starting transfers between devices, body(): part = lax.all_to_all(part, EVERY, 0, 0, axis_index_groups=lines)  7.19 us
    all_to_all x1, waiting for transfers between devices, body(): part = lax.all_to_all(part, EVERY, 0, 0, axis_index_groups=lines)  6.26 us
    all_to_all x1, starting transfers between devices, body(): whole = lax.all_to_all(part, EVERY, 0, 0, axis_index_groups=planes)  6.19 us
    all_to_all x1, waiting for transfers between devices, body(): whole = lax.all_to_all(part, EVERY, 0, 0, axis_index_groups=planes)  4.55 us
    ppermute x1, starting transfers between devices, body(): facing = lax.ppermute(whole, 'core', swap)  3.99 us
  transfers between devices with their start and end apart: 14, of which 8 were waited for; matrix products, arithmetic and copies ran while one was open for 0% of the time, Pallas kernels for 4%

profile of v13, /device:TPU:1, one launch (start us, length us, event | category | flops | bytes accessed | tf_op | source)
XLA Modules:
  0.0 100.9 jit_solution(16590970766630407472)
XLA Ops:
  1.4 12.0 %collective-permute-start = (f32[136,128]{1,0:T(8,128)S(1)}, f32[136,128]{1,0:T(8,128)S(1)}, u32[]{:S(2)}, u32[]{:S(2)}) collective-permute-start(f32[136,128]{1,0:T(8,128)S(1)} %get-tuple-element.26), channel_id=1, source_target_pairs={{16,32},{48,64},{80,96},{112,128},{144,160},{176,192},{208,224},{2... | collective-permute-start | bytes 208904 | tf_op jit(solution)/shard_map/ppermute | solution.py:417
  13.5 3.1 %collective-permute-start.1 = (f32[2,64,128]{2,1,0:T(8,128)S(1)}, f32[2,64,128]{2,1,0:T(8,128)S(1)}, u32[]{:S(2)}, u32[]{:S(2)}) collective-permute-start(f32[2,64,128]{2,1,0:T(8,128)S(1)} %get-tuple-element.27), channel_id=1, source_target_pairs={{0,1},{2,3},{4,5},{6,7},{8,9},{10,11},{12,13},{14,15},{1,0},{3,2},... | collective-permute-start | bytes 196616 | tf_op jit(solution)/shard_map/ppermute | solution.py:418
  17.3 2.1 %collective-permute-start.3 = (f32[8,128]{1,0:T(8,128)S(1)}, f32[8,128]{1,0:T(8,128)S(1)}, u32[]{:S(2)}, u32[]{:S(2)}) collective-permute-start(f32[8,128]{1,0:T(8,128)S(1)} %get-tuple-element.30), channel_id=1, source_target_pairs={{0,16},{16,0},{1,17},{17,1},{2,18},{18,2},{3,19},{19,3},{4,20},{20... | collective-permute-start | bytes 12296 | tf_op jit(solution)/shard_map/ppermute | solution.py:420
  20.2 3.2 %collective-permute-start.5 = (f32[264,128]{1,0:T(8,128)S(1)}, f32[264,128]{1,0:T(8,128)S(1)}, u32[]{:S(2)}, u32[]{:S(2)}) collective-permute-start(f32[264,128]{1,0:T(8,128)S(1)} %get-tuple-element.31), channel_id=1, source_target_pairs={{16,32},{48,64},{80,96},{112,128},{144,160},{176,192},{208,224},{2... | collective-permute-start | bytes 405512 | tf_op jit(solution)/shard_map/ppermute | solution.py:424
  23.8 1.9 %collective-permute-start.4 = (f32[256,128]{1,0:T(8,128)S(1)}, f32[256,128]{1,0:T(8,128)S(1)}, u32[]{:S(2)}, u32[]{:S(2)}) collective-permute-start(f32[256,128]{1,0:T(8,128)S(1)} %shard_map.81), channel_id=1, source_target_pairs={{0,16},{16,0},{1,17},{17,1},{2,18},{18,2},{3,19},{19,3},{4,20},{20... | collective-permute-start | bytes 393224 | tf_op jit(solution)/shard_map/ppermute | solution.py:426
  27.1 3.5 %collective-permute-done.5.beyond = f32[264,128]{1,0:T(8,128)S(1)} collective-permute-done((f32[264,128]{1,0:T(8,128)S(1)}, f32[264,128]{1,0:T(8,128)S(1)}, u32[]{:S(2)}, u32[]{:S(2)}) %collective-permute-start.5) | collective-permute-done | bytes 135200 | tf_op jit(solution)/shard_map/ppermute | solution.py:424
  30.6 3.7 %shard_map.82 = (f32[512,128]{1,0:T(8,128)S(1)}, f32[776,128]{1,0:T(8,128)S(1)}, f32[264,128]{1,0:T(8,128)S(1)}, f32[256,128]{1,0:T(8,128)S(1)}) custom-call(s32[2]{0:T(128)S(1)} %bitcast.10, s32[1]{0:T(128)} %bitcast.5.live, f32[256,128]{1,0:T(8,128)S(1)} %shard_map.80.near, f32[256,128]{1,0:T(8,128)S(1)} %collective-permute-done.4.other, ...), custom_call_target="tpu_custom_call" | custom-call | tf_op jit(solution)/shard_map/pallas_call | solution.py:434
  34.4 1.9 %collective-permute-start.6 = (f32[776,128]{1,0:T(8,128)S(1)}, f32[776,128]{1,0:T(8,128)S(1)}, u32[]{:S(2)}, u32[]{:S(2)}) collective-permute-start(f32[776,128]{1,0:T(8,128)S(1)} %get-tuple-element.36), channel_id=1, source_target_pairs={{0,16},{16,0},{1,17},{17,1},{2,18},{18,2},{3,19},{19,3},{4,20},{20... | collective-permute-start | bytes 1191944 | tf_op jit(solution)/shard_map/ppermute | solution.py:447
  36.3 1.7 %collective-permute-done.6.from_core.message = f32[776,128]{1,0:T(8,128)S(1)} collective-permute-done((f32[776,128]{1,0:T(8,128)S(1)}, f32[776,128]{1,0:T(8,128)S(1)}, u32[]{:S(2)}, u32[]{:S(2)}) %collective-permute-start.6) | collective-permute-done | bytes 397344 | tf_op jit(solution)/shard_map/ppermute | solution.py:447
  38.0 0.7 shard_map.84
  38.7 13.9 %all-to-all-start = ((f32[32,16,128]{2,1,0:T(8,128)}), f32[32,16,128]{2,1,0:T(8,128)S(1)}, u32[]{:S(2)}, u32[]{:S(2)}) async-start(f32[32,16,128]{2,1,0:T(8,128)} %bitcast.3), calls=%async_computation | async-start | bytes 524288 | tf_op jit(solution)/shard_map/all_to_all | solution.py:456
  52.6 8.2 %collective-permute-start.7 = (f32[264,128]{1,0:T(8,128)S(1)}, f32[264,128]{1,0:T(8,128)S(1)}, u32[]{:S(2)}, u32[]{:S(2)}) collective-permute-start(f32[264,128]{1,0:T(8,128)S(1)} %get-tuple-element.37), channel_id=1, source_target_pairs={{16,32},{48,64},{80,96},{112,128},{144,160},{176,192},{208,224},{2... | collective-permute-start | bytes 405512 | tf_op jit(solution)/shard_map/ppermute | solution.py:448
  60.8 1.5 %all-to-all-done.parts = f32[32,16,128]{2,1,0:T(8,128)S(1)} async-done(((f32[32,16,128]{2,1,0:T(8,128)}), f32[32,16,128]{2,1,0:T(8,128)S(1)}, u32[]{:S(2)}, u32[]{:S(2)}) %all-to-all-start) | async-done | bytes 262176 | tf_op jit(solution)/shard_map/all_to_all | solution.py:456
  63.0 7.2 %all-to-all-start.1 = ((f32[8,16,128]{2,1,0:T(8,128)}), f32[8,16,128]{2,1,0:T(8,128)S(1)}, u32[]{:S(2)}, u32[]{:S(2)}) async-start(f32[8,16,128]{2,1,0:T(8,128)} %shard_map.85), calls=%async_computation.1 | async-start | bytes 131072 | tf_op jit(solution)/shard_map/all_to_all | solution.py:468
  70.2 1.0 shard_map.83
  71.2 6.3 %all-to-all-done.1.parts = f32[8,16,128]{2,1,0:T(8,128)S(1)} async-done(((f32[8,16,128]{2,1,0:T(8,128)}), f32[8,16,128]{2,1,0:T(8,128)S(1)}, u32[]{:S(2)}, u32[]{:S(2)}) %all-to-all-start.1) | async-done | bytes 65568 | tf_op jit(solution)/shard_map/all_to_all | solution.py:468
  77.5 0.7 shard_map.86
  78.2 6.2 %all-to-all-start.2 = ((f32[32,16,128]{2,1,0:T(8,128)}), f32[32,16,128]{2,1,0:T(8,128)S(1)}, u32[]{:S(2)}, u32[]{:S(2)}) async-start(f32[32,16,128]{2,1,0:T(8,128)} %shard_map.86), calls=%async_computation.2 | async-start | bytes 524288 | tf_op jit(solution)/shard_map/all_to_all | solution.py:473
  84.4 3.1 %collective-permute-start.8 = (f32[2,64,128]{2,1,0:T(8,128)S(1)}, f32[2,64,128]{2,1,0:T(8,128)S(1)}, u32[]{:S(2)}, u32[]{:S(2)}) collective-permute-start(f32[2,64,128]{2,1,0:T(8,128)S(1)} %get-tuple-element.43), channel_id=1, source_target_pairs={{0,1},{2,3},{4,5},{6,7},{8,9},{10,11},{12,13},{14,15},{1,0},{3,2},... | collective-permute-start | bytes 196616 | tf_op jit(solution)/shard_map/ppermute | solution.py:471
  88.2 2.3 %collective-permute-done.8.with_even = f32[2,64,128]{2,1,0:T(8,128)S(1)} collective-permute-done((f32[2,64,128]{2,1,0:T(8,128)S(1)}, f32[2,64,128]{2,1,0:T(8,128)S(1)}, u32[]{:S(2)}, u32[]{:S(2)}) %collective-permute-start.8) | collective-permute-done | bytes 65568 | tf_op jit(solution)/shard_map/ppermute | solution.py:471
  90.5 4.5 %all-to-all-done.2 = f32[32,16,128]{2,1,0:T(8,128)S(1)} async-done(((f32[32,16,128]{2,1,0:T(8,128)}), f32[32,16,128]{2,1,0:T(8,128)S(1)}, u32[]{:S(2)}, u32[]{:S(2)}) %all-to-all-start.2) | async-done | bytes 262176 | tf_op jit(solution)/shard_map/all_to_all | solution.py:473
  95.0 4.0 %collective-permute-start.10 = (f32[4,128,128]{2,1,0:T(8,128)S(1)}, f32[4,128,128]{2,1,0:T(8,128)S(1)}, u32[]{:S(2)}, u32[]{:S(2)}) collective-permute-start(f32[4,128,128]{2,1,0:T(8,128)S(1)} %bitcast.6), channel_id=1, source_target_pairs={{0,16},{16,0},{1,17},{17,1},{2,18},{18,2},{3,19},{19,3},{4,20},{20... | collective-permute-start | bytes 786440 | tf_op jit(solution)/shard_map/ppermute | solution.py:476
  99.0 0.8 shard_map.87
  100.2 0.7 shard_map.88
  (26 shorter events, 5.0 us)
Async XLA Ops:
  0.6 0.7 copy-start.4
  1.3 12.1 %copy-start.2 = (f32[2,2,64,256]{3,2,1,0:T(8,128)S(1)}, f32[2,2,64,256]{3,2,1,0:T(8,128)}, u32[]{:S(2)}) copy-start(f32[2,2,64,256]{3,2,1,0:T(8,128)} %own.3) | copy-start | bytes 786436
  1.4 18.6 %collective-permute-start = (f32[136,128]{1,0:T(8,128)S(1)}, f32[136,128]{1,0:T(8,128)S(1)}, u32[]{:S(2)}, u32[]{:S(2)}) collective-permute-start(f32[136,128]{1,0:T(8,128)S(1)} %get-tuple-element.26), channel_id=1, source_target_pairs={{16,32},{48,64},{80,96},{112,128},{144,160},{176,192},{208,224},{2... | collective-permute-start | bytes 208904 | tf_op jit(solution)/shard_map/ppermute | solution.py:417
  13.5 6.4 %collective-permute-start.1 = (f32[2,64,128]{2,1,0:T(8,128)S(1)}, f32[2,64,128]{2,1,0:T(8,128)S(1)}, u32[]{:S(2)}, u32[]{:S(2)}) collective-permute-start(f32[2,64,128]{2,1,0:T(8,128)S(1)} %get-tuple-element.27), channel_id=1, source_target_pairs={{0,1},{2,3},{4,5},{6,7},{8,9},{10,11},{12,13},{14,15},{1,0},{3,2},... | collective-permute-start | bytes 196616 | tf_op jit(solution)/shard_map/ppermute | solution.py:418
  16.6 3.3 %collective-permute-start.2 = (f32[2,64,128]{2,1,0:T(8,128)S(1)}, f32[2,64,128]{2,1,0:T(8,128)S(1)}, u32[]{:S(2)}, u32[]{:S(2)}) collective-permute-start(f32[2,64,128]{2,1,0:T(8,128)S(1)} %get-tuple-element.28), channel_id=1, source_target_pairs={{1,2},{3,4},{5,6},{7,8},{9,10},{11,12},{13,14},{2,1},{4,3},{6,5},{... | collective-permute-start | bytes 196616 | tf_op jit(solution)/shard_map/ppermute | solution.py:419
  17.3 9.1 %copy-start = (f32[2,4,128,128]{3,2,1,0:T(8,128)S(1)}, f32[2,4,128,128]{3,2,1,0:T(8,128)}, u32[]{:S(2)}) copy-start(f32[2,4,128,128]{3,2,1,0:T(8,128)} %probe.3) | copy-start | bytes 1572868
  17.3 6.2 %collective-permute-start.3 = (f32[8,128]{1,0:T(8,128)S(1)}, f32[8,128]{1,0:T(8,128)S(1)}, u32[]{:S(2)}, u32[]{:S(2)}) collective-permute-start(f32[8,128]{1,0:T(8,128)S(1)} %get-tuple-element.30), channel_id=1, source_target_pairs={{0,16},{16,0},{1,17},{17,1},{2,18},{18,2},{3,19},{19,3},{4,20},{20... | collective-permute-start | bytes 12296 | tf_op jit(solution)/shard_map/ppermute | solution.py:420
  20.2 6.1 %copy-start.1 = (bf16[12,128,128]{2,1,0:T(8,128)(2,1)S(1)}, bf16[12,128,128]{2,1,0:T(8,128)(2,1)}, u32[]{:S(2)}) copy-start(bf16[12,128,128]{2,1,0:T(8,128)(2,1)} %constant.2.clone.tabs) | copy-start | bytes 1179652
  20.2 10.4 %collective-permute-start.5 = (f32[264,128]{1,0:T(8,128)S(1)}, f32[264,128]{1,0:T(8,128)S(1)}, u32[]{:S(2)}, u32[]{:S(2)}) collective-permute-start(f32[264,128]{1,0:T(8,128)S(1)} %get-tuple-element.31), channel_id=1, source_target_pairs={{16,32},{48,64},{80,96},{112,128},{144,160},{176,192},{208,224},{2... | collective-permute-start | bytes 405512 | tf_op jit(solution)/shard_map/ppermute | solution.py:424
  23.5 2.9 %copy-start.3 = (f32[1,1,1,128,128]{4,3,2,1,0:T(8,128)S(1)}, f32[1,1,1,128,128]{4,3,2,1,0:T(8,128)}, u32[]{:S(2)}) copy-start(f32[1,1,1,128,128]{4,3,2,1,0:T(8,128)} %pattern.3) | copy-start | bytes 196612
  23.8 3.3 %collective-permute-start.4 = (f32[256,128]{1,0:T(8,128)S(1)}, f32[256,128]{1,0:T(8,128)S(1)}, u32[]{:S(2)}, u32[]{:S(2)}) collective-permute-start(f32[256,128]{1,0:T(8,128)S(1)} %shard_map.81), channel_id=1, source_target_pairs={{0,16},{16,0},{1,17},{17,1},{2,18},{18,2},{3,19},{19,3},{4,20},{20... | collective-permute-start | bytes 393224 | tf_op jit(solution)/shard_map/ppermute | solution.py:426
  34.4 3.6 %collective-permute-start.6 = (f32[776,128]{1,0:T(8,128)S(1)}, f32[776,128]{1,0:T(8,128)S(1)}, u32[]{:S(2)}, u32[]{:S(2)}) collective-permute-start(f32[776,128]{1,0:T(8,128)S(1)} %get-tuple-element.36), channel_id=1, source_target_pairs={{0,16},{16,0},{1,17},{17,1},{2,18},{18,2},{3,19},{19,3},{4,20},{20... | collective-permute-start | bytes 1191944 | tf_op jit(solution)/shard_map/ppermute | solution.py:447
  38.7 23.7 %all-to-all-start = ((f32[32,16,128]{2,1,0:T(8,128)}), f32[32,16,128]{2,1,0:T(8,128)S(1)}, u32[]{:S(2)}, u32[]{:S(2)}) async-start(f32[32,16,128]{2,1,0:T(8,128)} %bitcast.3), calls=%async_computation | async-start | bytes 524288 | tf_op jit(solution)/shard_map/all_to_all | solution.py:456
  52.6 17.6 %collective-permute-start.7 = (f32[264,128]{1,0:T(8,128)S(1)}, f32[264,128]{1,0:T(8,128)S(1)}, u32[]{:S(2)}, u32[]{:S(2)}) collective-permute-start(f32[264,128]{1,0:T(8,128)S(1)} %get-tuple-element.37), channel_id=1, source_target_pairs={{16,32},{48,64},{80,96},{112,128},{144,160},{176,192},{208,224},{2... | collective-permute-start | bytes 405512 | tf_op jit(solution)/shard_map/ppermute | solution.py:448
  63.0 14.4 %all-to-all-start.1 = ((f32[8,16,128]{2,1,0:T(8,128)}), f32[8,16,128]{2,1,0:T(8,128)S(1)}, u32[]{:S(2)}, u32[]{:S(2)}) async-start(f32[8,16,128]{2,1,0:T(8,128)} %shard_map.85), calls=%async_computation.1 | async-start | bytes 131072 | tf_op jit(solution)/shard_map/all_to_all | solution.py:468
  78.2 16.8 %all-to-all-start.2 = ((f32[32,16,128]{2,1,0:T(8,128)}), f32[32,16,128]{2,1,0:T(8,128)S(1)}, u32[]{:S(2)}, u32[]{:S(2)}) async-start(f32[32,16,128]{2,1,0:T(8,128)} %shard_map.86), calls=%async_computation.2 | async-start | bytes 524288 | tf_op jit(solution)/shard_map/all_to_all | solution.py:473
  84.4 6.1 %collective-permute-start.8 = (f32[2,64,128]{2,1,0:T(8,128)S(1)}, f32[2,64,128]{2,1,0:T(8,128)S(1)}, u32[]{:S(2)}, u32[]{:S(2)}) collective-permute-start(f32[2,64,128]{2,1,0:T(8,128)S(1)} %get-tuple-element.43), channel_id=1, source_target_pairs={{0,1},{2,3},{4,5},{6,7},{8,9},{10,11},{12,13},{14,15},{1,0},{3,2},... | collective-permute-start | bytes 196616 | tf_op jit(solution)/shard_map/ppermute | solution.py:471
  87.5 2.9 %collective-permute-start.9 = (f32[2,64,128]{2,1,0:T(8,128)S(1)}, f32[2,64,128]{2,1,0:T(8,128)S(1)}, u32[]{:S(2)}, u32[]{:S(2)}) collective-permute-start(f32[2,64,128]{2,1,0:T(8,128)S(1)} %get-tuple-element.44), channel_id=1, source_target_pairs={{1,2},{3,4},{5,6},{7,8},{9,10},{11,12},{13,14},{2,1},{4,3},{6,5},{... | collective-permute-start | bytes 196616 | tf_op jit(solution)/shard_map/ppermute | solution.py:472
  95.0 5.1 %collective-permute-start.10 = (f32[4,128,128]{2,1,0:T(8,128)S(1)}, f32[4,128,128]{2,1,0:T(8,128)S(1)}, u32[]{:S(2)}, u32[]{:S(2)}) collective-permute-start(f32[4,128,128]{2,1,0:T(8,128)S(1)} %bitcast.6), channel_id=1, source_target_pairs={{0,16},{16,0},{1,17},{17,1},{2,18},{18,2},{3,19},{19,3},{4,20},{20... | collective-permute-start | bytes 786440 | tf_op jit(solution)/shard_map/ppermute | solution.py:476
